TPU v7x, 512 devices: a whole 4x8x8 slice. The times are simulated.
512 devices in a mesh: ctx: 64 (over z, y_hi, core), head: 8 (over x, y_lo).
Axes of the slice: x: 4, y: 8 (y_hi: 4, y_lo: 2; y = y_hi * 2 + y_lo), z: 8, core: 2. Of those that a mesh axis runs over, the one named last changes fastest.
Arguments:
- query_rows: bfloat16 [32768, 4096], P('ctx', 'head'), may hold values from -43 to 43
- key_rows: bfloat16 [32768, 4096], P('ctx', 'head'), may hold values from -4 to 4
- value_rows: bfloat16 [32768, 4096], P('ctx', 'head'), may hold values from -16 to 16
- out_gain: float32 [4096], P('head'), may hold values from 0.5 to 1.5
Outputs:
- normed: bfloat16 [32768, 4096], P('ctx', 'head')
All inputs are finite; a program needn't handle non-finite values.
Results may differ from a plain program's by a relative error of at most 0.0085.
Values may be sent and summed in bfloat16 or wider, within the bound.
No kernel may reach another device: no remote copies, remote signals or barrier semaphores. Data moves between devices by JAX's collectives and lax.ppermute only.
A program may use at most 64 MiB of HBM per device.

v0:
```python
import math

import jax
import jax.numpy as jnp
from jax import lax
from jax.sharding import PartitionSpec as P

HEADS = 32
HEAD_DIM = 128
BLOCK = 256
SUMMARY = 16


def band_block(block_items):
    query_part, key_part, value_part = block_items
    scores = jnp.einsum(
        "qhd,khd->hqk", query_part, key_part, preferred_element_type=jnp.float32
    ) * HEAD_DIM ** (-0.5)
    causal = lax.broadcasted_iota(jnp.int32, (BLOCK, BLOCK), 0) >= lax.broadcasted_iota(
        jnp.int32, (BLOCK, BLOCK), 1
    )
    scores = jnp.where(causal[None], scores, -1e30)
    row_max = jnp.max(scores, axis=-1)
    weights = jnp.where(causal[None], jnp.exp(scores - row_max[..., None]), 0.0)
    row_sum = jnp.sum(weights, axis=-1)
    joint_acc = jnp.einsum(
        "hqk,khd->qhd", weights.astype(jnp.bfloat16), value_part, preferred_element_type=jnp.float32
    )
    return (row_max, row_sum, joint_acc)


def summary_update(run_state, query_set, set_blocks, key_sub, value_sub, first_row):
    sub_rows = key_sub.shape[0]
    key_block = (first_row + jnp.arange(sub_rows, dtype=jnp.int32)) // SUMMARY

    def update(group_state):
        old_max, old_sum, old_acc = group_state
        scores = jnp.einsum(
            "gqhd,khd->ghqk", query_set, key_sub, preferred_element_type=jnp.float32
        ) * HEAD_DIM ** (-0.5)
        allowed = (key_block[None, :] < set_blocks[:, None])[:, None, None, :]
        scores = jnp.where(allowed, scores, -1e30)
        joint_max = jnp.maximum(old_max, jnp.max(scores, axis=-1))
        weights = jnp.where(allowed, jnp.exp(scores - joint_max[..., None]), 0.0)
        shrink = jnp.exp(old_max - joint_max)
        new_sum = old_sum * shrink + jnp.sum(weights, axis=-1)
        new_acc = old_acc * jnp.transpose(shrink, (0, 2, 1))[..., None] + jnp.einsum(
            "ghqk,khd->gqhd",
            weights.astype(jnp.bfloat16),
            value_sub,
            preferred_element_type=jnp.float32,
        )
        return (joint_max, new_sum, new_acc)

    def unchanged(group_state):
        return group_state

    return lax.cond(first_row // SUMMARY < jnp.max(set_blocks), update, unchanged, run_state)


def sweep_rows(run_state, query_set, set_blocks, key_part, value_part):
    piece_rows, head_count = (key_part.shape[0], key_part.shape[1])
    sub_rows = math.gcd(piece_rows, 512)
    sub_count = piece_rows // sub_rows
    key_split = key_part.reshape(sub_count, sub_rows, head_count, HEAD_DIM)
    value_split = value_part.reshape(sub_count, sub_rows, head_count, HEAD_DIM)
    first_rows = jnp.arange(sub_count, dtype=jnp.int32) * sub_rows

    def inner(state, sub_items):
        key_sub, value_sub, first_row = sub_items
        return (summary_update(state, query_set, set_blocks, key_sub, value_sub, first_row), None)

    run_state, _ = lax.scan(inner, run_state, (key_split, value_split, first_rows))
    return run_state


def summary_pass(query_set, set_blocks, summary_keys, summary_values):
    group_count, _, head_count, _ = query_set.shape
    initial = (
        jnp.full((group_count, head_count, BLOCK), -1e30, jnp.float32),
        jnp.zeros((group_count, head_count, BLOCK), jnp.float32),
        jnp.zeros((group_count, BLOCK, head_count, HEAD_DIM), jnp.float32),
    )
    return sweep_rows(
        initial,
        query_set,
        set_blocks,
        lax.all_gather(summary_keys, "ctx", axis=0, tiled=True),
        lax.all_gather(summary_values, "ctx", axis=0, tiled=True),
    )


def local(query_rows, key_rows, value_rows, out_gain):
    row_count, width = query_rows.shape
    head_count = width // HEAD_DIM
    block_count = row_count // BLOCK
    my_index = lax.axis_index("ctx")
    block_shape = (block_count, BLOCK, head_count, HEAD_DIM)
    query_blocks = query_rows.reshape(block_shape)
    key_blocks = key_rows.reshape(block_shape)
    value_blocks = value_rows.reshape(block_shape)
    band_max, band_sum, band_acc = lax.map(band_block, (query_blocks, key_blocks, value_blocks))
    summary_keys = key_blocks[:, BLOCK - SUMMARY :].reshape(
        block_count * SUMMARY, head_count, HEAD_DIM
    )
    summary_values = value_blocks[:, BLOCK - SUMMARY :].reshape(
        block_count * SUMMARY, head_count, HEAD_DIM
    )
    local_blocks = my_index * block_count + jnp.arange(block_count, dtype=jnp.int32)
    summary_state = summary_pass(query_blocks, local_blocks, summary_keys, summary_values)
    far_max, far_sum, far_acc = summary_state
    joint_max = jnp.maximum(band_max, far_max)
    band_scale = jnp.exp(band_max - joint_max)
    far_scale = jnp.exp(far_max - joint_max)
    joint_sum = band_sum * band_scale + far_sum * far_scale
    joint_acc = (
        band_acc * jnp.transpose(band_scale, (0, 2, 1))[..., None]
        + far_acc * jnp.transpose(far_scale, (0, 2, 1))[..., None]
    )
    attended = joint_acc / jnp.transpose(joint_sum, (0, 2, 1))[..., None]
    attended = attended.reshape(row_count, width)
    squares = jnp.sum(attended * attended, axis=-1)
    row_totals = lax.psum(squares, "head")
    row_scale = lax.rsqrt(row_totals / (HEADS * HEAD_DIM) + 1e-06)
    return (attended * row_scale[:, None] * out_gain).astype(jnp.bfloat16)


def solution(mesh):
    placed = (P("ctx", "head"), P("ctx", "head"), P("ctx", "head"), P("head"))
    return jax.shard_map(
        local, mesh=mesh, in_specs=placed, out_specs=P("ctx", "head"), check_vma=False
    )
```

profile of v0, /device:TPU:448, one launch (start us, length us, event | category | flops | bytes accessed | tf_op | source)
XLA Modules:
  0.0 243.3 jit_solution(7592375874192132577)
XLA Ops:
  6.5 1.2 reshape.64
  8.4 2.0 reshape.65
  12.4 1.2 reshape.63
  13.7 1.1 broadcast.81.clone3
  14.8 7.0 %while.32 = (s32[]{:T(128)}, f32[2,4,256]{2,0,1:T(2,128)S(1)}, f32[2,4,256]{2,0,1:T(2,128)S(1)}, f32[2,256,4,128]{3,1,0,2:T(8,128)}, bf16[2,256,4,128]{3,2,1,0:T...) while((s32[]{:T(128)}, f32[2,4,256]{2,0,1:T(2,128)S(1)}, ...), condition=%wide.region_3.4_spmd, body=%wide.region_0.3_spmd.sunk | while | flops 136640512 | bytes 8962169 | solution.py:102
  14.9 1.1 constant_dynamic-slice_fusion.5
  18.4 1.1 constant_dynamic-slice_fusion.5
  21.8 66.7 %all-gather.3.cloned.1.call-done = bf16[2048,4,128]{2,0,1:T(8,128)(2,1)} async-done(((bf16[32,4,128]{2,0,1:T(8,128)(2,1)}), bf16[2048,4,128]{2,0,1:T(8,128)(2,1)}) %all-gather.3.cloned.1.call-update) | async-done | bytes 2097168 | tf_op jit(solution)/shard_map/all_gather | solution.py:88
  88.5 1.7 copy.26
  90.2 78.9 %all-gather.5.cloned.1.call-done = bf16[2048,4,128]{2,0,1:T(8,128)(2,1)} async-done(((bf16[32,4,128]{2,0,1:T(8,128)(2,1)}), bf16[2048,4,128]{2,0,1:T(8,128)(2,1)}) %all-gather.5.cloned.1.call-update) | async-done | bytes 2097168 | tf_op jit(solution)/shard_map/all_gather | solution.py:89
  169.2 3.1 %copy.28 = bf16[4,512,4,128]{3,1,2,0:T(8,128)(2,1)} copy(bf16[4,512,4,128]{3,1,0,2:T(8,128)(2,1)} %bitcast.98) | data formatting | bytes 4194304
  172.2 1.1 broadcast.81.clone3.1
  173.3 40.3 %while.33 = (s32[]{:T(128)}, f32[2,4,256]{2,0,1:T(2,128)S(1)}, f32[2,4,256]{2,0,1:T(2,128)S(1)}, f32[2,256,4,128]{3,1,0,2:T(8,128)}, s32[4]{0:T(128)S(1)}, /*ind...) while((s32[]{:T(128)}, f32[2,4,256]{2,0,1:T(2,128)S(1)}, ...), condition=%wide.region_10.11_spmd.clone, body=%wide.region_5.10_spmd.clone.sunk | while | flops 551042048 | bytes 24787012 | solution.py:73
  177.1 6.2 %conditional.3 = ((f32[2,4,256]{2,0,1:T(2,128)S(1)}, f32[2,4,256]{2,0,1:T(2,128)S(1)}, f32[2,256,4,128]{3,1,0,2:T(8,128)})) conditional(s32[]{:T(128)} %convert_element_type.34, (f32[2,4,256]{2,0,1:T(2,128)S(1)}, f32[2,4,256]{2,0,1:T(2,128)S(1)}, f32[2,256,4,128]{3,1,0,2:T(8,128)}) %tuple.82, (s32[]{:T(128)}, s32[512]{0:T(512)S(1)}, s32[]{:T(128)}, ...), branch_computations={%region_6.6_spmd, %region_7.9_spmd.clone} | conditional | flops 551042048 | bytes 24784512 | solution.py:58
  178.0 1.0 fusion.11
  179.0 3.2 %fusion.20 = f32[2,256,4,128]{3,1,0,2:T(8,128)S(1)} fusion(f32[4,512,2,256]{3,1,2,0:T(8,128)S(1)} %get-tuple-element.523, f32[2,4,256]{2,0,1:T(2,128)S(1)} %get-tuple-element.648, pred[2,512]{1,0:T(4,128)(4,1)S(1)} %broadcast_compare_fusion, f32[2,256,4,128]{3,1,0,2:T(8,128)S(1)} %copy-done, bf16[4,512,4,128]{3,1,2,0:T(8,128)(2,1)} %get-tuple-element.410, ...), kind=kOutput, calls=%fused_computation.27 | convolution fusion | flops 274202624 | bytes 6833664 | tf_op jit(solution)/shard_map/while/body/eval_jaxpr/cond/branch_1_fun/ghqk,khd->gqhd/dot_general | solution.py:47
  182.2 1.1 fusion.13
  187.2 6.2 %conditional.3 = ((f32[2,4,256]{2,0,1:T(2,128)S(1)}, f32[2,4,256]{2,0,1:T(2,128)S(1)}, f32[2,256,4,128]{3,1,0,2:T(8,128)})) conditional(s32[]{:T(128)} %convert_element_type.34, (f32[2,4,256]{2,0,1:T(2,128)S(1)}, f32[2,4,256]{2,0,1:T(2,128)S(1)}, f32[2,256,4,128]{3,1,0,2:T(8,128)}) %tuple.82, (s32[]{:T(128)}, s32[512]{0:T(512)S(1)}, s32[]{:T(128)}, ...), branch_computations={%region_6.6_spmd, %region_7.9_spmd.clone} | conditional | flops 551042048 | bytes 24784512 | solution.py:58
  188.0 1.0 fusion.11
  189.1 3.2 %fusion.20 = f32[2,256,4,128]{3,1,0,2:T(8,128)S(1)} fusion(f32[4,512,2,256]{3,1,2,0:T(8,128)S(1)} %get-tuple-element.523, f32[2,4,256]{2,0,1:T(2,128)S(1)} %get-tuple-element.648, pred[2,512]{1,0:T(4,128)(4,1)S(1)} %broadcast_compare_fusion, f32[2,256,4,128]{3,1,0,2:T(8,128)S(1)} %copy-done, bf16[4,512,4,128]{3,1,2,0:T(8,128)(2,1)} %get-tuple-element.410, ...), kind=kOutput, calls=%fused_computation.27 | convolution fusion | flops 274202624 | bytes 6833664 | tf_op jit(solution)/shard_map/while/body/eval_jaxpr/cond/branch_1_fun/ghqk,khd->gqhd/dot_general | solution.py:47
  192.3 1.1 fusion.13
  197.3 6.3 %conditional.3 = ((f32[2,4,256]{2,0,1:T(2,128)S(1)}, f32[2,4,256]{2,0,1:T(2,128)S(1)}, f32[2,256,4,128]{3,1,0,2:T(8,128)})) conditional(s32[]{:T(128)} %convert_element_type.34, (f32[2,4,256]{2,0,1:T(2,128)S(1)}, f32[2,4,256]{2,0,1:T(2,128)S(1)}, f32[2,256,4,128]{3,1,0,2:T(8,128)}) %tuple.82, (s32[]{:T(128)}, s32[512]{0:T(512)S(1)}, s32[]{:T(128)}, ...), branch_computations={%region_6.6_spmd, %region_7.9_spmd.clone} | conditional | flops 551042048 | bytes 24784512 | solution.py:58
  198.1 1.0 fusion.11
  199.1 3.2 %fusion.20 = f32[2,256,4,128]{3,1,0,2:T(8,128)S(1)} fusion(f32[4,512,2,256]{3,1,2,0:T(8,128)S(1)} %get-tuple-element.523, f32[2,4,256]{2,0,1:T(2,128)S(1)} %get-tuple-element.648, pred[2,512]{1,0:T(4,128)(4,1)S(1)} %broadcast_compare_fusion, f32[2,256,4,128]{3,1,0,2:T(8,128)S(1)} %copy-done, bf16[4,512,4,128]{3,1,2,0:T(8,128)(2,1)} %get-tuple-element.410, ...), kind=kOutput, calls=%fused_computation.27 | convolution fusion | flops 274202624 | bytes 6833664 | tf_op jit(solution)/shard_map/while/body/eval_jaxpr/cond/branch_1_fun/ghqk,khd->gqhd/dot_general | solution.py:47
  202.4 1.1 fusion.13
  207.3 6.2 %conditional.3 = ((f32[2,4,256]{2,0,1:T(2,128)S(1)}, f32[2,4,256]{2,0,1:T(2,128)S(1)}, f32[2,256,4,128]{3,1,0,2:T(8,128)})) conditional(s32[]{:T(128)} %convert_element_type.34, (f32[2,4,256]{2,0,1:T(2,128)S(1)}, f32[2,4,256]{2,0,1:T(2,128)S(1)}, f32[2,256,4,128]{3,1,0,2:T(8,128)}) %tuple.82, (s32[]{:T(128)}, s32[512]{0:T(512)S(1)}, s32[]{:T(128)}, ...), branch_computations={%region_6.6_spmd, %region_7.9_spmd.clone} | conditional | flops 551042048 | bytes 24784512 | solution.py:58
  208.2 1.0 fusion.11
  209.2 3.2 %fusion.20 = f32[2,256,4,128]{3,1,0,2:T(8,128)S(1)} fusion(f32[4,512,2,256]{3,1,2,0:T(8,128)S(1)} %get-tuple-element.523, f32[2,4,256]{2,0,1:T(2,128)S(1)} %get-tuple-element.648, pred[2,512]{1,0:T(4,128)(4,1)S(1)} %broadcast_compare_fusion, f32[2,256,4,128]{3,1,0,2:T(8,128)S(1)} %copy-done, bf16[4,512,4,128]{3,1,2,0:T(8,128)(2,1)} %get-tuple-element.410, ...), kind=kOutput, calls=%fused_computation.27 | convolution fusion | flops 274202624 | bytes 6833664 | tf_op jit(solution)/shard_map/while/body/eval_jaxpr/cond/branch_1_fun/ghqk,khd->gqhd/dot_general | solution.py:47
  212.5 1.1 fusion.13
  213.6 2.4 multiply_reduce_fusion
  216.0 18.8 %psum.7 = f32[512]{0:T(512)S(1)} all-reduce(f32[512]{0:T(512)S(1)} %bitcast.107), channel_id=1, replica_groups=mesh['ctx'=64,'head'=8] {'head'}, use_global_device_ids=true, to_apply=%region_12.13 | all-reduce | flops 512 | bytes 4096 | tf_op jit(solution)/shard_map/psum | solution.py:123
  235.5 0.9 fusion.37
  (97 shorter events, 14.0 us)
Async XLA Ops:
  6.5 82.0 %all-gather.3.cloned.1.call-start = ((), (), s32[]{:S(2)}) async-start(), calls=%async_computation | async-start | bytes 2129920 | tf_op jit(solution)/shard_map/all_gather | solution.py:88
  8.4 160.8 %all-gather.5.cloned.1.call-start = ((), (), s32[]{:S(2)}) async-start(), calls=%async_computation.1 | async-start | bytes 2129920 | tf_op jit(solution)/shard_map/all_gather | solution.py:89
  177.1 1.8 copy-start
  182.2 1.1 copy-start.1
  187.2 1.8 copy-start
  192.3 1.1 copy-start.1
  197.3 1.9 copy-start
  202.4 1.1 copy-start.1
  207.4 1.8 copy-start
  212.4 1.1 copy-start.1
  213.6 21.9 %copy-start.2 = (f32[512]{0:T(512)S(1)}, f32[512]{0:T(512)}, u32[]{:S(2)}) copy-start(f32[512]{0:T(512)} %param.13) | copy-start | bytes 6148
Sparse Core Ops, SparseCore 0:
  10.6 77.8 all-gather.2
  91.7 77.3 all-gather.4
where the time goes:
time: 244 us; the launch traced here: 243 us
  waiting for transfers between devices  146 us (60%)
  local copies, waits for them, and re-layouts  21.7 us (9%)
  blocking collectives  18.8 us (8%)
  matrix products  18.1 us (7%)
  between operations  13.5 us (6%)
  loops' own time  13.4 us (5%)
  other arithmetic  12.1 us (5%)
    all_gather x1, waiting for transfers between devices, summary_pass(): lax.all_gather(summary_values, 'ctx', axis=0, tiled=True)  78.9 us
    all_gather x1, waiting for transfers between devices, summary_pass(): lax.all_gather(summary_keys, 'ctx', axis=0, tiled=True)  66.7 us
    psum x1, blocking collectives, local(): row_totals = lax.psum(squares, 'head')  18.8 us
    dot_general x4, matrix products, update(): jnp.einsum('ghqk,khd->gqhd', weights.astype(jnp.bfloat16), value_sub, pre...  12.9 us
    another operation x1, loops' own time, sweep_rows(): lax.scan(inner, run_state, (key_split, value_split, first_rows))  12.8 us
    unnamed x6, local copies, waits for them, and re-layouts  4.9 us
  transfers between devices with their start and end apart: 2, of which 2 were waited for; matrix products, arithmetic and copies ran while one was open for 6% of the time, Pallas kernels for 0%

commit v1 on v0

v1 whole, which is shorter than its diff:
```python
import functools
import math

import jax
import jax.numpy as jnp
from jax import lax
from jax.experimental import pallas as pl
from jax.experimental.pallas import tpu as pltpu
from jax.sharding import PartitionSpec as P

HEAD_DIM = 128
BLOCK = 256
SUMMARY = 16
FEATURES = 4096
CHIPS_Z, CHIPS_Y, CORES = 8, 4, 2
SLAB = CHIPS_Y * CORES
HALF = 256
ROWS = 512
SCALE = HEAD_DIM**-0.5 * math.log2(math.e)
MINUS = -1e30
VIRTUAL = 4
VMEM = pl.BlockSpec(memory_space=pltpu.VMEM)
SMEM = pl.BlockSpec(memory_space=pltpu.SMEM)
LIMIT = 48 * 1024 * 1024

F32 = jnp.float32
BF16 = jnp.bfloat16


def rows_dot(a, b):
    return lax.dot_general(a, b, (((1,), (1,)), ((), ())), preferred_element_type=F32)


def columns_dot(a, b):
    return lax.dot_general(a, b, (((0,), (0,)), ((), ())), preferred_element_type=F32)


def pack_summary(key_ref, value_ref, out_ref):
    for core in range(CORES):
        columns = slice(core * HALF, (core + 1) * HALF)
        for start, ref in ((0, key_ref), (2 * SUMMARY, value_ref)):
            for block in range(2):
                end = (block + 1) * BLOCK
                piece = ref[end - SUMMARY : end, columns]
                first = start + block * SUMMARY
                for y in range(CHIPS_Y):
                    out_ref[y * CORES + core, first : first + SUMMARY] = piece


def pack_other(place_ref, query_ref, key_ref, value_ref, out_ref):
    other = pl.multiple_of((1 - place_ref[2]) * HALF, HALF)
    for part, ref in enumerate((query_ref, key_ref, value_ref)):
        out_ref[part * ROWS : (part + 1) * ROWS] = ref[:, pl.ds(other, HALF)]


def slab_keys(slab, head):
    columns = slice(head * HEAD_DIM, (head + 1) * HEAD_DIM)
    sources = slab.shape[0]
    keys = slab[:, : 2 * SUMMARY, columns].reshape(sources * 2 * SUMMARY, HEAD_DIM)
    values = slab[:, 2 * SUMMARY :, columns].reshape(sources * 2 * SUMMARY, HEAD_DIM)
    return keys, values


def fold_slab(queries, state, slab, first_blocks):
    max_ref, sum_ref, acc_ref = state
    for virtual in range(VIRTUAL):
        keys, values = slab_keys(slab, virtual % 2)
        scores = rows_dot(keys, queries[virtual]) * SCALE
        if first_blocks is not None:
            shape = scores.shape
            key_block = lax.broadcasted_iota(jnp.int32, shape, 0) // SUMMARY
            query_block = first_blocks[virtual // 2] + lax.broadcasted_iota(jnp.int32, shape, 1) // BLOCK
            allowed = key_block < query_block
            scores = jnp.where(allowed, scores, MINUS)
        old_max = max_ref[virtual]
        new_max = jnp.maximum(old_max, jnp.max(scores, axis=0, keepdims=True))
        weights = jnp.exp2(scores - new_max)
        shrink = jnp.exp2(old_max - new_max)
        max_ref[virtual] = new_max
        sum_ref[virtual] = sum_ref[virtual] * shrink + jnp.sum(weights, axis=0, keepdims=True)
        acc_ref[virtual] = acc_ref[virtual] * shrink + columns_dot(values, weights.astype(BF16))


def band(query_ref, key_ref, value_ref, mine, other_ref, state, queries_ref):
    max_ref, sum_ref, acc_ref = state
    shape = (BLOCK, BLOCK)
    causal = lax.broadcasted_iota(jnp.int32, shape, 0) <= lax.broadcasted_iota(jnp.int32, shape, 1)
    for virtual in range(VIRTUAL):
        owner, head = divmod(virtual, 2)
        for block in range(2):
            rows = slice(block * BLOCK, (block + 1) * BLOCK)
            if owner == 0:
                columns = pl.ds(mine + head * HEAD_DIM, HEAD_DIM)
                query, key, value = (ref[rows, columns] for ref in (query_ref, key_ref, value_ref))
            else:
                columns = slice(head * HEAD_DIM, (head + 1) * HEAD_DIM)
                query, key, value = (
                    other_ref[part * ROWS + block * BLOCK : part * ROWS + (block + 1) * BLOCK, columns]
                    for part in range(3)
                )
            queries_ref[virtual, rows] = query
            scores = jnp.where(causal, rows_dot(key, query) * SCALE, MINUS)
            new_max = jnp.max(scores, axis=0, keepdims=True)
            weights = jnp.exp2(scores - new_max)
            max_ref[virtual, :, rows] = new_max
            sum_ref[virtual, :, rows] = jnp.sum(weights, axis=0, keepdims=True)
            acc_ref[virtual, :, rows] = columns_dot(value, weights.astype(BF16))


def finish(core, state, own_ref, other_ref, square_ref):
    _, sum_ref, acc_ref = state
    for owner, ref in enumerate((own_ref, other_ref)):
        total = jnp.zeros((1, ROWS), F32)
        for head in range(2):
            virtual = owner * 2 + head
            attended = acc_ref[virtual] / sum_ref[virtual]
            ref[head] = attended
            total += jnp.sum(attended * attended, axis=0, keepdims=True)
        square_ref[core if owner == 0 else 1 - core] = jnp.broadcast_to(total, square_ref.shape[1:])


def attend_all(place_ref, query_ref, key_ref, value_ref, other_in_ref, slabs_ref, own_ref, other_ref, square_ref, *scratch):
    queries_ref, *state = scratch
    here, chip, core = place_ref[0], place_ref[1], place_ref[2]
    mine = pl.multiple_of(core * HALF, HALF)
    band(query_ref, key_ref, value_ref, mine, other_in_ref, state, queries_ref)
    first_blocks = [(chip * CORES + core) * 2, (chip * CORES + 1 - core) * 2]
    fold_slab(queries_ref, state, slabs_ref[here], first_blocks)

    @pl.loop(0, here)
    def _(z):
        fold_slab(queries_ref, state, slabs_ref[z], None)

    finish(core, state, own_ref, other_ref, square_ref)


def scale_rows(place_ref, own_ref, other_ref, square_ref, gain_ref, out_ref):
    core = place_ref[2]
    total = jnp.sum(square_ref[...], axis=0, keepdims=True)
    scale = lax.rsqrt(total * (1.0 / FEATURES) + 1e-06)
    for owner, ref in enumerate((own_ref, other_ref)):
        first = pl.multiple_of((core if owner == 0 else 1 - core) * HALF, HALF)
        for head in range(2):
            columns = pl.ds(first + head * HEAD_DIM, HEAD_DIM)
            rows = jnp.transpose(ref[head] * scale)
            out_ref[:, columns] = (rows * gain_ref[:, columns]).astype(BF16)


def call(body, out_shape, in_specs, scratch=(), cost=None, **more):
    outs = jax.tree.map(lambda _: VMEM, out_shape)
    return pl.pallas_call(
        body,
        out_shape=out_shape,
        in_specs=in_specs,
        out_specs=outs,
        scratch_shapes=list(scratch),
        cost_estimate=cost,
        compiler_params=pltpu.CompilerParams(vmem_limit_bytes=LIMIT),
        **more,
    )


def groups(axes):
    made = {}
    for index in range(CHIPS_Z * SLAB):
        coordinate = {"z": index // SLAB, "y": index // CORES % CHIPS_Y, "c": index % CORES}
        made.setdefault(tuple(v for k, v in coordinate.items() if k not in axes), []).append(index)
    return list(made.values())


def swap_cores(array):
    pairs = [(index, index ^ 1) for index in range(CHIPS_Z * SLAB)]
    return lax.ppermute(array, "ctx", pairs)


def local(head_count, query_rows, key_rows, value_rows, out_gain):
    index = lax.axis_index("ctx")
    place = jnp.stack([index >> 3, (index >> 1) & (CHIPS_Y - 1), index & 1]).astype(jnp.int32)

    packed = call(pack_summary, jax.ShapeDtypeStruct((SLAB, 4 * SUMMARY, HALF), BF16), [VMEM] * 2)(key_rows, value_rows)
    slab = lax.all_to_all(packed, "ctx", 0, 0, axis_index_groups=groups("yc"), tiled=True)
    to_other = call(pack_other, jax.ShapeDtypeStruct((3 * ROWS, HALF), BF16), [SMEM] + [VMEM] * 3)(
        place, query_rows, key_rows, value_rows
    )
    from_other = swap_cores(to_other)
    slabs = lax.all_to_all(
        jnp.broadcast_to(slab[None], (CHIPS_Z, *slab.shape)), "ctx", 0, 0, axis_index_groups=groups("z"), tiled=True
    )

    attended = jax.ShapeDtypeStruct((2, HEAD_DIM, ROWS), F32)
    own, other, squares = call(
        attend_all,
        (attended, attended, jax.ShapeDtypeStruct((CORES, head_count, ROWS), F32)),
        [SMEM] + [VMEM] * 5,
        scratch=[
            pltpu.VMEM((VIRTUAL, ROWS, HEAD_DIM), BF16),
            pltpu.VMEM((VIRTUAL, 1, ROWS), F32),
            pltpu.VMEM((VIRTUAL, 1, ROWS), F32),
            pltpu.VMEM((VIRTUAL, HEAD_DIM, ROWS), F32),
        ],
    )(place, query_rows, key_rows, value_rows, from_other, slabs)
    back = swap_cores(other)
    chips = [
        [(chip * CORES + core) * head_count + head for core in range(CORES) for head in range(head_count)]
        for chip in range(CHIPS_Z * CHIPS_Y)
    ]
    totals = lax.all_to_all(
        squares.reshape(CORES * head_count, ROWS), ("ctx", "head"), 0, 0, axis_index_groups=chips, tiled=True
    )
    return call(scale_rows, jax.ShapeDtypeStruct((ROWS, 4 * HEAD_DIM), BF16), [SMEM] + [VMEM] * 4)(
        place, own, back, totals, out_gain[None]
    )


def solution(mesh):
    placed = (P("ctx", "head"), P("ctx", "head"), P("ctx", "head"), P("head"))
    return jax.shard_map(
        functools.partial(local, mesh.shape["head"]),
        mesh=mesh,
        in_specs=placed,
        out_specs=P("ctx", "head"),
        check_vma=False,
    )
```

time: 244 us -> 106 us (0.43)
  the two profiles are of different devices: /device:TPU:448 before, /device:TPU:1 now
where the time goes in v1:
time: 106 us; the launch traced here: 105 us
  waiting for transfers between devices  45.3 us (43%)
  blocking collectives  29.7 us (28%)
  starting transfers between devices  15.3 us (14%)
  local copies, waits for them, and re-layouts  7.82 us (7%)
  Pallas kernels  6.66 us (6%)
    all_to_all x1, waiting for transfers between devices, local(): lax.all_to_all(jnp.broadcast_to(slab[None], (CHIPS_Z, *slab.shape)), 'ctx...  43.4 us
    all_to_all x1, blocking collectives, local(): lax.all_to_all(packed, 'ctx', 0, 0, axis_index_groups=groups('yc'), tiled...  20 us
    all_to_all x1, blocking collectives, local(): lax.all_to_all(squares.reshape(CORES * head_count, ROWS), ('ctx', 'head')...  9.74 us
    all_to_all x1, starting transfers between devices, local(): lax.all_to_all(jnp.broadcast_to(slab[None], (CHIPS_Z, *slab.shape)), 'ctx...  9.16 us
    unnamed x19, local copies, waits for them, and re-layouts  6.2 us
    ppermute x2, starting transfers between devices, swap_cores(): return lax.ppermute(array, 'ctx', pairs)  6.16 us
    pallas_call x1, Pallas kernels, local(): call(attend_all, (attended, attended, jax.ShapeDtypeStruct((CORES, head_c...  4.36 us
  transfers between devices with their start and end apart: 3, of which 2 were waited for; matrix products, arithmetic and copies ran while one was open for 0% of the time, Pallas kernels for 1%

profile of v1, /device:TPU:1, one launch (start us, length us, event | category | flops | bytes accessed | tf_op | source)
XLA Modules:
  0.0 105.0 jit_solution(8434678777906013070)
XLA Ops:
  0.0 0.0 copy-start
  0.0 1.0 copy-done
  1.0 0.0 copy-start.2
  1.0 1.0 copy-done.2
  2.1 20.0 %all_to_all.21 = bf16[8,64,256]{2,1,0:T(8,128)(2,1)S(1)} all-to-all(bf16[8,64,256]{2,1,0:T(8,128)(2,1)S(1)} %shard_map.47), channel_id=1, replica_groups={{0,8,16,24,32,40,48,56},{64,72,80,88,96,104,112,120},{128,136,144,152,1..., dimensions={0} | all-to-all | bytes 524288 | tf_op jit(solution)/shard_map/all_to_all | solution.py:181
  22.1 1.6 %broadcast_in_dim.4 = bf16[8,8,64,256]{3,2,1,0:T(8,128)(2,1)} broadcast(bf16[8,64,256]{2,1,0:T(8,128)(2,1)S(1)} %all_to_all.21), dimensions={1,2,3} | broadcast | bytes 2359296 | tf_op jit(solution)/shard_map/broadcast_in_dim | solution.py:187
  23.7 0.0 copy-start.1
  23.7 0.0 copy-start.3
  23.7 9.2 %all-to-all-start.1 = ((bf16[8,8,64,256]{3,2,1,0:T(8,128)(2,1)}), bf16[8,8,64,256]{3,2,1,0:T(8,128)(2,1)S(1)}, u32[]{:S(2)}, u32[]{:S(2)}) async-start(bf16[8,8,64,256]{3,2,1,0:T(8,128)(2,1)} %broadcast_in_dim.4), calls=%async_computation.1 | async-start | bytes 4194304 | tf_op jit(solution)/shard_map/all_to_all | solution.py:186
  32.9 0.1 pad_add_fusion.place_ref
  32.9 0.0 copy-done.1
  32.9 0.0 copy-done.3
  32.9 0.0 copy-start.4
  32.9 1.0 copy-done.4
  34.0 0.0 copy-start.8
  34.0 0.6 shard_map.46
  34.6 3.7 %collective-permute-start = (bf16[1536,256]{1,0:T(8,128)(2,1)S(1)}, bf16[1536,256]{1,0:T(8,128)(2,1)S(1)}, u32[]{:S(2)}, u32[]{:S(2)}) collective-permute-start(bf16[1536,256]{1,0:T(8,128)(2,1)S(1)} %shard_map.46), channel_id=1, source_target_pairs={{0,8},{8,0},{16,24},{24,16},{32,40},{40,32},{48,56},{56,48},{64,72... | collective-permute-start | bytes 2359304 | tf_op jit(solution)/shard_map/ppermute | solution.py:173
  38.3 1.9 %collective-permute-done.other_in_ref = bf16[1536,256]{1,0:T(8,128)(2,1)S(1)} collective-permute-done((bf16[1536,256]{1,0:T(8,128)(2,1)S(1)}, bf16[1536,256]{1,0:T(8,128)(2,1)S(1)}, u32[]{:S(2)}, u32[]{:S(2)}) %collective-permute-start) | collective-permute-done | bytes 786464 | tf_op jit(solution)/shard_map/ppermute | solution.py:173
  40.2 0.0 copy-start.6
  40.2 0.9 copy-done.6
  41.1 43.4 %all-to-all-done.1.slabs_ref = bf16[8,8,64,256]{3,2,1,0:T(8,128)(2,1)S(1)} async-done(((bf16[8,8,64,256]{3,2,1,0:T(8,128)(2,1)}), bf16[8,8,64,256]{3,2,1,0:T(8,128)(2,1)S(1)}, u32[]{:S(2)}, u32[]{:S(2)}) %all-to-all-start.1) | async-done | bytes 2097184 | tf_op jit(solution)/shard_map/all_to_all | solution.py:186
  84.5 0.0 copy-start.5
  84.5 1.0 copy-done.5
  85.6 0.0 copy-start.7
  85.6 1.1 %copy-done.7 = bf16[1536,256]{1,0:T(8,128)(2,1)S(1)} copy-done((bf16[1536,256]{1,0:T(8,128)(2,1)S(1)}, bf16[1536,256]{1,0:T(8,128)(2,1)}, u32[]{:S(2)}) %copy-start.7) | copy-done | bytes 786456
  86.7 4.4 %shard_map.48 = (f32[2,128,512]{2,1,0:T(8,128)S(1)}, f32[2,128,512]{2,1,0:T(8,128)S(1)}, f32[2,8,512]{2,1,0:T(8,128)S(1)}) custom-call(s32[3]{0:T(128)S(1)} %pad_add_fusion.place_ref, bf16[512,512]{1,0:T(8,128)(2,1)S(1)} %copy-done.5, bf16[512,512]{1,0:T(8,128)(2,1)S(1)} %copy-done.1, bf16[512,512]{1,0:T(8,128)(2,1)S(1)} %copy-done.3, ...), custom_call_target="tpu_custom_call" | custom-call | tf_op jit(solution)/shard_map/pallas_call | solution.py:191
  91.1 2.4 %collective-permute-start.1 = (f32[2,128,512]{2,1,0:T(8,128)S(1)}, f32[2,128,512]{2,1,0:T(8,128)S(1)}, u32[]{:S(2)}, u32[]{:S(2)}) collective-permute-start(f32[2,128,512]{2,1,0:T(8,128)S(1)} %get-tuple-element.9), channel_id=1, source_target_pairs={{0,8},{8,0},{16,24},{24,16},{32,40},{40,32},{48,56},{56,48},{64,72... | collective-permute-start | bytes 1572872 | tf_op jit(solution)/shard_map/ppermute | solution.py:173
  93.6 9.7 %all_to_all.22 = f32[16,1,512]{2,1,0:T(1,128)S(1)} all-to-all(f32[16,1,512]{2,1,0:T(1,128)S(1)} %copy.5), channel_id=1, replica_groups={{0,1,2,3,4,5,6,7,8,9,10,11,12,13,14,15},{16,17,18,19,20,21,22,23,24,25,..., dimensions={0} | all-to-all | bytes 65536 | tf_op jit(solution)/shard_map/all_to_all | solution.py:207
  103.3 0.0 collective-permute-done.1.other_ref
  103.3 0.0 copy-done.8
  103.3 1.7 %shard_map.49 = bf16[512,512]{1,0:T(8,128)(2,1)} custom-call(s32[3]{0:T(128)S(1)} %pad_add_fusion.place_ref, f32[2,128,512]{2,1,0:T(8,128)S(1)} %get-tuple-element.8.own_ref, f32[2,128,512]{2,1,0:T(8,128)S(1)} %collective-permute-done.1.other_ref, f32[16,512]{1,0:T(8,128)S(1)} %bitcast.8, f32[1,512]{1,0:T(1,128)S(1)} %bitcast.10), custom_call_target="tpu_custom_call" | custom-call | tf_op jit(solution)/shard_map/pallas_call | solution.py:210
  (3 shorter events, 0.1 us)
Async XLA Ops:
  0.0 1.0 copy-start
  1.0 1.0 copy-start.2
  23.7 9.2 %copy-start.1 = (bf16[512,512]{1,0:T(8,128)(2,1)S(1)}, bf16[512,512]{1,0:T(8,128)(2,1)}, u32[]{:S(2)}) copy-start(bf16[512,512]{1,0:T(8,128)(2,1)} %key_ref.5) | copy-start | bytes 1572868
  23.7 9.2 %copy-start.3 = (bf16[512,512]{1,0:T(8,128)(2,1)S(1)}, bf16[512,512]{1,0:T(8,128)(2,1)}, u32[]{:S(2)}) copy-start(bf16[512,512]{1,0:T(8,128)(2,1)} %value_ref.5) | copy-start | bytes 1572868
  23.7 60.8 %all-to-all-start.1 = ((bf16[8,8,64,256]{3,2,1,0:T(8,128)(2,1)}), bf16[8,8,64,256]{3,2,1,0:T(8,128)(2,1)S(1)}, u32[]{:S(2)}, u32[]{:S(2)}) async-start(bf16[8,8,64,256]{3,2,1,0:T(8,128)(2,1)} %broadcast_in_dim.4), calls=%async_computation.1 | async-start | bytes 4194304 | tf_op jit(solution)/shard_map/all_to_all | solution.py:186
  32.9 1.0 copy-start.4
  34.0 69.3 %copy-start.8 = (f32[512]{0:T(512)S(1)}, f32[512]{0:T(512)}, u32[]{:S(2)}) copy-start(f32[512]{0:T(512)} %param.7) | copy-start | bytes 6148
  34.6 5.6 %collective-permute-start = (bf16[1536,256]{1,0:T(8,128)(2,1)S(1)}, bf16[1536,256]{1,0:T(8,128)(2,1)S(1)}, u32[]{:S(2)}, u32[]{:S(2)}) collective-permute-start(bf16[1536,256]{1,0:T(8,128)(2,1)S(1)} %shard_map.46), channel_id=1, source_target_pairs={{0,8},{8,0},{16,24},{24,16},{32,40},{40,32},{48,56},{56,48},{64,72... | collective-permute-start | bytes 2359304 | tf_op jit(solution)/shard_map/ppermute | solution.py:173
  40.2 0.9 copy-start.6
  84.5 1.0 copy-start.5
  85.6 1.1 %copy-start.7 = (bf16[1536,256]{1,0:T(8,128)(2,1)S(1)}, bf16[1536,256]{1,0:T(8,128)(2,1)}, u32[]{:S(2)}) copy-start(bf16[1536,256]{1,0:T(8,128)(2,1)} %copy-done.6) | copy-start | bytes 2359300
  91.1 12.2 %collective-permute-start.1 = (f32[2,128,512]{2,1,0:T(8,128)S(1)}, f32[2,128,512]{2,1,0:T(8,128)S(1)}, u32[]{:S(2)}, u32[]{:S(2)}) collective-permute-start(f32[2,128,512]{2,1,0:T(8,128)S(1)} %get-tuple-element.9), channel_id=1, source_target_pairs={{0,8},{8,0},{16,24},{24,16},{32,40},{40,32},{48,56},{56,48},{64,72... | collective-permute-start | bytes 1572872 | tf_op jit(solution)/shard_map/ppermute | solution.py:173

commit v2 on v1

--- a/solution.py
+++ b/solution.py
@@ -35,16 +35,14 @@
     return lax.dot_general(a, b, (((0,), (0,)), ((), ())), preferred_element_type=F32)
 
 
-def pack_summary(key_ref, value_ref, out_ref):
+def pack_summary(*refs):
+    *pieces, out_ref = refs
     for core in range(CORES):
         columns = slice(core * HALF, (core + 1) * HALF)
-        for start, ref in ((0, key_ref), (2 * SUMMARY, value_ref)):
-            for block in range(2):
-                end = (block + 1) * BLOCK
-                piece = ref[end - SUMMARY : end, columns]
-                first = start + block * SUMMARY
-                for y in range(CHIPS_Y):
-                    out_ref[y * CORES + core, first : first + SUMMARY] = piece
+        for place, ref in enumerate(pieces):
+            rows = slice(place * SUMMARY, (place + 1) * SUMMARY)
+            for chip in range(CHIPS_Y):
+                out_ref[chip * CORES + core, rows] = ref[:, columns]
 
 
 def pack_other(place_ref, query_ref, key_ref, value_ref, out_ref):
@@ -119,19 +117,31 @@
         square_ref[core if owner == 0 else 1 - core] = jnp.broadcast_to(total, square_ref.shape[1:])
 
 
-def attend_all(place_ref, query_ref, key_ref, value_ref, other_in_ref, slabs_ref, own_ref, other_ref, square_ref, *scratch):
-    queries_ref, *state = scratch
-    here, chip, core = place_ref[0], place_ref[1], place_ref[2]
+def start_attention(place_ref, query_ref, key_ref, value_ref, other_in_ref, slab_ref, queries_ref, *state):
+    chip, core = place_ref[1], place_ref[2]
     mine = pl.multiple_of(core * HALF, HALF)
     band(query_ref, key_ref, value_ref, mine, other_in_ref, state, queries_ref)
     first_blocks = [(chip * CORES + core) * 2, (chip * CORES + 1 - core) * 2]
-    fold_slab(queries_ref, state, slabs_ref[here], first_blocks)
-
-    @pl.loop(0, here)
-    def _(z):
-        fold_slab(queries_ref, state, slabs_ref[z], None)
-
-    finish(core, state, own_ref, other_ref, square_ref)
+    fold_slab(queries_ref, state, slab_ref, first_blocks)
+
+
+def go_on(steps, place_ref, queries_ref, *refs):
+    slabs, old_state, state = refs[: 2 * len(steps)], refs[2 * len(steps) : -3], refs[-3:]
+    here = place_ref[0]
+    for old_ref, ref in zip(old_state, state):
+        ref[...] = old_ref[...]
+    for turn, step in enumerate(steps):
+        for slab, reached in zip(slabs[2 * turn : 2 * turn + 2], (here >= step, here + step >= CHIPS_Z)):
+
+            @pl.when(reached)
+            def _(slab=slab):
+                fold_slab(queries_ref, state, slab, None)
+
+
+def end_attention(steps, place_ref, queries_ref, *refs):
+    inputs, outs, state = refs[:-6], refs[-6:-3], refs[-3:]
+    go_on(steps, place_ref, queries_ref, *inputs, *state)
+    finish(place_ref[2], state, *outs)
 
 
 def scale_rows(place_ref, own_ref, other_ref, square_ref, gain_ref, out_ref):
@@ -173,32 +183,74 @@
     return lax.ppermute(array, "ctx", pairs)
 
 
+def pass_on(array, step, way):
+    pairs = []
+    for index in range(CHIPS_Z * SLAB):
+        here = index // SLAB
+        there = here + way
+        source = (there - way * step) % CHIPS_Z
+        needed = there >= step if way == 1 else source < CHIPS_Z // 2
+        if needed and there < CHIPS_Z:
+            pairs.append((index, there % CHIPS_Z * SLAB + index % SLAB))
+    return lax.ppermute(array, "ctx", pairs)
+
+
+def cost_of(slabs):
+    scores = VIRTUAL * ROWS * SLAB * 2 * SUMMARY * slabs
+    return pl.CostEstimate(flops=4 * HEAD_DIM * scores, bytes_accessed=slabs * 2**21, transcendentals=scores)
+
+
 def local(head_count, query_rows, key_rows, value_rows, out_gain):
     index = lax.axis_index("ctx")
     place = jnp.stack([index >> 3, (index >> 1) & (CHIPS_Y - 1), index & 1]).astype(jnp.int32)
 
-    packed = call(pack_summary, jax.ShapeDtypeStruct((SLAB, 4 * SUMMARY, HALF), BF16), [VMEM] * 2)(key_rows, value_rows)
+    summary_rows = [pl.BlockSpec((SUMMARY, 2 * HALF), lambda _, block=block: (block, 0)) for block in (15, 31)]
+    packed = pl.pallas_call(
+        pack_summary,
+        grid=(1,),
+        out_shape=jax.ShapeDtypeStruct((SLAB, 4 * SUMMARY, HALF), BF16),
+        in_specs=summary_rows * 2,
+        out_specs=pl.BlockSpec((SLAB, 4 * SUMMARY, HALF), lambda _: (0, 0, 0)),
+    )(key_rows, key_rows, value_rows, value_rows)
     slab = lax.all_to_all(packed, "ctx", 0, 0, axis_index_groups=groups("yc"), tiled=True)
     to_other = call(pack_other, jax.ShapeDtypeStruct((3 * ROWS, HALF), BF16), [SMEM] + [VMEM] * 3)(
         place, query_rows, key_rows, value_rows
     )
     from_other = swap_cores(to_other)
-    slabs = lax.all_to_all(
-        jnp.broadcast_to(slab[None], (CHIPS_Z, *slab.shape)), "ctx", 0, 0, axis_index_groups=groups("z"), tiled=True
-    )
-
+    up, down, arrived = slab, slab, []
+    for step in range(1, 5):
+        if step == 4:
+            up, down = up[: SLAB // 2], down[SLAB // 2 :]
+        up, down = pass_on(up, step, 1), pass_on(down, step, -1)
+        arrived.append((up, down))
+
+    state = (
+        jax.ShapeDtypeStruct((VIRTUAL, 1, ROWS), F32),
+        jax.ShapeDtypeStruct((VIRTUAL, 1, ROWS), F32),
+        jax.ShapeDtypeStruct((VIRTUAL, HEAD_DIM, ROWS), F32),
+    )
+    queries, *now = call(
+        start_attention,
+        (jax.ShapeDtypeStruct((VIRTUAL, ROWS, HEAD_DIM), BF16), *state),
+        [SMEM] + [VMEM] * 5,
+        cost=cost_of(2),
+    )(place, query_rows, key_rows, value_rows, from_other, slab)
+    for steps in ((1, 2), (3,)):
+        slabs = [part for step in steps for part in arrived[step - 1]]
+        now = call(
+            functools.partial(go_on, steps),
+            state,
+            [SMEM] + [VMEM] * (4 + len(slabs)),
+            cost=cost_of(len(slabs)),
+            input_output_aliases={2 + len(slabs) + i: i for i in range(3)},
+        )(place, queries, *slabs, *now)
     attended = jax.ShapeDtypeStruct((2, HEAD_DIM, ROWS), F32)
     own, other, squares = call(
-        attend_all,
+        functools.partial(end_attention, (4,)),
         (attended, attended, jax.ShapeDtypeStruct((CORES, head_count, ROWS), F32)),
-        [SMEM] + [VMEM] * 5,
-        scratch=[
-            pltpu.VMEM((VIRTUAL, ROWS, HEAD_DIM), BF16),
-            pltpu.VMEM((VIRTUAL, 1, ROWS), F32),
-            pltpu.VMEM((VIRTUAL, 1, ROWS), F32),
-            pltpu.VMEM((VIRTUAL, HEAD_DIM, ROWS), F32),
-        ],
-    )(place, query_rows, key_rows, value_rows, from_other, slabs)
+        [SMEM] + [VMEM] * 6,
+        scratch=[pltpu.VMEM(part.shape, F32) for part in state],
+    )(place, queries, *arrived[3], *now)
     back = swap_cores(other)
     chips = [
         [(chip * CORES + core) * head_count + head for core in range(CORES) for head in range(head_count)]

time: 106 us -> 83.4 us (0.79)
  the two profiles are of different devices: /device:TPU:1 before, /device:TPU:448 now
where the time goes in v2:
time: 83.4 us; the launch traced here: 82.9 us
  starting transfers between devices  26.2 us (31%)
  waiting for transfers between devices  23.3 us (28%)
  Pallas kernels  21.7 us (26%)
  blocking collectives  10.6 us (13%)
    ppermute x8, starting transfers between devices, pass_on(): return lax.ppermute(array, 'ctx', pairs)  14.7 us
    ppermute x8, waiting for transfers between devices, pass_on(): return lax.ppermute(array, 'ctx', pairs)  14.3 us
    all_to_all x1, blocking collectives, local(): lax.all_to_all(squares.reshape(CORES * head_count, ROWS), ('ctx', 'head')...  10.6 us
    pallas_call x2, Pallas kernels, local(): call(functools.partial(go_on, steps), state, [SMEM] + [VMEM] * (4 + len(s...  10.4 us
    all_to_all x1, waiting for transfers between devices, local(): lax.all_to_all(packed, 'ctx', 0, 0, axis_index_groups=groups('yc'), tiled...  8.99 us
    all_to_all x1, starting transfers between devices, local(): lax.all_to_all(packed, 'ctx', 0, 0, axis_index_groups=groups('yc'), tiled...  7.23 us
    ppermute x2, starting transfers between devices, swap_cores(): return lax.ppermute(array, 'ctx', pairs)  4.33 us
    pallas_call x1, Pallas kernels, local(): call(start_attention, (jax.ShapeDtypeStruct((VIRTUAL, ROWS, HEAD_DIM), BF...  4.2 us
  transfers between devices with their start and end apart: 11, of which 6 were waited for; matrix products, arithmetic and copies ran while one was open for 0% of the time, Pallas kernels for 18%

profile of v2, /device:TPU:448, one launch (start us, length us, event | category | flops | bytes accessed | tf_op | source)
XLA Modules:
  0.0 82.9 jit_solution(18380683038463502130)
XLA Ops:
  0.0 1.6 %shard_map.47 = bf16[8,64,256]{2,1,0:T(8,128)(2,1)} custom-call(bf16[512,512]{1,0:T(8,128)(2,1)} %key_ref.3, bf16[512,512]{1,0:T(8,128)(2,1)} %key_ref.3, bf16[512,512]{1,0:T(8,128)(2,1)} %value_ref.3, bf16[512,512]{1,0:T(8,128)(2,1)} %value_ref.3), custom_call_target="tpu_custom_call" | custom-call | tf_op jit(solution)/shard_map/pallas_call | solution.py:208
  1.6 7.2 %all-to-all-start = ((bf16[8,64,256]{2,1,0:T(8,128)(2,1)}), bf16[8,64,256]{2,1,0:T(8,128)(2,1)S(1)}, u32[]{:S(2)}, u32[]{:S(2)}) async-start(bf16[8,64,256]{2,1,0:T(8,128)(2,1)} %shard_map.47), calls=%async_computation | async-start | bytes 524288 | tf_op jit(solution)/shard_map/all_to_all | solution.py:215
  8.8 0.1 pad_add_fusion.place_ref
  8.9 0.6 shard_map.46
  9.5 2.4 %collective-permute-start = (bf16[1536,256]{1,0:T(8,128)(2,1)S(1)}, bf16[1536,256]{1,0:T(8,128)(2,1)S(1)}, u32[]{:S(2)}, u32[]{:S(2)}) collective-permute-start(bf16[1536,256]{1,0:T(8,128)(2,1)S(1)} %shard_map.46), channel_id=1, source_target_pairs={{0,8},{8,0},{16,24},{24,16},{32,40},{40,32},{48,56},{56,48},{64,72... | collective-permute-start | bytes 2359304 | tf_op jit(solution)/shard_map/ppermute | solution.py:183
  11.9 9.0 %all-to-all-done.slab_ref = bf16[8,64,256]{2,1,0:T(8,128)(2,1)S(1)} async-done(((bf16[8,64,256]{2,1,0:T(8,128)(2,1)}), bf16[8,64,256]{2,1,0:T(8,128)(2,1)S(1)}, u32[]{:S(2)}, u32[]{:S(2)}) %all-to-all-start) | async-done | bytes 262176 | tf_op jit(solution)/shard_map/all_to_all | solution.py:215
  20.9 1.3 %collective-permute-start.1 = (bf16[8,64,256]{2,1,0:T(8,128)(2,1)S(1)}, bf16[8,64,256]{2,1,0:T(8,128)(2,1)S(1)}, u32[]{:S(2)}, u32[]{:S(2)}) collective-permute-start(bf16[8,64,256]{2,1,0:T(8,128)(2,1)S(1)} %all-to-all-done.slab_ref), channel_id=1, source_target_pairs={{0,64},{8,72},{16,80},{24,88},{32,96},{40,104},{48,112},{56,120},{... | collective-permute-start | bytes 786440 | tf_op jit(solution)/shard_map/ppermute | solution.py:195
  22.2 1.3 %collective-permute-start.5 = (bf16[8,64,256]{2,1,0:T(8,128)(2,1)S(1)}, bf16[8,64,256]{2,1,0:T(8,128)(2,1)S(1)}, u32[]{:S(2)}, u32[]{:S(2)}) collective-permute-start(bf16[8,64,256]{2,1,0:T(8,128)(2,1)S(1)} %all-to-all-done.slab_ref), channel_id=1, source_target_pairs={{0,448},{8,456},{16,464},{24,472},{32,480},{40,488},{48,496},{56,5... | collective-permute-start | bytes 786440 | tf_op jit(solution)/shard_map/ppermute | solution.py:195
  23.5 6.5 %collective-permute-done.1.refs_0_ = bf16[8,64,256]{2,1,0:T(8,128)(2,1)S(1)} collective-permute-done((bf16[8,64,256]{2,1,0:T(8,128)(2,1)S(1)}, bf16[8,64,256]{2,1,0:T(8,128)(2,1)S(1)}, u32[]{:S(2)}, u32[]{:S(2)}) %collective-permute-start.1) | collective-permute-done | bytes 262176 | tf_op jit(solution)/shard_map/ppermute | solution.py:195
  30.0 1.3 %collective-permute-start.2 = (bf16[8,64,256]{2,1,0:T(8,128)(2,1)S(1)}, bf16[8,64,256]{2,1,0:T(8,128)(2,1)S(1)}, u32[]{:S(2)}, u32[]{:S(2)}) collective-permute-start(bf16[8,64,256]{2,1,0:T(8,128)(2,1)S(1)} %collective-permute-done.1.refs_0_), channel_id=1, source_target_pairs={{64,128},{72,136},{80,144},{88,152},{96,160},{104,168},{112,176},{... | collective-permute-start | bytes 786440 | tf_op jit(solution)/shard_map/ppermute | solution.py:195
  31.3 1.2 %collective-permute-done.5.refs_1_ = bf16[8,64,256]{2,1,0:T(8,128)(2,1)S(1)} collective-permute-done((bf16[8,64,256]{2,1,0:T(8,128)(2,1)S(1)}, bf16[8,64,256]{2,1,0:T(8,128)(2,1)S(1)}, u32[]{:S(2)}, u32[]{:S(2)}) %collective-permute-start.5) | collective-permute-done | bytes 262176 | tf_op jit(solution)/shard_map/ppermute | solution.py:195
  32.5 3.3 %collective-permute-start.6 = (bf16[8,64,256]{2,1,0:T(8,128)(2,1)S(1)}, bf16[8,64,256]{2,1,0:T(8,128)(2,1)S(1)}, u32[]{:S(2)}, u32[]{:S(2)}) collective-permute-start(bf16[8,64,256]{2,1,0:T(8,128)(2,1)S(1)} %collective-permute-done.5.refs_1_), channel_id=1, source_target_pairs={{0,448},{8,456},{16,464},{24,472},{32,480},{40,488},{48,496},{56,5... | collective-permute-start | bytes 786440 | tf_op jit(solution)/shard_map/ppermute | solution.py:195
  35.9 2.4 %collective-permute-done.2.refs_2_ = bf16[8,64,256]{2,1,0:T(8,128)(2,1)S(1)} collective-permute-done((bf16[8,64,256]{2,1,0:T(8,128)(2,1)S(1)}, bf16[8,64,256]{2,1,0:T(8,128)(2,1)S(1)}, u32[]{:S(2)}, u32[]{:S(2)}) %collective-permute-start.2) | collective-permute-done | bytes 262176 | tf_op jit(solution)/shard_map/ppermute | solution.py:195
  38.3 1.3 %collective-permute-start.3 = (bf16[8,64,256]{2,1,0:T(8,128)(2,1)S(1)}, bf16[8,64,256]{2,1,0:T(8,128)(2,1)S(1)}, u32[]{:S(2)}, u32[]{:S(2)}) collective-permute-start(bf16[8,64,256]{2,1,0:T(8,128)(2,1)S(1)} %collective-permute-done.2.refs_2_), channel_id=1, source_target_pairs={{128,192},{136,200},{144,208},{152,216},{160,224},{168,232},{176,2... | collective-permute-start | bytes 786440 | tf_op jit(solution)/shard_map/ppermute | solution.py:195
  39.5 2.4 %collective-permute-done.6.refs_3_ = bf16[8,64,256]{2,1,0:T(8,128)(2,1)S(1)} collective-permute-done((bf16[8,64,256]{2,1,0:T(8,128)(2,1)S(1)}, bf16[8,64,256]{2,1,0:T(8,128)(2,1)S(1)}, u32[]{:S(2)}, u32[]{:S(2)}) %collective-permute-start.6) | collective-permute-done | bytes 262176 | tf_op jit(solution)/shard_map/ppermute | solution.py:195
  42.0 2.1 %collective-permute-start.7 = (bf16[8,64,256]{2,1,0:T(8,128)(2,1)S(1)}, bf16[8,64,256]{2,1,0:T(8,128)(2,1)S(1)}, u32[]{:S(2)}, u32[]{:S(2)}) collective-permute-start(bf16[8,64,256]{2,1,0:T(8,128)(2,1)S(1)} %collective-permute-done.6.refs_3_), channel_id=1, source_target_pairs={{0,448},{8,456},{16,464},{24,472},{32,480},{40,488},{48,496},{56,5... | collective-permute-start | bytes 786440 | tf_op jit(solution)/shard_map/ppermute | solution.py:195
  44.1 0.0 collective-permute-done.other_in_ref
  44.1 4.2 %shard_map.48 = (bf16[4,512,128]{2,1,0:T(8,128)(2,1)S(1)}, f32[4,1,512]{2,1,0:T(1,128)S(1)}, f32[4,1,512]{2,1,0:T(1,128)S(1)}, f32[4,128,512]{2,1,0:T(8,128)S(1)}) custom-call(s32[3]{0:T(128)S(1)} %pad_add_fusion.place_ref, bf16[512,512]{1,0:T(8,128)(2,1)S(1)} %copy-done.2, bf16[512,512]{1,0:T(8,128)(2,1)S(1)} %copy-done, bf16[512,512]{1,0:T(8,128)(2,1)S(1)} %copy-done.1, ...), custom_call_target="tpu_custom_call" | custom-call | flops 536870912 | bytes 4194304 | tf_op jit(solution)/shard_map/pallas_call | solution.py:232
  48.3 0.0 collective-permute-done.3.refs_0_
  48.4 1.3 %collective-permute-start.4 = (bf16[4,64,256]{2,1,0:T(8,128)(2,1)S(1)}, bf16[4,64,256]{2,1,0:T(8,128)(2,1)S(1)}, u32[]{:S(2)}, u32[]{:S(2)}) collective-permute-start(bf16[4,64,256]{2,1,0:T(8,128)(2,1)S(1)} %slice.8), channel_id=1, source_target_pairs={{192,256},{200,264},{208,272},{216,280},{224,288},{232,296},{240,3... | collective-permute-start | bytes 393224 | tf_op jit(solution)/shard_map/ppermute | solution.py:195
  49.7 1.8 %collective-permute-done.7.refs_1_ = bf16[8,64,256]{2,1,0:T(8,128)(2,1)S(1)} collective-permute-done((bf16[8,64,256]{2,1,0:T(8,128)(2,1)S(1)}, bf16[8,64,256]{2,1,0:T(8,128)(2,1)S(1)}, u32[]{:S(2)}, u32[]{:S(2)}) %collective-permute-start.7) | collective-permute-done | bytes 262176 | tf_op jit(solution)/shard_map/ppermute | solution.py:195
  51.5 2.8 %collective-permute-start.8 = (bf16[4,64,256]{2,1,0:T(8,128)(2,1)S(1)}, bf16[4,64,256]{2,1,0:T(8,128)(2,1)S(1)}, u32[]{:S(2)}, u32[]{:S(2)}) collective-permute-start(bf16[4,64,256]{2,1,0:T(8,128)(2,1)S(1)} %slice.9), channel_id=1, source_target_pairs={{0,448},{8,456},{16,464},{24,472},{32,480},{40,488},{48,496},{56,5... | collective-permute-start | bytes 393224 | tf_op jit(solution)/shard_map/ppermute | solution.py:195
  54.3 6.7 %shard_map.49 = (f32[4,1,512]{2,1,0:T(1,128)S(1)}, f32[4,1,512]{2,1,0:T(1,128)S(1)}, f32[4,128,512]{2,1,0:T(8,128)S(1)}) custom-call(s32[3]{0:T(128)S(1)} %pad_add_fusion.place_ref, bf16[4,512,128]{2,1,0:T(8,128)(2,1)S(1)} %get-tuple-element.18.queries_ref, ...), custom_call_target="tpu_custom_call", output_to_operand_aliasing={{0}: (6, {}), {1}: (7, {}), {2}: (8, {})} | custom-call | flops 1073741824 | bytes 8388608 | tf_op jit(solution)/shard_map/pallas_call | solution.py:240
  61.0 3.7 %shard_map.50 = (f32[4,1,512]{2,1,0:T(1,128)S(1)}, f32[4,1,512]{2,1,0:T(1,128)S(1)}, f32[4,128,512]{2,1,0:T(8,128)S(1)}) custom-call(s32[3]{0:T(128)S(1)} %pad_add_fusion.place_ref, bf16[4,512,128]{2,1,0:T(8,128)(2,1)S(1)} %get-tuple-element.18.queries_ref, ...), custom_call_target="tpu_custom_call", output_to_operand_aliasing={{0}: (4, {}), {1}: (5, {}), {2}: (6, {})} | custom-call | flops 536870912 | bytes 4194304 | tf_op jit(solution)/shard_map/pallas_call | solution.py:240
  64.7 0.0 collective-permute-done.4.refs_0_
  64.7 0.0 collective-permute-done.8.refs_1_
  64.7 3.2 %shard_map.51 = (f32[2,128,512]{2,1,0:T(8,128)S(1)}, f32[2,128,512]{2,1,0:T(8,128)S(1)}, f32[2,8,512]{2,1,0:T(8,128)S(1)}) custom-call(s32[3]{0:T(128)S(1)} %pad_add_fusion.place_ref, bf16[4,512,128]{2,1,0:T(8,128)(2,1)S(1)} %get-tuple-element.18.queries_ref, bf16[4,64,256]{2,1,0:T(8,128)(2,1)S(1)} %collective-permute-done.4.refs_0_, ...), custom_call_target="tpu_custom_call" | custom-call | tf_op jit(solution)/shard_map/pallas_call | solution.py:248
  67.9 1.9 %collective-permute-start.9 = (f32[2,128,512]{2,1,0:T(8,128)S(1)}, f32[2,128,512]{2,1,0:T(8,128)S(1)}, u32[]{:S(2)}, u32[]{:S(2)}) collective-permute-start(f32[2,128,512]{2,1,0:T(8,128)S(1)} %get-tuple-element.29), channel_id=1, source_target_pairs={{0,8},{8,0},{16,24},{24,16},{32,40},{40,32},{48,56},{56,48},{64,72... | collective-permute-start | bytes 1572872 | tf_op jit(solution)/shard_map/ppermute | solution.py:183
  69.9 10.6 %all_to_all.16 = f32[16,1,512]{2,1,0:T(1,128)S(1)} all-to-all(f32[16,1,512]{2,1,0:T(1,128)S(1)} %copy.11), channel_id=1, replica_groups={{0,1,2,3,4,5,6,7,8,9,10,11,12,13,14,15},{16,17,18,19,20,21,22,23,24,25,..., dimensions={0} | all-to-all | bytes 65536 | tf_op jit(solution)/shard_map/all_to_all | solution.py:259
  80.5 0.0 collective-permute-done.9.other_ref
  80.5 0.7 copy-done.3
  81.2 1.7 %shard_map.52 = bf16[512,512]{1,0:T(8,128)(2,1)} custom-call(s32[3]{0:T(128)S(1)} %pad_add_fusion.place_ref, f32[2,128,512]{2,1,0:T(8,128)S(1)} %get-tuple-element.28.own_ref, f32[2,128,512]{2,1,0:T(8,128)S(1)} %collective-permute-done.9.other_ref, f32[16,512]{1,0:T(8,128)S(1)} %bitcast.8, f32[1,512]{1,0:T(1,128)S(1)} %bitcast.10), custom_call_target="tpu_custom_call" | custom-call | tf_op jit(solution)/shard_map/pallas_call | solution.py:262
  (11 shorter events, 0.1 us)
Async XLA Ops:
  0.0 8.9 %copy-start.1 = (bf16[512,512]{1,0:T(8,128)(2,1)S(1)}, bf16[512,512]{1,0:T(8,128)(2,1)}, u32[]{:S(2)}) copy-start(bf16[512,512]{1,0:T(8,128)(2,1)} %value_ref.3) | copy-start | bytes 1572868
  0.0 8.9 %copy-start.2 = (bf16[512,512]{1,0:T(8,128)(2,1)S(1)}, bf16[512,512]{1,0:T(8,128)(2,1)}, u32[]{:S(2)}) copy-start(bf16[512,512]{1,0:T(8,128)(2,1)} %query_ref.3) | copy-start | bytes 1572868
  1.6 7.3 %copy-start = (bf16[512,512]{1,0:T(8,128)(2,1)S(1)}, bf16[512,512]{1,0:T(8,128)(2,1)}, u32[]{:S(2)}) copy-start(bf16[512,512]{1,0:T(8,128)(2,1)} %key_ref.3) | copy-start | bytes 1572868
  1.6 19.3 %all-to-all-start = ((bf16[8,64,256]{2,1,0:T(8,128)(2,1)}), bf16[8,64,256]{2,1,0:T(8,128)(2,1)S(1)}, u32[]{:S(2)}, u32[]{:S(2)}) async-start(bf16[8,64,256]{2,1,0:T(8,128)(2,1)} %shard_map.47), calls=%async_computation | async-start | bytes 524288 | tf_op jit(solution)/shard_map/all_to_all | solution.py:215
  9.5 34.6 %collective-permute-start = (bf16[1536,256]{1,0:T(8,128)(2,1)S(1)}, bf16[1536,256]{1,0:T(8,128)(2,1)S(1)}, u32[]{:S(2)}, u32[]{:S(2)}) collective-permute-start(bf16[1536,256]{1,0:T(8,128)(2,1)S(1)} %shard_map.46), channel_id=1, source_target_pairs={{0,8},{8,0},{16,24},{24,16},{32,40},{40,32},{48,56},{56,48},{64,72... | collective-permute-start | bytes 2359304 | tf_op jit(solution)/shard_map/ppermute | solution.py:183
  20.9 9.1 %collective-permute-start.1 = (bf16[8,64,256]{2,1,0:T(8,128)(2,1)S(1)}, bf16[8,64,256]{2,1,0:T(8,128)(2,1)S(1)}, u32[]{:S(2)}, u32[]{:S(2)}) collective-permute-start(bf16[8,64,256]{2,1,0:T(8,128)(2,1)S(1)} %all-to-all-done.slab_ref), channel_id=1, source_target_pairs={{0,64},{8,72},{16,80},{24,88},{32,96},{40,104},{48,112},{56,120},{... | collective-permute-start | bytes 786440 | tf_op jit(solution)/shard_map/ppermute | solution.py:195
  22.2 10.3 %collective-permute-start.5 = (bf16[8,64,256]{2,1,0:T(8,128)(2,1)S(1)}, bf16[8,64,256]{2,1,0:T(8,128)(2,1)S(1)}, u32[]{:S(2)}, u32[]{:S(2)}) collective-permute-start(bf16[8,64,256]{2,1,0:T(8,128)(2,1)S(1)} %all-to-all-done.slab_ref), channel_id=1, source_target_pairs={{0,448},{8,456},{16,464},{24,472},{32,480},{40,488},{48,496},{56,5... | collective-permute-start | bytes 786440 | tf_op jit(solution)/shard_map/ppermute | solution.py:195
  30.0 8.3 %collective-permute-start.2 = (bf16[8,64,256]{2,1,0:T(8,128)(2,1)S(1)}, bf16[8,64,256]{2,1,0:T(8,128)(2,1)S(1)}, u32[]{:S(2)}, u32[]{:S(2)}) collective-permute-start(bf16[8,64,256]{2,1,0:T(8,128)(2,1)S(1)} %collective-permute-done.1.refs_0_), channel_id=1, source_target_pairs={{64,128},{72,136},{80,144},{88,152},{96,160},{104,168},{112,176},{... | collective-permute-start | bytes 786440 | tf_op jit(solution)/shard_map/ppermute | solution.py:195
  32.5 9.5 %collective-permute-start.6 = (bf16[8,64,256]{2,1,0:T(8,128)(2,1)S(1)}, bf16[8,64,256]{2,1,0:T(8,128)(2,1)S(1)}, u32[]{:S(2)}, u32[]{:S(2)}) collective-permute-start(bf16[8,64,256]{2,1,0:T(8,128)(2,1)S(1)} %collective-permute-done.5.refs_1_), channel_id=1, source_target_pairs={{0,448},{8,456},{16,464},{24,472},{32,480},{40,488},{48,496},{56,5... | collective-permute-start | bytes 786440 | tf_op jit(solution)/shard_map/ppermute | solution.py:195
  38.3 10.1 %collective-permute-start.3 = (bf16[8,64,256]{2,1,0:T(8,128)(2,1)S(1)}, bf16[8,64,256]{2,1,0:T(8,128)(2,1)S(1)}, u32[]{:S(2)}, u32[]{:S(2)}) collective-permute-start(bf16[8,64,256]{2,1,0:T(8,128)(2,1)S(1)} %collective-permute-done.2.refs_2_), channel_id=1, source_target_pairs={{128,192},{136,200},{144,208},{152,216},{160,224},{168,232},{176,2... | collective-permute-start | bytes 786440 | tf_op jit(solution)/shard_map/ppermute | solution.py:195
  42.0 9.5 %collective-permute-start.7 = (bf16[8,64,256]{2,1,0:T(8,128)(2,1)S(1)}, bf16[8,64,256]{2,1,0:T(8,128)(2,1)S(1)}, u32[]{:S(2)}, u32[]{:S(2)}) collective-permute-start(bf16[8,64,256]{2,1,0:T(8,128)(2,1)S(1)} %collective-permute-done.6.refs_3_), channel_id=1, source_target_pairs={{0,448},{8,456},{16,464},{24,472},{32,480},{40,488},{48,496},{56,5... | collective-permute-start | bytes 786440 | tf_op jit(solution)/shard_map/ppermute | solution.py:195
  48.4 16.3 %collective-permute-start.4 = (bf16[4,64,256]{2,1,0:T(8,128)(2,1)S(1)}, bf16[4,64,256]{2,1,0:T(8,128)(2,1)S(1)}, u32[]{:S(2)}, u32[]{:S(2)}) collective-permute-start(bf16[4,64,256]{2,1,0:T(8,128)(2,1)S(1)} %slice.8), channel_id=1, source_target_pairs={{192,256},{200,264},{208,272},{216,280},{224,288},{232,296},{240,3... | collective-permute-start | bytes 393224 | tf_op jit(solution)/shard_map/ppermute | solution.py:195
  51.5 13.2 %collective-permute-start.8 = (bf16[4,64,256]{2,1,0:T(8,128)(2,1)S(1)}, bf16[4,64,256]{2,1,0:T(8,128)(2,1)S(1)}, u32[]{:S(2)}, u32[]{:S(2)}) collective-permute-start(bf16[4,64,256]{2,1,0:T(8,128)(2,1)S(1)} %slice.9), channel_id=1, source_target_pairs={{0,448},{8,456},{16,464},{24,472},{32,480},{40,488},{48,496},{56,5... | collective-permute-start | bytes 393224 | tf_op jit(solution)/shard_map/ppermute | solution.py:195
  67.9 12.6 %collective-permute-start.9 = (f32[2,128,512]{2,1,0:T(8,128)S(1)}, f32[2,128,512]{2,1,0:T(8,128)S(1)}, u32[]{:S(2)}, u32[]{:S(2)}) collective-permute-start(f32[2,128,512]{2,1,0:T(8,128)S(1)} %get-tuple-element.29), channel_id=1, source_target_pairs={{0,8},{8,0},{16,24},{24,16},{32,40},{40,32},{48,56},{56,48},{64,72... | collective-permute-start | bytes 1572872 | tf_op jit(solution)/shard_map/ppermute | solution.py:183
  80.5 0.7 copy-start.3

commit v3 on v2

--- a/solution.py
+++ b/solution.py
@@ -21,7 +21,7 @@
 VIRTUAL = 4
 VMEM = pl.BlockSpec(memory_space=pltpu.VMEM)
 SMEM = pl.BlockSpec(memory_space=pltpu.SMEM)
-LIMIT = 48 * 1024 * 1024
+LIMIT = 24 * 1024 * 1024
 
 F32 = jnp.float32
 BF16 = jnp.bfloat16
@@ -61,66 +61,80 @@
 
 def fold_slab(queries, state, slab, first_blocks):
     max_ref, sum_ref, acc_ref = state
+    parts = [slab_keys(slab, head) for head in range(2)]
+    staged = []
     for virtual in range(VIRTUAL):
-        keys, values = slab_keys(slab, virtual % 2)
-        scores = rows_dot(keys, queries[virtual]) * SCALE
+        scores = rows_dot(parts[virtual % 2][0], queries[virtual]) * SCALE
         if first_blocks is not None:
             shape = scores.shape
             key_block = lax.broadcasted_iota(jnp.int32, shape, 0) // SUMMARY
             query_block = first_blocks[virtual // 2] + lax.broadcasted_iota(jnp.int32, shape, 1) // BLOCK
-            allowed = key_block < query_block
-            scores = jnp.where(allowed, scores, MINUS)
+            scores = jnp.where(key_block < query_block, scores, MINUS)
         old_max = max_ref[virtual]
         new_max = jnp.maximum(old_max, jnp.max(scores, axis=0, keepdims=True))
-        weights = jnp.exp2(scores - new_max)
-        shrink = jnp.exp2(old_max - new_max)
+        staged.append((jnp.exp2(scores - new_max), jnp.exp2(old_max - new_max)))
         max_ref[virtual] = new_max
+    for virtual, (weights, shrink) in enumerate(staged):
         sum_ref[virtual] = sum_ref[virtual] * shrink + jnp.sum(weights, axis=0, keepdims=True)
-        acc_ref[virtual] = acc_ref[virtual] * shrink + columns_dot(values, weights.astype(BF16))
-
-
-def band(query_ref, key_ref, value_ref, mine, other_ref, state, queries_ref):
+        acc_ref[virtual] = acc_ref[virtual] * shrink + columns_dot(parts[virtual % 2][1], weights.astype(BF16))
+
+
+def band(pieces, first, state, queries_ref):
     max_ref, sum_ref, acc_ref = state
     shape = (BLOCK, BLOCK)
     causal = lax.broadcasted_iota(jnp.int32, shape, 0) <= lax.broadcasted_iota(jnp.int32, shape, 1)
-    for virtual in range(VIRTUAL):
-        owner, head = divmod(virtual, 2)
+    staged = []
+    for head in range(2):
         for block in range(2):
-            rows = slice(block * BLOCK, (block + 1) * BLOCK)
-            if owner == 0:
-                columns = pl.ds(mine + head * HEAD_DIM, HEAD_DIM)
-                query, key, value = (ref[rows, columns] for ref in (query_ref, key_ref, value_ref))
-            else:
-                columns = slice(head * HEAD_DIM, (head + 1) * HEAD_DIM)
-                query, key, value = (
-                    other_ref[part * ROWS + block * BLOCK : part * ROWS + (block + 1) * BLOCK, columns]
-                    for part in range(3)
-                )
+            virtual, rows = first + head, slice(block * BLOCK, (block + 1) * BLOCK)
+            query, key, value = pieces(head, block)
             queries_ref[virtual, rows] = query
             scores = jnp.where(causal, rows_dot(key, query) * SCALE, MINUS)
             new_max = jnp.max(scores, axis=0, keepdims=True)
-            weights = jnp.exp2(scores - new_max)
             max_ref[virtual, :, rows] = new_max
-            sum_ref[virtual, :, rows] = jnp.sum(weights, axis=0, keepdims=True)
-            acc_ref[virtual, :, rows] = columns_dot(value, weights.astype(BF16))
-
-
-def finish(core, state, own_ref, other_ref, square_ref):
+            staged.append((virtual, rows, value, jnp.exp2(scores - new_max)))
+    for virtual, rows, value, weights in staged:
+        sum_ref[virtual, :, rows] = jnp.sum(weights, axis=0, keepdims=True)
+        acc_ref[virtual, :, rows] = columns_dot(value, weights.astype(BF16))
+
+
+def finish(core, gain_ref, state, own_ref, other_ref, square_ref):
     _, sum_ref, acc_ref = state
+    mine = pl.multiple_of(core * HALF, HALF)
     for owner, ref in enumerate((own_ref, other_ref)):
         total = jnp.zeros((1, ROWS), F32)
         for head in range(2):
             virtual = owner * 2 + head
-            attended = acc_ref[virtual] / sum_ref[virtual]
-            ref[head] = attended
+            gain = jnp.broadcast_to(gain_ref[:, pl.ds(mine + head * HEAD_DIM, HEAD_DIM)], (8, HEAD_DIM))
+            attended = acc_ref[virtual] * (1.0 / sum_ref[virtual])
+            ref[head] = attended * jnp.transpose(gain)[:, :1]
             total += jnp.sum(attended * attended, axis=0, keepdims=True)
         square_ref[core if owner == 0 else 1 - core] = jnp.broadcast_to(total, square_ref.shape[1:])
 
 
-def start_attention(place_ref, query_ref, key_ref, value_ref, other_in_ref, slab_ref, queries_ref, *state):
+def start_attention(place_ref, query_ref, key_ref, value_ref, queries_ref, *state):
+    mine = pl.multiple_of(place_ref[2] * HALF, HALF)
+
+    def pieces(head, block):
+        rows, columns = slice(block * BLOCK, (block + 1) * BLOCK), pl.ds(mine + head * HEAD_DIM, HEAD_DIM)
+        return (ref[rows, columns] for ref in (query_ref, key_ref, value_ref))
+
+    band(pieces, 0, state, queries_ref)
+
+
+def own_slab(place_ref, other_in_ref, slab_ref, *refs):
+    inputs, outs = refs[:4], refs[4:]
+    queries_ref, *state = outs
+    for ref_in, ref in zip(inputs, outs):
+        ref[:2] = ref_in[...]
+
+    def pieces(head, block):
+        columns = slice(head * HEAD_DIM, (head + 1) * HEAD_DIM)
+        starts = [part * ROWS + block * BLOCK for part in range(3)]
+        return (other_in_ref[start : start + BLOCK, columns] for start in starts)
+
+    band(pieces, 2, state, queries_ref)
     chip, core = place_ref[1], place_ref[2]
-    mine = pl.multiple_of(core * HALF, HALF)
-    band(query_ref, key_ref, value_ref, mine, other_in_ref, state, queries_ref)
     first_blocks = [(chip * CORES + core) * 2, (chip * CORES + 1 - core) * 2]
     fold_slab(queries_ref, state, slab_ref, first_blocks)
 
@@ -138,13 +152,13 @@
                 fold_slab(queries_ref, state, slab, None)
 
 
-def end_attention(steps, place_ref, queries_ref, *refs):
+def end_attention(steps, place_ref, gain_ref, queries_ref, *refs):
     inputs, outs, state = refs[:-6], refs[-6:-3], refs[-3:]
     go_on(steps, place_ref, queries_ref, *inputs, *state)
-    finish(place_ref[2], state, *outs)
-
-
-def scale_rows(place_ref, own_ref, other_ref, square_ref, gain_ref, out_ref):
+    finish(place_ref[2], gain_ref, state, *outs)
+
+
+def scale_rows(place_ref, own_ref, other_ref, square_ref, out_ref):
     core = place_ref[2]
     total = jnp.sum(square_ref[...], axis=0, keepdims=True)
     scale = lax.rsqrt(total * (1.0 / FEATURES) + 1e-06)
@@ -152,8 +166,7 @@
         first = pl.multiple_of((core if owner == 0 else 1 - core) * HALF, HALF)
         for head in range(2):
             columns = pl.ds(first + head * HEAD_DIM, HEAD_DIM)
-            rows = jnp.transpose(ref[head] * scale)
-            out_ref[:, columns] = (rows * gain_ref[:, columns]).astype(BF16)
+            out_ref[:, columns] = jnp.transpose(ref[head] * scale).astype(BF16)
 
 
 def call(body, out_shape, in_specs, scratch=(), cost=None, **more):
@@ -195,9 +208,8 @@
     return lax.ppermute(array, "ctx", pairs)
 
 
-def cost_of(slabs):
-    scores = VIRTUAL * ROWS * SLAB * 2 * SUMMARY * slabs
-    return pl.CostEstimate(flops=4 * HEAD_DIM * scores, bytes_accessed=slabs * 2**21, transcendentals=scores)
+FIRST_COST = pl.CostEstimate(flops=3 * 10**10, bytes_accessed=2**20, transcendentals=2**20)
+COST = pl.CostEstimate(flops=3 * 10**9, bytes_accessed=2**20, transcendentals=2**20)
 
 
 def local(head_count, query_rows, key_rows, value_rows, out_gain):
@@ -213,44 +225,50 @@
         out_specs=pl.BlockSpec((SLAB, 4 * SUMMARY, HALF), lambda _: (0, 0, 0)),
     )(key_rows, key_rows, value_rows, value_rows)
     slab = lax.all_to_all(packed, "ctx", 0, 0, axis_index_groups=groups("yc"), tiled=True)
+    query_rows, key_rows, value_rows, _ = lax.optimization_barrier((query_rows, key_rows, value_rows, packed))
     to_other = call(pack_other, jax.ShapeDtypeStruct((3 * ROWS, HALF), BF16), [SMEM] + [VMEM] * 3)(
         place, query_rows, key_rows, value_rows
     )
     from_other = swap_cores(to_other)
+
+    def attention(virtuals):
+        return (
+            jax.ShapeDtypeStruct((virtuals, ROWS, HEAD_DIM), BF16),
+            jax.ShapeDtypeStruct((virtuals, 1, ROWS), F32),
+            jax.ShapeDtypeStruct((virtuals, 1, ROWS), F32),
+            jax.ShapeDtypeStruct((virtuals, HEAD_DIM, ROWS), F32),
+        )
+
+    mine = call(start_attention, attention(2), [SMEM] + [VMEM] * 3, cost=FIRST_COST)(place, query_rows, key_rows, value_rows)
+    state = attention(VIRTUAL)[1:]
     up, down, arrived = slab, slab, []
     for step in range(1, 5):
+        if step == 1:
+            up, down, mine = lax.optimization_barrier((up, down, mine))
+        else:
+            up, now = lax.optimization_barrier((up, now))
+            down, now = lax.optimization_barrier((down, now))
         if step == 4:
             up, down = up[: SLAB // 2], down[SLAB // 2 :]
         up, down = pass_on(up, step, 1), pass_on(down, step, -1)
+        if step == 1:
+            queries, *now = call(own_slab, attention(VIRTUAL), [SMEM] + [VMEM] * 6, cost=COST)(place, from_other, slab, *mine)
+        else:
+            now = call(
+                functools.partial(go_on, (step - 1,)),
+                state,
+                [SMEM] + [VMEM] * 6,
+                cost=COST,
+                input_output_aliases={4 + i: i for i in range(3)},
+            )(place, queries, *arrived[-1], *now)
         arrived.append((up, down))
-
-    state = (
-        jax.ShapeDtypeStruct((VIRTUAL, 1, ROWS), F32),
-        jax.ShapeDtypeStruct((VIRTUAL, 1, ROWS), F32),
-        jax.ShapeDtypeStruct((VIRTUAL, HEAD_DIM, ROWS), F32),
-    )
-    queries, *now = call(
-        start_attention,
-        (jax.ShapeDtypeStruct((VIRTUAL, ROWS, HEAD_DIM), BF16), *state),
-        [SMEM] + [VMEM] * 5,
-        cost=cost_of(2),
-    )(place, query_rows, key_rows, value_rows, from_other, slab)
-    for steps in ((1, 2), (3,)):
-        slabs = [part for step in steps for part in arrived[step - 1]]
-        now = call(
-            functools.partial(go_on, steps),
-            state,
-            [SMEM] + [VMEM] * (4 + len(slabs)),
-            cost=cost_of(len(slabs)),
-            input_output_aliases={2 + len(slabs) + i: i for i in range(3)},
-        )(place, queries, *slabs, *now)
     attended = jax.ShapeDtypeStruct((2, HEAD_DIM, ROWS), F32)
     own, other, squares = call(
         functools.partial(end_attention, (4,)),
         (attended, attended, jax.ShapeDtypeStruct((CORES, head_count, ROWS), F32)),
-        [SMEM] + [VMEM] * 6,
+        [SMEM] + [VMEM] * 7,
         scratch=[pltpu.VMEM(part.shape, F32) for part in state],
-    )(place, queries, *arrived[3], *now)
+    )(place, out_gain[None], queries, *arrived[3], *now)
     back = swap_cores(other)
     chips = [
         [(chip * CORES + core) * head_count + head for core in range(CORES) for head in range(head_count)]
@@ -259,8 +277,8 @@
     totals = lax.all_to_all(
         squares.reshape(CORES * head_count, ROWS), ("ctx", "head"), 0, 0, axis_index_groups=chips, tiled=True
     )
-    return call(scale_rows, jax.ShapeDtypeStruct((ROWS, 4 * HEAD_DIM), BF16), [SMEM] + [VMEM] * 4)(
-        place, own, back, totals, out_gain[None]
+    return call(scale_rows, jax.ShapeDtypeStruct((ROWS, 4 * HEAD_DIM), BF16), [SMEM] + [VMEM] * 3)(
+        place, own, back, totals
     )
 
 

time: 83.4 us -> 84.7 us (1.016)
  the two profiles are of different devices: /device:TPU:448 before, /device:TPU:1 now
where the time goes in v3:
time: 84.7 us; the launch traced here: 84.1 us
  starting transfers between devices  48.6 us (57%)
  waiting for transfers between devices  11.1 us (13%)
  blocking collectives  9.98 us (12%)
  Pallas kernels  9.88 us (12%)
  local copies, waits for them, and re-layouts  4.23 us (5%)
    ppermute x8, starting transfers between devices, pass_on(): return lax.ppermute(array, 'ctx', pairs)  28.8 us
    all_to_all x1, starting transfers between devices, local(): lax.all_to_all(packed, 'ctx', 0, 0, axis_index_groups=groups('yc'), tiled...  10.3 us
    all_to_all x1, blocking collectives, local(): lax.all_to_all(squares.reshape(CORES * head_count, ROWS), ('ctx', 'head')...  9.98 us
    ppermute x2, starting transfers between devices, swap_cores(): return lax.ppermute(array, 'ctx', pairs)  9.53 us
    ppermute x8, waiting for transfers between devices, pass_on(): return lax.ppermute(array, 'ctx', pairs)  5.72 us
    all_to_all x1, waiting for transfers between devices, local(): lax.all_to_all(packed, 'ctx', 0, 0, axis_index_groups=groups('yc'), tiled...  5.37 us
    unnamed x17, local copies, waits for them, and re-layouts  4.17 us
    pallas_call x3, Pallas kernels, local(): call(functools.partial(go_on, (step - 1,)), state, [SMEM] + [VMEM] * 6, c...  2.07 us
  transfers between devices with their start and end apart: 11, of which 4 were waited for; matrix products, arithmetic and copies ran while one was open for 0% of the time, Pallas kernels for 7%

profile of v3, /device:TPU:1, one launch (start us, length us, event | category | flops | bytes accessed | tf_op | source)
XLA Modules:
  0.0 84.1 jit_solution(15634926768184407378)
XLA Ops:
  0.0 1.6 %shard_map.46 = bf16[8,64,256]{2,1,0:T(8,128)(2,1)} custom-call(bf16[512,512]{1,0:T(8,128)(2,1)} %key_ref.1, bf16[512,512]{1,0:T(8,128)(2,1)} %key_ref.1, bf16[512,512]{1,0:T(8,128)(2,1)} %value_ref.1, bf16[512,512]{1,0:T(8,128)(2,1)} %value_ref.1), custom_call_target="tpu_custom_call" | custom-call | tf_op jit(solution)/shard_map/pallas_call | solution.py:220
  1.6 10.3 %all-to-all-start = ((bf16[8,64,256]{2,1,0:T(8,128)(2,1)}), bf16[8,64,256]{2,1,0:T(8,128)(2,1)S(1)}, u32[]{:S(2)}, u32[]{:S(2)}) async-start(bf16[8,64,256]{2,1,0:T(8,128)(2,1)} %shard_map.46), calls=%async_computation | async-start | bytes 524288 | tf_op jit(solution)/shard_map/all_to_all | solution.py:227
  11.9 0.1 pad_add_fusion.place_ref
  12.0 0.6 shard_map.47
  12.6 2.0 %collective-permute-start = (bf16[1536,256]{1,0:T(8,128)(2,1)S(1)}, bf16[1536,256]{1,0:T(8,128)(2,1)S(1)}, u32[]{:S(2)}, u32[]{:S(2)}) collective-permute-start(bf16[1536,256]{1,0:T(8,128)(2,1)S(1)} %shard_map.47), channel_id=1, source_target_pairs={{0,8},{8,0},{16,24},{24,16},{32,40},{40,32},{48,56},{56,48},{64,72... | collective-permute-start | bytes 2359304 | tf_op jit(solution)/shard_map/ppermute | solution.py:196
  14.6 1.1 %shard_map.48 = (bf16[2,512,128]{2,1,0:T(8,128)(2,1)S(1)}, f32[2,1,512]{2,1,0:T(1,128)S(1)}, f32[2,1,512]{2,1,0:T(1,128)S(1)}, f32[2,128,512]{2,1,0:T(8,128)S(1)}) custom-call(s32[3]{0:T(128)S(1)} %pad_add_fusion.place_ref, bf16[512,512]{1,0:T(8,128)(2,1)S(1)} %copy-done.2, bf16[512,512]{1,0:T(8,128)(2,1)S(1)} %copy-done, bf16[512,512]{1,0:T(8,128)(2,1)S(1)} %copy-done.1), custom_call_target="tpu_custom_call" | custom-call | flops 30000001024 | bytes 1048576 | tf_op jit(solution)/shard_map/pallas_call | solution.py:242
  15.8 0.0 copy-start.4
  15.8 0.8 copy-done.4
  16.6 0.7 copy-done.6
  17.3 5.4 %all-to-all-done.slab_ref = bf16[8,64,256]{2,1,0:T(8,128)(2,1)S(1)} async-done(((bf16[8,64,256]{2,1,0:T(8,128)(2,1)}), bf16[8,64,256]{2,1,0:T(8,128)(2,1)S(1)}, u32[]{:S(2)}, u32[]{:S(2)}) %all-to-all-start) | async-done | bytes 262176 | tf_op jit(solution)/shard_map/all_to_all | solution.py:227
  22.6 2.3 %collective-permute-start.1 = (bf16[8,64,256]{2,1,0:T(8,128)(2,1)S(1)}, bf16[8,64,256]{2,1,0:T(8,128)(2,1)S(1)}, u32[]{:S(2)}, u32[]{:S(2)}) collective-permute-start(bf16[8,64,256]{2,1,0:T(8,128)(2,1)S(1)} %all-to-all-done.slab_ref), channel_id=1, source_target_pairs={{0,64},{8,72},{16,80},{24,88},{32,96},{40,104},{48,112},{56,120},{... | collective-permute-start | bytes 786440 | tf_op jit(solution)/shard_map/ppermute | solution.py:208
  24.9 7.9 %collective-permute-start.3 = (bf16[8,64,256]{2,1,0:T(8,128)(2,1)S(1)}, bf16[8,64,256]{2,1,0:T(8,128)(2,1)S(1)}, u32[]{:S(2)}, u32[]{:S(2)}) collective-permute-start(bf16[8,64,256]{2,1,0:T(8,128)(2,1)S(1)} %all-to-all-done.slab_ref), channel_id=1, source_target_pairs={{0,448},{8,456},{16,464},{24,472},{32,480},{40,488},{48,496},{56,5... | collective-permute-start | bytes 786440 | tf_op jit(solution)/shard_map/ppermute | solution.py:208
  32.9 1.0 %copy-done.5 = f32[2,128,512]{2,1,0:T(8,128)S(1)} copy-done((f32[2,128,512]{2,1,0:T(8,128)S(1)}, f32[2,128,512]{2,1,0:T(8,128)}, u32[]{:S(2)}) %copy-start.5) | copy-done | bytes 524312
  33.9 0.9 %copy-done.7 = bf16[2,512,128]{2,1,0:T(8,128)(2,1)S(1)} copy-done((bf16[2,512,128]{2,1,0:T(8,128)(2,1)S(1)}, bf16[2,512,128]{2,1,0:T(8,128)(2,1)}, u32[]{:S(2)}) %copy-start.7) | copy-done | bytes 262168
  34.9 2.0 %shard_map.49 = (bf16[4,512,128]{2,1,0:T(8,128)(2,1)S(1)}, f32[4,1,512]{2,1,0:T(1,128)S(1)}, f32[4,1,512]{2,1,0:T(1,128)S(1)}, f32[4,128,512]{2,1,0:T(8,128)S(1)}) custom-call(s32[3]{0:T(128)S(1)} %pad_add_fusion.place_ref, bf16[1536,256]{1,0:T(8,128)(2,1)S(1)} %collective-permute-done.other_in_ref, bf16[8,64,256]{2,1,0:T(8,128)(2,1)S(1)} %all-to-all-done.slab_ref, ...), custom_call_target="tpu_custom_call" | custom-call | flops 3000000000 | bytes 1048576 | tf_op jit(solution)/shard_map/pallas_call | solution.py:255
  36.9 0.7 collective-permute-start.2
  37.6 5.9 %collective-permute-start.5 = (bf16[8,64,256]{2,1,0:T(8,128)(2,1)S(1)}, bf16[8,64,256]{2,1,0:T(8,128)(2,1)S(1)}, u32[]{:S(2)}, u32[]{:S(2)}) collective-permute-start(bf16[8,64,256]{2,1,0:T(8,128)(2,1)S(1)} %collective-permute-done.3.refs_1_), channel_id=1, source_target_pairs={{0,448},{8,456},{16,464},{24,472},{32,480},{40,488},{48,496},{56,5... | collective-permute-start | bytes 786440 | tf_op jit(solution)/shard_map/ppermute | solution.py:208
  43.5 0.7 shard_map.50
  44.2 2.6 %collective-permute-done.5.refs_1_ = bf16[8,64,256]{2,1,0:T(8,128)(2,1)S(1)} collective-permute-done((bf16[8,64,256]{2,1,0:T(8,128)(2,1)S(1)}, bf16[8,64,256]{2,1,0:T(8,128)(2,1)S(1)}, u32[]{:S(2)}, u32[]{:S(2)}) %collective-permute-start.5) | collective-permute-done | bytes 262176 | tf_op jit(solution)/shard_map/ppermute | solution.py:208
  46.8 0.7 collective-permute-start.4
  47.5 5.6 %collective-permute-start.7 = (bf16[8,64,256]{2,1,0:T(8,128)(2,1)S(1)}, bf16[8,64,256]{2,1,0:T(8,128)(2,1)S(1)}, u32[]{:S(2)}, u32[]{:S(2)}) collective-permute-start(bf16[8,64,256]{2,1,0:T(8,128)(2,1)S(1)} %collective-permute-done.5.refs_1_), channel_id=1, source_target_pairs={{0,448},{8,456},{16,464},{24,472},{32,480},{40,488},{48,496},{56,5... | collective-permute-start | bytes 786440 | tf_op jit(solution)/shard_map/ppermute | solution.py:208
  53.2 0.7 shard_map.51
  53.9 2.6 %collective-permute-done.7.refs_1_ = bf16[8,64,256]{2,1,0:T(8,128)(2,1)S(1)} collective-permute-done((bf16[8,64,256]{2,1,0:T(8,128)(2,1)S(1)}, bf16[8,64,256]{2,1,0:T(8,128)(2,1)S(1)}, u32[]{:S(2)}, u32[]{:S(2)}) %collective-permute-start.7) | collective-permute-done | bytes 262176 | tf_op jit(solution)/shard_map/ppermute | solution.py:208
  56.5 5.0 %collective-permute-start.8 = (bf16[4,64,256]{2,1,0:T(8,128)(2,1)S(1)}, bf16[4,64,256]{2,1,0:T(8,128)(2,1)S(1)}, u32[]{:S(2)}, u32[]{:S(2)}) collective-permute-start(bf16[4,64,256]{2,1,0:T(8,128)(2,1)S(1)} %slice.7), channel_id=1, source_target_pairs={{0,448},{8,456},{16,464},{24,472},{32,480},{40,488},{48,496},{56,5... | collective-permute-start | bytes 393224 | tf_op jit(solution)/shard_map/ppermute | solution.py:208
  61.5 0.7 collective-permute-start.6
  62.2 0.7 shard_map.52
  62.9 0.5 collective-permute-done.8.refs_1_
  63.4 0.7 copy-done.3
  64.1 0.9 %shard_map.53 = (f32[2,128,512]{2,1,0:T(8,128)S(1)}, f32[2,128,512]{2,1,0:T(8,128)S(1)}, f32[2,8,512]{2,1,0:T(8,128)S(1)}) custom-call(s32[3]{0:T(128)S(1)} %pad_add_fusion.place_ref, f32[1,512]{1,0:T(1,128)S(1)} %bitcast.10, bf16[4,512,128]{2,1,0:T(8,128)(2,1)S(1)} %get-tuple-element.69.queries_ref, bf16[4,64,256]{2,1,0:T(8,128)(2,1)S(1)} %collective-permute-done.6.refs_0_, ...), custom_call_target="tpu_custom_call" | custom-call | tf_op jit(solution)/shard_map/pallas_call | solution.py:266
  65.0 7.5 %collective-permute-start.9 = (f32[2,128,512]{2,1,0:T(8,128)S(1)}, f32[2,128,512]{2,1,0:T(8,128)S(1)}, u32[]{:S(2)}, u32[]{:S(2)}) collective-permute-start(f32[2,128,512]{2,1,0:T(8,128)S(1)} %get-tuple-element.109), channel_id=1, source_target_pairs={{0,8},{8,0},{16,24},{24,16},{32,40},{40,32},{48,56},{56,48},{64,72... | collective-permute-start | bytes 1572872 | tf_op jit(solution)/shard_map/ppermute | solution.py:196
  72.6 10.0 %all_to_all.16 = f32[16,1,512]{2,1,0:T(1,128)S(1)} all-to-all(f32[16,1,512]{2,1,0:T(1,128)S(1)} %copy.14), channel_id=1, replica_groups={{0,1,2,3,4,5,6,7,8,9,10,11,12,13,14,15},{16,17,18,19,20,21,22,23,24,25,..., dimensions={0} | all-to-all | bytes 65536 | tf_op jit(solution)/shard_map/all_to_all | solution.py:277
  82.6 1.6 %shard_map.54 = bf16[512,512]{1,0:T(8,128)(2,1)} custom-call(s32[3]{0:T(128)S(1)} %pad_add_fusion.place_ref, f32[2,128,512]{2,1,0:T(8,128)S(1)} %get-tuple-element.108.own_ref, f32[2,128,512]{2,1,0:T(8,128)S(1)} %collective-permute-done.9.other_ref, f32[16,512]{1,0:T(8,128)S(1)} %bitcast.8), custom_call_target="tpu_custom_call" | custom-call | tf_op jit(solution)/shard_map/pallas_call | solution.py:280
  (21 shorter events, 0.1 us)
Async XLA Ops:
  0.0 12.0 %copy-start.1 = (bf16[512,512]{1,0:T(8,128)(2,1)S(1)}, bf16[512,512]{1,0:T(8,128)(2,1)}, u32[]{:S(2)}) copy-start(bf16[512,512]{1,0:T(8,128)(2,1)} %value_ref.1) | copy-start | bytes 1572868
  0.0 12.0 %copy-start.2 = (bf16[512,512]{1,0:T(8,128)(2,1)S(1)}, bf16[512,512]{1,0:T(8,128)(2,1)}, u32[]{:S(2)}) copy-start(bf16[512,512]{1,0:T(8,128)(2,1)} %query_ref.1) | copy-start | bytes 1572868
  1.6 10.4 %copy-start = (bf16[512,512]{1,0:T(8,128)(2,1)S(1)}, bf16[512,512]{1,0:T(8,128)(2,1)}, u32[]{:S(2)}) copy-start(bf16[512,512]{1,0:T(8,128)(2,1)} %key_ref.1) | copy-start | bytes 1572868
  1.6 21.1 %all-to-all-start = ((bf16[8,64,256]{2,1,0:T(8,128)(2,1)}), bf16[8,64,256]{2,1,0:T(8,128)(2,1)S(1)}, u32[]{:S(2)}, u32[]{:S(2)}) async-start(bf16[8,64,256]{2,1,0:T(8,128)(2,1)} %shard_map.46), calls=%async_computation | async-start | bytes 524288 | tf_op jit(solution)/shard_map/all_to_all | solution.py:227
  12.6 20.3 %collective-permute-start = (bf16[1536,256]{1,0:T(8,128)(2,1)S(1)}, bf16[1536,256]{1,0:T(8,128)(2,1)S(1)}, u32[]{:S(2)}, u32[]{:S(2)}) collective-permute-start(bf16[1536,256]{1,0:T(8,128)(2,1)S(1)} %shard_map.47), channel_id=1, source_target_pairs={{0,8},{8,0},{16,24},{24,16},{32,40},{40,32},{48,56},{56,48},{64,72... | collective-permute-start | bytes 2359304 | tf_op jit(solution)/shard_map/ppermute | solution.py:196
  15.8 0.8 copy-start.4
  16.6 0.7 copy-start.6
  22.6 14.3 %collective-permute-start.1 = (bf16[8,64,256]{2,1,0:T(8,128)(2,1)S(1)}, bf16[8,64,256]{2,1,0:T(8,128)(2,1)S(1)}, u32[]{:S(2)}, u32[]{:S(2)}) collective-permute-start(bf16[8,64,256]{2,1,0:T(8,128)(2,1)S(1)} %all-to-all-done.slab_ref), channel_id=1, source_target_pairs={{0,64},{8,72},{16,80},{24,88},{32,96},{40,104},{48,112},{56,120},{... | collective-permute-start | bytes 786440 | tf_op jit(solution)/shard_map/ppermute | solution.py:208
  24.9 12.0 %collective-permute-start.3 = (bf16[8,64,256]{2,1,0:T(8,128)(2,1)S(1)}, bf16[8,64,256]{2,1,0:T(8,128)(2,1)S(1)}, u32[]{:S(2)}, u32[]{:S(2)}) collective-permute-start(bf16[8,64,256]{2,1,0:T(8,128)(2,1)S(1)} %all-to-all-done.slab_ref), channel_id=1, source_target_pairs={{0,448},{8,456},{16,464},{24,472},{32,480},{40,488},{48,496},{56,5... | collective-permute-start | bytes 786440 | tf_op jit(solution)/shard_map/ppermute | solution.py:208
  32.9 1.0 %copy-start.5 = (f32[2,128,512]{2,1,0:T(8,128)S(1)}, f32[2,128,512]{2,1,0:T(8,128)}, u32[]{:S(2)}) copy-start(f32[2,128,512]{2,1,0:T(8,128)} %copy-done.4) | copy-start | bytes 1572868
  33.9 0.9 %copy-start.7 = (bf16[2,512,128]{2,1,0:T(8,128)(2,1)S(1)}, bf16[2,512,128]{2,1,0:T(8,128)(2,1)}, u32[]{:S(2)}) copy-start(bf16[2,512,128]{2,1,0:T(8,128)(2,1)} %copy-done.6) | copy-start | bytes 786436
  36.9 7.3 %collective-permute-start.2 = (bf16[8,64,256]{2,1,0:T(8,128)(2,1)S(1)}, bf16[8,64,256]{2,1,0:T(8,128)(2,1)S(1)}, u32[]{:S(2)}, u32[]{:S(2)}) collective-permute-start(bf16[8,64,256]{2,1,0:T(8,128)(2,1)S(1)} %collective-permute-done.1.refs_0_), channel_id=1, source_target_pairs={{64,128},{72,136},{80,144},{88,152},{96,160},{104,168},{112,176},{... | collective-permute-start | bytes 786440 | tf_op jit(solution)/shard_map/ppermute | solution.py:208
  37.6 9.2 %collective-permute-start.5 = (bf16[8,64,256]{2,1,0:T(8,128)(2,1)S(1)}, bf16[8,64,256]{2,1,0:T(8,128)(2,1)S(1)}, u32[]{:S(2)}, u32[]{:S(2)}) collective-permute-start(bf16[8,64,256]{2,1,0:T(8,128)(2,1)S(1)} %collective-permute-done.3.refs_1_), channel_id=1, source_target_pairs={{0,448},{8,456},{16,464},{24,472},{32,480},{40,488},{48,496},{56,5... | collective-permute-start | bytes 786440 | tf_op jit(solution)/shard_map/ppermute | solution.py:208
  46.8 7.0 %collective-permute-start.4 = (bf16[8,64,256]{2,1,0:T(8,128)(2,1)S(1)}, bf16[8,64,256]{2,1,0:T(8,128)(2,1)S(1)}, u32[]{:S(2)}, u32[]{:S(2)}) collective-permute-start(bf16[8,64,256]{2,1,0:T(8,128)(2,1)S(1)} %collective-permute-done.2.refs_0_), channel_id=1, source_target_pairs={{128,192},{136,200},{144,208},{152,216},{160,224},{168,232},{176,2... | collective-permute-start | bytes 786440 | tf_op jit(solution)/shard_map/ppermute | solution.py:208
  47.5 8.9 %collective-permute-start.7 = (bf16[8,64,256]{2,1,0:T(8,128)(2,1)S(1)}, bf16[8,64,256]{2,1,0:T(8,128)(2,1)S(1)}, u32[]{:S(2)}, u32[]{:S(2)}) collective-permute-start(bf16[8,64,256]{2,1,0:T(8,128)(2,1)S(1)} %collective-permute-done.5.refs_1_), channel_id=1, source_target_pairs={{0,448},{8,456},{16,464},{24,472},{32,480},{40,488},{48,496},{56,5... | collective-permute-start | bytes 786440 | tf_op jit(solution)/shard_map/ppermute | solution.py:208
  56.5 7.0 %collective-permute-start.8 = (bf16[4,64,256]{2,1,0:T(8,128)(2,1)S(1)}, bf16[4,64,256]{2,1,0:T(8,128)(2,1)S(1)}, u32[]{:S(2)}, u32[]{:S(2)}) collective-permute-start(bf16[4,64,256]{2,1,0:T(8,128)(2,1)S(1)} %slice.7), channel_id=1, source_target_pairs={{0,448},{8,456},{16,464},{24,472},{32,480},{40,488},{48,496},{56,5... | collective-permute-start | bytes 393224 | tf_op jit(solution)/shard_map/ppermute | solution.py:208
  61.5 1.9 %collective-permute-start.6 = (bf16[4,64,256]{2,1,0:T(8,128)(2,1)S(1)}, bf16[4,64,256]{2,1,0:T(8,128)(2,1)S(1)}, u32[]{:S(2)}, u32[]{:S(2)}) collective-permute-start(bf16[4,64,256]{2,1,0:T(8,128)(2,1)S(1)} %slice.6), channel_id=1, source_target_pairs={{192,256},{200,264},{208,272},{216,280},{224,288},{232,296},{240,3... | collective-permute-start | bytes 393224 | tf_op jit(solution)/shard_map/ppermute | solution.py:208
  63.4 0.7 copy-start.3
  65.0 17.5 %collective-permute-start.9 = (f32[2,128,512]{2,1,0:T(8,128)S(1)}, f32[2,128,512]{2,1,0:T(8,128)S(1)}, u32[]{:S(2)}, u32[]{:S(2)}) collective-permute-start(f32[2,128,512]{2,1,0:T(8,128)S(1)} %get-tuple-element.109), channel_id=1, source_target_pairs={{0,8},{8,0},{16,24},{24,16},{32,40},{40,32},{48,56},{56,48},{64,72... | collective-permute-start | bytes 1572872 | tf_op jit(solution)/shard_map/ppermute | solution.py:196

commit v4 on v3

--- a/solution.py
+++ b/solution.py
@@ -51,17 +51,18 @@
         out_ref[part * ROWS : (part + 1) * ROWS] = ref[:, pl.ds(other, HALF)]
 
 
-def slab_keys(slab, head):
+def slab_keys(slabs, head):
     columns = slice(head * HEAD_DIM, (head + 1) * HEAD_DIM)
-    sources = slab.shape[0]
-    keys = slab[:, : 2 * SUMMARY, columns].reshape(sources * 2 * SUMMARY, HEAD_DIM)
-    values = slab[:, 2 * SUMMARY :, columns].reshape(sources * 2 * SUMMARY, HEAD_DIM)
-    return keys, values
-
-
-def fold_slab(queries, state, slab, first_blocks):
+
+    def joined(rows):
+        return jnp.concatenate([slab[:, rows, columns].reshape(-1, HEAD_DIM) for slab in slabs])
+
+    return joined(slice(0, 2 * SUMMARY)), joined(slice(2 * SUMMARY, 4 * SUMMARY))
+
+
+def fold_slab(queries, state, slabs, first_blocks):
     max_ref, sum_ref, acc_ref = state
-    parts = [slab_keys(slab, head) for head in range(2)]
+    parts = [slab_keys(slabs, head) for head in range(2)]
     staged = []
     for virtual in range(VIRTUAL):
         scores = rows_dot(parts[virtual % 2][0], queries[virtual]) * SCALE
@@ -98,63 +99,66 @@
         acc_ref[virtual, :, rows] = columns_dot(value, weights.astype(BF16))
 
 
+def gain_columns(place_ref, gain_ref, out_ref):
+    mine = pl.multiple_of(place_ref[2] * HALF, HALF)
+    for head in range(2):
+        gain = gain_ref[:, pl.ds(mine + head * HEAD_DIM, HEAD_DIM)]
+        out_ref[head] = jnp.transpose(jnp.broadcast_to(gain, (8, HEAD_DIM)))
+
+
 def finish(core, gain_ref, state, own_ref, other_ref, square_ref):
     _, sum_ref, acc_ref = state
-    mine = pl.multiple_of(core * HALF, HALF)
     for owner, ref in enumerate((own_ref, other_ref)):
         total = jnp.zeros((1, ROWS), F32)
         for head in range(2):
             virtual = owner * 2 + head
-            gain = jnp.broadcast_to(gain_ref[:, pl.ds(mine + head * HEAD_DIM, HEAD_DIM)], (8, HEAD_DIM))
             attended = acc_ref[virtual] * (1.0 / sum_ref[virtual])
-            ref[head] = attended * jnp.transpose(gain)[:, :1]
+            ref[head] = attended * gain_ref[head, :, :1]
             total += jnp.sum(attended * attended, axis=0, keepdims=True)
         square_ref[core if owner == 0 else 1 - core] = jnp.broadcast_to(total, square_ref.shape[1:])
 
 
-def start_attention(place_ref, query_ref, key_ref, value_ref, queries_ref, *state):
+def start_attention(place_ref, query_ref, key_ref, value_ref, other_in_ref, slab_ref, queries_ref, *state):
     mine = pl.multiple_of(place_ref[2] * HALF, HALF)
 
-    def pieces(head, block):
+    def own_pieces(head, block):
         rows, columns = slice(block * BLOCK, (block + 1) * BLOCK), pl.ds(mine + head * HEAD_DIM, HEAD_DIM)
         return (ref[rows, columns] for ref in (query_ref, key_ref, value_ref))
 
-    band(pieces, 0, state, queries_ref)
-
-
-def own_slab(place_ref, other_in_ref, slab_ref, *refs):
-    inputs, outs = refs[:4], refs[4:]
-    queries_ref, *state = outs
-    for ref_in, ref in zip(inputs, outs):
-        ref[:2] = ref_in[...]
-
-    def pieces(head, block):
+    def other_pieces(head, block):
         columns = slice(head * HEAD_DIM, (head + 1) * HEAD_DIM)
         starts = [part * ROWS + block * BLOCK for part in range(3)]
         return (other_in_ref[start : start + BLOCK, columns] for start in starts)
 
-    band(pieces, 2, state, queries_ref)
+    band(own_pieces, 0, state, queries_ref)
+    band(other_pieces, 2, state, queries_ref)
     chip, core = place_ref[1], place_ref[2]
     first_blocks = [(chip * CORES + core) * 2, (chip * CORES + 1 - core) * 2]
-    fold_slab(queries_ref, state, slab_ref, first_blocks)
-
-
-def go_on(steps, place_ref, queries_ref, *refs):
-    slabs, old_state, state = refs[: 2 * len(steps)], refs[2 * len(steps) : -3], refs[-3:]
+    fold_slab(queries_ref, state, [slab_ref], first_blocks)
+
+
+def go_on(step, place_ref, queries_ref, up_ref, down_ref, *refs):
+    old_state, state = refs[:3], refs[3:]
     here = place_ref[0]
     for old_ref, ref in zip(old_state, state):
         ref[...] = old_ref[...]
-    for turn, step in enumerate(steps):
-        for slab, reached in zip(slabs[2 * turn : 2 * turn + 2], (here >= step, here + step >= CHIPS_Z)):
-
-            @pl.when(reached)
-            def _(slab=slab):
-                fold_slab(queries_ref, state, slab, None)
-
-
-def end_attention(steps, place_ref, gain_ref, queries_ref, *refs):
-    inputs, outs, state = refs[:-6], refs[-6:-3], refs[-3:]
-    go_on(steps, place_ref, queries_ref, *inputs, *state)
+    below, above = here >= step, here + step >= CHIPS_Z
+    if step == 4:
+        cases = ((below, [up_ref, down_ref]),)
+    elif step == 1:
+        cases = ((below & ~above, [up_ref]), (below & above, [up_ref, down_ref]))
+    else:
+        cases = ((below & ~above, [up_ref]), (above & ~below, [down_ref]), (below & above, [up_ref, down_ref]))
+    for reached, slabs in cases:
+
+        @pl.when(reached)
+        def _(slabs=slabs):
+            fold_slab(queries_ref, state, slabs, None)
+
+
+def end_attention(step, place_ref, gain_ref, queries_ref, up_ref, down_ref, *refs):
+    old_state, outs, state = refs[:3], refs[3:6], refs[6:]
+    go_on(step, place_ref, queries_ref, up_ref, down_ref, *old_state, *state)
     finish(place_ref[2], gain_ref, state, *outs)
 
 
@@ -199,8 +203,7 @@
 def pass_on(array, step, way):
     pairs = []
     for index in range(CHIPS_Z * SLAB):
-        here = index // SLAB
-        there = here + way
+        there = index // SLAB + way
         source = (there - way * step) % CHIPS_Z
         needed = there >= step if way == 1 else source < CHIPS_Z // 2
         if needed and there < CHIPS_Z:
@@ -208,7 +211,7 @@
     return lax.ppermute(array, "ctx", pairs)
 
 
-FIRST_COST = pl.CostEstimate(flops=3 * 10**10, bytes_accessed=2**20, transcendentals=2**20)
+LONG = pl.CostEstimate(flops=3 * 10**10, bytes_accessed=2**20, transcendentals=0)
 COST = pl.CostEstimate(flops=3 * 10**9, bytes_accessed=2**20, transcendentals=2**20)
 
 
@@ -230,6 +233,7 @@
         place, query_rows, key_rows, value_rows
     )
     from_other = swap_cores(to_other)
+    gain = call(gain_columns, jax.ShapeDtypeStruct((2, HEAD_DIM, 8), F32), [SMEM, VMEM], cost=LONG)(place, out_gain[None])
 
     def attention(virtuals):
         return (
@@ -239,23 +243,23 @@
             jax.ShapeDtypeStruct((virtuals, HEAD_DIM, ROWS), F32),
         )
 
-    mine = call(start_attention, attention(2), [SMEM] + [VMEM] * 3, cost=FIRST_COST)(place, query_rows, key_rows, value_rows)
     state = attention(VIRTUAL)[1:]
     up, down, arrived = slab, slab, []
     for step in range(1, 5):
         if step == 1:
-            up, down, mine = lax.optimization_barrier((up, down, mine))
+            up, down, gain = lax.optimization_barrier((up, down, gain))
         else:
             up, now = lax.optimization_barrier((up, now))
-            down, now = lax.optimization_barrier((down, now))
         if step == 4:
             up, down = up[: SLAB // 2], down[SLAB // 2 :]
         up, down = pass_on(up, step, 1), pass_on(down, step, -1)
         if step == 1:
-            queries, *now = call(own_slab, attention(VIRTUAL), [SMEM] + [VMEM] * 6, cost=COST)(place, from_other, slab, *mine)
+            queries, *now = call(start_attention, attention(VIRTUAL), [SMEM] + [VMEM] * 5, cost=COST)(
+                place, query_rows, key_rows, value_rows, from_other, slab
+            )
         else:
             now = call(
-                functools.partial(go_on, (step - 1,)),
+                functools.partial(go_on, step - 1),
                 state,
                 [SMEM] + [VMEM] * 6,
                 cost=COST,
@@ -264,11 +268,11 @@
         arrived.append((up, down))
     attended = jax.ShapeDtypeStruct((2, HEAD_DIM, ROWS), F32)
     own, other, squares = call(
-        functools.partial(end_attention, (4,)),
+        functools.partial(end_attention, 4),
         (attended, attended, jax.ShapeDtypeStruct((CORES, head_count, ROWS), F32)),
         [SMEM] + [VMEM] * 7,
         scratch=[pltpu.VMEM(part.shape, F32) for part in state],
-    )(place, out_gain[None], queries, *arrived[3], *now)
+    )(place, gain, queries, *arrived[3], *now)
     back = swap_cores(other)
     chips = [
         [(chip * CORES + core) * head_count + head for core in range(CORES) for head in range(head_count)]

time: 84.7 us -> 79.7 us (0.941)
  local copies, waits for them, and re-layouts: 4.23 us -> 0.08 us
  starting transfers between devices: 48.6 us -> 46.8 us
  waiting for transfers between devices: 11.1 us -> 12.3 us
    unnamed x17 -> x9, local copies, waits for them, and re-layouts: 4.17 us -> 0.02 us
    all_to_all x1, waiting for transfers between devices: 5.37 us -> 7.33 us  [local(): lax.all_to_all(packed, 'ctx', 0, 0, axis_index_groups=groups('yc'), tiled...]
    ppermute x8, starting transfers between devices: 28.8 us -> 27 us  [pass_on(): return lax.ppermute(array, 'ctx', pairs)]
  transfers between devices with their start and end apart: 11 -> 11, of which waited for: 4 -> 4; matrix products, arithmetic and copies ran while one was open for 0% -> 0% of each run, Pallas kernels for 7% -> 8%
where the time goes in v4:
time: 79.7 us; the launch traced here: 79.2 us
  starting transfers between devices  46.8 us (59%)
  waiting for transfers between devices  12.3 us (15%)
  Pallas kernels  9.93 us (12%)
  blocking collectives  9.75 us (12%)
    ppermute x8, starting transfers between devices, pass_on(): return lax.ppermute(array, 'ctx', pairs)  27 us
    all_to_all x1, starting transfers between devices, local(): lax.all_to_all(packed, 'ctx', 0, 0, axis_index_groups=groups('yc'), tiled...  10.3 us
    all_to_all x1, blocking collectives, local(): lax.all_to_all(squares.reshape(CORES * head_count, ROWS), ('ctx', 'head')...  9.75 us
    ppermute x2, starting transfers between devices, swap_cores(): return lax.ppermute(array, 'ctx', pairs)  9.53 us
    all_to_all x1, waiting for transfers between devices, local(): lax.all_to_all(packed, 'ctx', 0, 0, axis_index_groups=groups('yc'), tiled...  7.33 us
    ppermute x8, waiting for transfers between devices, pass_on(): return lax.ppermute(array, 'ctx', pairs)  4.98 us
    pallas_call x1, Pallas kernels, local(): call(start_attention, attention(VIRTUAL), [SMEM] + [VMEM] * 5, cost=COST)  2.48 us
    pallas_call x3, Pallas kernels, local(): call(functools.partial(go_on, step - 1), state, [SMEM] + [VMEM] * 6, cost...  2.26 us
  transfers between devices with their start and end apart: 11, of which 4 were waited for; matrix products, arithmetic and copies ran while one was open for 0% of the time, Pallas kernels for 8%

profile of v4, /device:TPU:1, one launch (start us, length us, event | category | flops | bytes accessed | tf_op | source)
XLA Modules:
  0.0 79.2 jit_solution(16451392783092502576)
XLA Ops:
  0.0 1.6 %shard_map.46 = bf16[8,64,256]{2,1,0:T(8,128)(2,1)} custom-call(bf16[512,512]{1,0:T(8,128)(2,1)} %key_ref.1, bf16[512,512]{1,0:T(8,128)(2,1)} %key_ref.1, bf16[512,512]{1,0:T(8,128)(2,1)} %value_ref.1, bf16[512,512]{1,0:T(8,128)(2,1)} %value_ref.1), custom_call_target="tpu_custom_call" | custom-call | tf_op jit(solution)/shard_map/pallas_call | solution.py:223
  1.6 10.3 %all-to-all-start = ((bf16[8,64,256]{2,1,0:T(8,128)(2,1)}), bf16[8,64,256]{2,1,0:T(8,128)(2,1)S(1)}, u32[]{:S(2)}, u32[]{:S(2)}) async-start(bf16[8,64,256]{2,1,0:T(8,128)(2,1)} %shard_map.46), calls=%async_computation | async-start | bytes 524288 | tf_op jit(solution)/shard_map/all_to_all | solution.py:230
  11.9 0.1 pad_add_fusion.place_ref
  12.0 0.0 copy-start.3
  12.0 0.6 shard_map.48
  12.6 2.0 %collective-permute-start = (bf16[1536,256]{1,0:T(8,128)(2,1)S(1)}, bf16[1536,256]{1,0:T(8,128)(2,1)S(1)}, u32[]{:S(2)}, u32[]{:S(2)}) collective-permute-start(bf16[1536,256]{1,0:T(8,128)(2,1)S(1)} %shard_map.48), channel_id=1, source_target_pairs={{0,8},{8,0},{16,24},{24,16},{32,40},{40,32},{48,56},{56,48},{64,72... | collective-permute-start | bytes 2359304 | tf_op jit(solution)/shard_map/ppermute | solution.py:200
  14.7 0.7 shard_map.47.gain_ref
  15.3 7.3 %all-to-all-done.slab_ref = bf16[8,64,256]{2,1,0:T(8,128)(2,1)S(1)} async-done(((bf16[8,64,256]{2,1,0:T(8,128)(2,1)}), bf16[8,64,256]{2,1,0:T(8,128)(2,1)S(1)}, u32[]{:S(2)}, u32[]{:S(2)}) %all-to-all-start) | async-done | bytes 262176 | tf_op jit(solution)/shard_map/all_to_all | solution.py:230
  22.7 8.9 %collective-permute-start.3 = (bf16[8,64,256]{2,1,0:T(8,128)(2,1)S(1)}, bf16[8,64,256]{2,1,0:T(8,128)(2,1)S(1)}, u32[]{:S(2)}, u32[]{:S(2)}) collective-permute-start(bf16[8,64,256]{2,1,0:T(8,128)(2,1)S(1)} %all-to-all-done.slab_ref), channel_id=1, source_target_pairs={{0,448},{8,456},{16,464},{24,472},{32,480},{40,488},{48,496},{56,5... | collective-permute-start | bytes 786440 | tf_op jit(solution)/shard_map/ppermute | solution.py:211
  31.6 1.3 %collective-permute-start.1 = (bf16[8,64,256]{2,1,0:T(8,128)(2,1)S(1)}, bf16[8,64,256]{2,1,0:T(8,128)(2,1)S(1)}, u32[]{:S(2)}, u32[]{:S(2)}) collective-permute-start(bf16[8,64,256]{2,1,0:T(8,128)(2,1)S(1)} %all-to-all-done.slab_ref), channel_id=1, source_target_pairs={{0,64},{8,72},{16,80},{24,88},{32,96},{40,104},{48,112},{56,120},{... | collective-permute-start | bytes 786440 | tf_op jit(solution)/shard_map/ppermute | solution.py:211
  32.9 2.7 %collective-permute-done.3.down_ref = bf16[8,64,256]{2,1,0:T(8,128)(2,1)S(1)} collective-permute-done((bf16[8,64,256]{2,1,0:T(8,128)(2,1)S(1)}, bf16[8,64,256]{2,1,0:T(8,128)(2,1)S(1)}, u32[]{:S(2)}, u32[]{:S(2)}) %collective-permute-start.3) | collective-permute-done | bytes 262176 | tf_op jit(solution)/shard_map/ppermute | solution.py:211
  35.6 5.3 %collective-permute-start.5 = (bf16[8,64,256]{2,1,0:T(8,128)(2,1)S(1)}, bf16[8,64,256]{2,1,0:T(8,128)(2,1)S(1)}, u32[]{:S(2)}, u32[]{:S(2)}) collective-permute-start(bf16[8,64,256]{2,1,0:T(8,128)(2,1)S(1)} %collective-permute-done.3.down_ref), channel_id=1, source_target_pairs={{0,448},{8,456},{16,464},{24,472},{32,480},{40,488},{48,496},{56,5... | collective-permute-start | bytes 786440 | tf_op jit(solution)/shard_map/ppermute | solution.py:211
  40.9 2.5 %shard_map.49 = (bf16[4,512,128]{2,1,0:T(8,128)(2,1)S(1)}, f32[4,1,512]{2,1,0:T(1,128)S(1)}, f32[4,1,512]{2,1,0:T(1,128)S(1)}, f32[4,128,512]{2,1,0:T(8,128)S(1)}) custom-call(s32[3]{0:T(128)S(1)} %pad_add_fusion.place_ref, bf16[512,512]{1,0:T(8,128)(2,1)S(1)} %copy-done.2, bf16[512,512]{1,0:T(8,128)(2,1)S(1)} %copy-done, bf16[512,512]{1,0:T(8,128)(2,1)S(1)} %copy-done.1, ...), custom_call_target="tpu_custom_call" | custom-call | flops 3000000000 | bytes 1048576 | tf_op jit(solution)/shard_map/pallas_call | solution.py:257
  43.4 0.0 collective-permute-done.1.up_ref
  43.4 0.7 collective-permute-start.2
  44.1 0.7 shard_map.50
  44.8 0.0 collective-permute-done.5.down_ref
  44.8 4.4 %collective-permute-start.7 = (bf16[8,64,256]{2,1,0:T(8,128)(2,1)S(1)}, bf16[8,64,256]{2,1,0:T(8,128)(2,1)S(1)}, u32[]{:S(2)}, u32[]{:S(2)}) collective-permute-start(bf16[8,64,256]{2,1,0:T(8,128)(2,1)S(1)} %collective-permute-done.5.down_ref), channel_id=1, source_target_pairs={{0,448},{8,456},{16,464},{24,472},{32,480},{40,488},{48,496},{56,5... | collective-permute-start | bytes 786440 | tf_op jit(solution)/shard_map/ppermute | solution.py:211
  49.3 0.0 collective-permute-done.2.up_ref
  49.3 0.7 collective-permute-start.4
  49.9 0.7 shard_map.51
  50.6 1.9 %collective-permute-done.7.down_ref = bf16[8,64,256]{2,1,0:T(8,128)(2,1)S(1)} collective-permute-done((bf16[8,64,256]{2,1,0:T(8,128)(2,1)S(1)}, bf16[8,64,256]{2,1,0:T(8,128)(2,1)S(1)}, u32[]{:S(2)}, u32[]{:S(2)}) %collective-permute-start.7) | collective-permute-done | bytes 262176 | tf_op jit(solution)/shard_map/ppermute | solution.py:211
  52.6 5.0 %collective-permute-start.8 = (bf16[4,64,256]{2,1,0:T(8,128)(2,1)S(1)}, bf16[4,64,256]{2,1,0:T(8,128)(2,1)S(1)}, u32[]{:S(2)}, u32[]{:S(2)}) collective-permute-start(bf16[4,64,256]{2,1,0:T(8,128)(2,1)S(1)} %slice.8), channel_id=1, source_target_pairs={{0,448},{8,456},{16,464},{24,472},{32,480},{40,488},{48,496},{56,5... | collective-permute-start | bytes 393224 | tf_op jit(solution)/shard_map/ppermute | solution.py:211
  57.6 0.0 collective-permute-done.4.up_ref
  57.6 0.7 collective-permute-start.6
  58.3 0.9 %shard_map.52 = (f32[4,1,512]{2,1,0:T(1,128)S(1)}, f32[4,1,512]{2,1,0:T(1,128)S(1)}, f32[4,128,512]{2,1,0:T(8,128)S(1)}) custom-call(s32[3]{0:T(128)S(1)} %pad_add_fusion.place_ref, bf16[4,512,128]{2,1,0:T(8,128)(2,1)S(1)} %get-tuple-element.43.queries_ref, ...), custom_call_target="tpu_custom_call", output_to_operand_aliasing={{0}: (4, {}), {1}: (5, {}), {2}: (6, {})} | custom-call | flops 3000000000 | bytes 1048576 | tf_op jit(solution)/shard_map/pallas_call | solution.py:261
  59.2 0.3 collective-permute-done.8.down_ref
  59.5 0.0 collective-permute-done.6.up_ref
  59.5 0.8 %shard_map.53 = (f32[2,128,512]{2,1,0:T(8,128)S(1)}, f32[2,128,512]{2,1,0:T(8,128)S(1)}, f32[2,8,512]{2,1,0:T(8,128)S(1)}) custom-call(s32[3]{0:T(128)S(1)} %pad_add_fusion.place_ref, f32[2,128,8]{2,1,0:T(8,128)S(1)} %shard_map.47.gain_ref, bf16[4,512,128]{2,1,0:T(8,128)(2,1)S(1)} %get-tuple-element.43.queries_ref, ...), custom_call_target="tpu_custom_call" | custom-call | tf_op jit(solution)/shard_map/pallas_call | solution.py:270
  60.3 7.5 %collective-permute-start.9 = (f32[2,128,512]{2,1,0:T(8,128)S(1)}, f32[2,128,512]{2,1,0:T(8,128)S(1)}, u32[]{:S(2)}, u32[]{:S(2)}) collective-permute-start(f32[2,128,512]{2,1,0:T(8,128)S(1)} %get-tuple-element.71), channel_id=1, source_target_pairs={{0,8},{8,0},{16,24},{24,16},{32,40},{40,32},{48,56},{56,48},{64,72... | collective-permute-start | bytes 1572872 | tf_op jit(solution)/shard_map/ppermute | solution.py:200
  67.9 9.7 %all_to_all.16 = f32[16,1,512]{2,1,0:T(1,128)S(1)} all-to-all(f32[16,1,512]{2,1,0:T(1,128)S(1)} %copy.14), channel_id=1, replica_groups={{0,1,2,3,4,5,6,7,8,9,10,11,12,13,14,15},{16,17,18,19,20,21,22,23,24,25,..., dimensions={0} | all-to-all | bytes 65536 | tf_op jit(solution)/shard_map/all_to_all | solution.py:281
  77.6 1.6 %shard_map.54 = bf16[512,512]{1,0:T(8,128)(2,1)} custom-call(s32[3]{0:T(128)S(1)} %pad_add_fusion.place_ref, f32[2,128,512]{2,1,0:T(8,128)S(1)} %get-tuple-element.70.own_ref, f32[2,128,512]{2,1,0:T(8,128)S(1)} %collective-permute-done.9.other_ref, f32[16,512]{1,0:T(8,128)S(1)} %bitcast.8), custom_call_target="tpu_custom_call" | custom-call | tf_op jit(solution)/shard_map/pallas_call | solution.py:284
  (13 shorter events, 0.1 us)
Async XLA Ops:
  0.0 12.0 %copy-start.1 = (bf16[512,512]{1,0:T(8,128)(2,1)S(1)}, bf16[512,512]{1,0:T(8,128)(2,1)}, u32[]{:S(2)}) copy-start(bf16[512,512]{1,0:T(8,128)(2,1)} %value_ref.1) | copy-start | bytes 1572868
  0.0 12.0 %copy-start.2 = (bf16[512,512]{1,0:T(8,128)(2,1)S(1)}, bf16[512,512]{1,0:T(8,128)(2,1)}, u32[]{:S(2)}) copy-start(bf16[512,512]{1,0:T(8,128)(2,1)} %query_ref.1) | copy-start | bytes 1572868
  1.6 10.4 %copy-start = (bf16[512,512]{1,0:T(8,128)(2,1)S(1)}, bf16[512,512]{1,0:T(8,128)(2,1)}, u32[]{:S(2)}) copy-start(bf16[512,512]{1,0:T(8,128)(2,1)} %key_ref.1) | copy-start | bytes 1572868
  1.6 21.1 %all-to-all-start = ((bf16[8,64,256]{2,1,0:T(8,128)(2,1)}), bf16[8,64,256]{2,1,0:T(8,128)(2,1)S(1)}, u32[]{:S(2)}, u32[]{:S(2)}) async-start(bf16[8,64,256]{2,1,0:T(8,128)(2,1)} %shard_map.46), calls=%async_computation | async-start | bytes 524288 | tf_op jit(solution)/shard_map/all_to_all | solution.py:230
  12.0 2.7 %copy-start.3 = (f32[512]{0:T(512)S(1)}, f32[512]{0:T(512)}, u32[]{:S(2)}) copy-start(f32[512]{0:T(512)} %param.7) | copy-start | bytes 6148
  12.6 28.3 %collective-permute-start = (bf16[1536,256]{1,0:T(8,128)(2,1)S(1)}, bf16[1536,256]{1,0:T(8,128)(2,1)S(1)}, u32[]{:S(2)}, u32[]{:S(2)}) collective-permute-start(bf16[1536,256]{1,0:T(8,128)(2,1)S(1)} %shard_map.48), channel_id=1, source_target_pairs={{0,8},{8,0},{16,24},{24,16},{32,40},{40,32},{48,56},{56,48},{64,72... | collective-permute-start | bytes 2359304 | tf_op jit(solution)/shard_map/ppermute | solution.py:200
  22.7 13.0 %collective-permute-start.3 = (bf16[8,64,256]{2,1,0:T(8,128)(2,1)S(1)}, bf16[8,64,256]{2,1,0:T(8,128)(2,1)S(1)}, u32[]{:S(2)}, u32[]{:S(2)}) collective-permute-start(bf16[8,64,256]{2,1,0:T(8,128)(2,1)S(1)} %all-to-all-done.slab_ref), channel_id=1, source_target_pairs={{0,448},{8,456},{16,464},{24,472},{32,480},{40,488},{48,496},{56,5... | collective-permute-start | bytes 786440 | tf_op jit(solution)/shard_map/ppermute | solution.py:211
  31.6 11.9 %collective-permute-start.1 = (bf16[8,64,256]{2,1,0:T(8,128)(2,1)S(1)}, bf16[8,64,256]{2,1,0:T(8,128)(2,1)S(1)}, u32[]{:S(2)}, u32[]{:S(2)}) collective-permute-start(bf16[8,64,256]{2,1,0:T(8,128)(2,1)S(1)} %all-to-all-done.slab_ref), channel_id=1, source_target_pairs={{0,64},{8,72},{16,80},{24,88},{32,96},{40,104},{48,112},{56,120},{... | collective-permute-start | bytes 786440 | tf_op jit(solution)/shard_map/ppermute | solution.py:211
  35.6 9.2 %collective-permute-start.5 = (bf16[8,64,256]{2,1,0:T(8,128)(2,1)S(1)}, bf16[8,64,256]{2,1,0:T(8,128)(2,1)S(1)}, u32[]{:S(2)}, u32[]{:S(2)}) collective-permute-start(bf16[8,64,256]{2,1,0:T(8,128)(2,1)S(1)} %collective-permute-done.3.down_ref), channel_id=1, source_target_pairs={{0,448},{8,456},{16,464},{24,472},{32,480},{40,488},{48,496},{56,5... | collective-permute-start | bytes 786440 | tf_op jit(solution)/shard_map/ppermute | solution.py:211
  43.4 5.8 %collective-permute-start.2 = (bf16[8,64,256]{2,1,0:T(8,128)(2,1)S(1)}, bf16[8,64,256]{2,1,0:T(8,128)(2,1)S(1)}, u32[]{:S(2)}, u32[]{:S(2)}) collective-permute-start(bf16[8,64,256]{2,1,0:T(8,128)(2,1)S(1)} %collective-permute-done.1.up_ref), channel_id=1, source_target_pairs={{64,128},{72,136},{80,144},{88,152},{96,160},{104,168},{112,176},{... | collective-permute-start | bytes 786440 | tf_op jit(solution)/shard_map/ppermute | solution.py:211
  44.8 7.7 %collective-permute-start.7 = (bf16[8,64,256]{2,1,0:T(8,128)(2,1)S(1)}, bf16[8,64,256]{2,1,0:T(8,128)(2,1)S(1)}, u32[]{:S(2)}, u32[]{:S(2)}) collective-permute-start(bf16[8,64,256]{2,1,0:T(8,128)(2,1)S(1)} %collective-permute-done.5.down_ref), channel_id=1, source_target_pairs={{0,448},{8,456},{16,464},{24,472},{32,480},{40,488},{48,496},{56,5... | collective-permute-start | bytes 786440 | tf_op jit(solution)/shard_map/ppermute | solution.py:211
  49.3 8.3 %collective-permute-start.4 = (bf16[8,64,256]{2,1,0:T(8,128)(2,1)S(1)}, bf16[8,64,256]{2,1,0:T(8,128)(2,1)S(1)}, u32[]{:S(2)}, u32[]{:S(2)}) collective-permute-start(bf16[8,64,256]{2,1,0:T(8,128)(2,1)S(1)} %collective-permute-done.2.up_ref), channel_id=1, source_target_pairs={{128,192},{136,200},{144,208},{152,216},{160,224},{168,232},{176,2... | collective-permute-start | bytes 786440 | tf_op jit(solution)/shard_map/ppermute | solution.py:211
  52.6 7.0 %collective-permute-start.8 = (bf16[4,64,256]{2,1,0:T(8,128)(2,1)S(1)}, bf16[4,64,256]{2,1,0:T(8,128)(2,1)S(1)}, u32[]{:S(2)}, u32[]{:S(2)}) collective-permute-start(bf16[4,64,256]{2,1,0:T(8,128)(2,1)S(1)} %slice.8), channel_id=1, source_target_pairs={{0,448},{8,456},{16,464},{24,472},{32,480},{40,488},{48,496},{56,5... | collective-permute-start | bytes 393224 | tf_op jit(solution)/shard_map/ppermute | solution.py:211
  57.6 1.9 %collective-permute-start.6 = (bf16[4,64,256]{2,1,0:T(8,128)(2,1)S(1)}, bf16[4,64,256]{2,1,0:T(8,128)(2,1)S(1)}, u32[]{:S(2)}, u32[]{:S(2)}) collective-permute-start(bf16[4,64,256]{2,1,0:T(8,128)(2,1)S(1)} %slice.6), channel_id=1, source_target_pairs={{192,256},{200,264},{208,272},{216,280},{224,288},{232,296},{240,3... | collective-permute-start | bytes 393224 | tf_op jit(solution)/shard_map/ppermute | solution.py:211
  60.3 17.3 %collective-permute-start.9 = (f32[2,128,512]{2,1,0:T(8,128)S(1)}, f32[2,128,512]{2,1,0:T(8,128)S(1)}, u32[]{:S(2)}, u32[]{:S(2)}) collective-permute-start(f32[2,128,512]{2,1,0:T(8,128)S(1)} %get-tuple-element.71), channel_id=1, source_target_pairs={{0,8},{8,0},{16,24},{24,16},{32,40},{40,32},{48,56},{56,48},{64,72... | collective-permute-start | bytes 1572872 | tf_op jit(solution)/shard_map/ppermute | solution.py:200

commit v5 on v4

--- a/solution.py
+++ b/solution.py
@@ -144,7 +144,7 @@
         ref[...] = old_ref[...]
     below, above = here >= step, here + step >= CHIPS_Z
     if step == 4:
-        cases = ((below, [up_ref, down_ref]),)
+        cases = ((below, [up_ref]),)
     elif step == 1:
         cases = ((below & ~above, [up_ref]), (below & above, [up_ref, down_ref]))
     else:
@@ -205,7 +205,7 @@
     for index in range(CHIPS_Z * SLAB):
         there = index // SLAB + way
         source = (there - way * step) % CHIPS_Z
-        needed = there >= step if way == 1 else source < CHIPS_Z // 2
+        needed = there >= step if way == 1 else source < CHIPS_Z // 2 - 1
         if needed and there < CHIPS_Z:
             pairs.append((index, there % CHIPS_Z * SLAB + index % SLAB))
     return lax.ppermute(array, "ctx", pairs)
@@ -249,10 +249,14 @@
         if step == 1:
             up, down, gain = lax.optimization_barrier((up, down, gain))
         else:
-            up, now = lax.optimization_barrier((up, now))
+            if step < 4:
+                down, now = lax.optimization_barrier((down, now))
+            else:
+                up, now = lax.optimization_barrier((up, now))
         if step == 4:
-            up, down = up[: SLAB // 2], down[SLAB // 2 :]
-        up, down = pass_on(up, step, 1), pass_on(down, step, -1)
+            up = pass_on(up, step, 1)
+        else:
+            up, down = pass_on(up, step, 1), pass_on(down, step, -1)
         if step == 1:
             queries, *now = call(start_attention, attention(VIRTUAL), [SMEM] + [VMEM] * 5, cost=COST)(
                 place, query_rows, key_rows, value_rows, from_other, slab

time: 79.7 us -> 76 us (0.954); the launches traced: 79.2 us -> 74.6 us
  starting transfers between devices: 46.8 us -> 42.6 us
    ppermute x8 -> x7, starting transfers between devices: 27 us -> 23.9 us  [pass_on(): return lax.ppermute(array, 'ctx', pairs)]
    ppermute x2, starting transfers between devices: 9.53 us -> 8.39 us  [swap_cores(): return lax.ppermute(array, 'ctx', pairs)]
    ppermute x8 -> x7, waiting for transfers between devices: 4.98 us -> 4.66 us  [pass_on(): return lax.ppermute(array, 'ctx', pairs)]
  transfers between devices with their start and end apart: 11 -> 10, of which waited for: 4 -> 4; matrix products, arithmetic and copies ran while one was open for 0% -> 0% of each run, Pallas kernels for 8% -> 8%
where the time goes in v5:
time: 76 us; the launch traced here: 74.6 us
  starting transfers between devices  42.6 us (56%)
  waiting for transfers between devices  12 us (16%)
  Pallas kernels  9.93 us (13%)
  blocking collectives  9.74 us (13%)
    ppermute x7, starting transfers between devices, pass_on(): return lax.ppermute(array, 'ctx', pairs)  23.9 us
    all_to_all x1, starting transfers between devices, local(): lax.all_to_all(packed, 'ctx', 0, 0, axis_index_groups=groups('yc'), tiled...  10.3 us
    all_to_all x1, blocking collectives, local(): lax.all_to_all(squares.reshape(CORES * head_count, ROWS), ('ctx', 'head')...  9.74 us
    ppermute x2, starting transfers between devices, swap_cores(): return lax.ppermute(array, 'ctx', pairs)  8.39 us
    all_to_all x1, waiting for transfers between devices, local(): lax.all_to_all(packed, 'ctx', 0, 0, axis_index_groups=groups('yc'), tiled...  7.33 us
    ppermute x7, waiting for transfers between devices, pass_on(): return lax.ppermute(array, 'ctx', pairs)  4.66 us
    pallas_call x1, Pallas kernels, local(): call(start_attention, attention(VIRTUAL), [SMEM] + [VMEM] * 5, cost=COST)  2.48 us
    pallas_call x3, Pallas kernels, local(): call(functools.partial(go_on, step - 1), state, [SMEM] + [VMEM] * 6, cost...  2.25 us
  transfers between devices with their start and end apart: 10, of which 4 were waited for; matrix products, arithmetic and copies ran while one was open for 0% of the time, Pallas kernels for 8%

profile of v5, /device:TPU:1, one launch (start us, length us, event | category | flops | bytes accessed | tf_op | source)
XLA Modules:
  0.0 74.6 jit_solution(13583767458241846366)
XLA Ops:
  0.0 1.6 %shard_map.46 = bf16[8,64,256]{2,1,0:T(8,128)(2,1)} custom-call(bf16[512,512]{1,0:T(8,128)(2,1)} %key_ref.1, bf16[512,512]{1,0:T(8,128)(2,1)} %key_ref.1, bf16[512,512]{1,0:T(8,128)(2,1)} %value_ref.1, bf16[512,512]{1,0:T(8,128)(2,1)} %value_ref.1), custom_call_target="tpu_custom_call" | custom-call | tf_op jit(solution)/shard_map/pallas_call | solution.py:223
  1.6 10.3 %all-to-all-start = ((bf16[8,64,256]{2,1,0:T(8,128)(2,1)}), bf16[8,64,256]{2,1,0:T(8,128)(2,1)S(1)}, u32[]{:S(2)}, u32[]{:S(2)}) async-start(bf16[8,64,256]{2,1,0:T(8,128)(2,1)} %shard_map.46), calls=%async_computation | async-start | bytes 524288 | tf_op jit(solution)/shard_map/all_to_all | solution.py:230
  11.9 0.1 pad_add_fusion.place_ref
  12.0 0.0 copy-start.3
  12.0 0.6 shard_map.48
  12.6 2.0 %collective-permute-start = (bf16[1536,256]{1,0:T(8,128)(2,1)S(1)}, bf16[1536,256]{1,0:T(8,128)(2,1)S(1)}, u32[]{:S(2)}, u32[]{:S(2)}) collective-permute-start(bf16[1536,256]{1,0:T(8,128)(2,1)S(1)} %shard_map.48), channel_id=1, source_target_pairs={{0,8},{8,0},{16,24},{24,16},{32,40},{40,32},{48,56},{56,48},{64,72... | collective-permute-start | bytes 2359304 | tf_op jit(solution)/shard_map/ppermute | solution.py:200
  14.7 0.7 shard_map.47.gain_ref
  15.3 7.3 %all-to-all-done.slab_ref = bf16[8,64,256]{2,1,0:T(8,128)(2,1)S(1)} async-done(((bf16[8,64,256]{2,1,0:T(8,128)(2,1)}), bf16[8,64,256]{2,1,0:T(8,128)(2,1)S(1)}, u32[]{:S(2)}, u32[]{:S(2)}) %all-to-all-start) | async-done | bytes 262176 | tf_op jit(solution)/shard_map/all_to_all | solution.py:230
  22.7 2.3 %collective-permute-start.1 = (bf16[8,64,256]{2,1,0:T(8,128)(2,1)S(1)}, bf16[8,64,256]{2,1,0:T(8,128)(2,1)S(1)}, u32[]{:S(2)}, u32[]{:S(2)}) collective-permute-start(bf16[8,64,256]{2,1,0:T(8,128)(2,1)S(1)} %all-to-all-done.slab_ref), channel_id=1, source_target_pairs={{0,64},{8,72},{16,80},{24,88},{32,96},{40,104},{48,112},{56,120},{... | collective-permute-start | bytes 786440 | tf_op jit(solution)/shard_map/ppermute | solution.py:211
  24.9 7.9 %collective-permute-start.4 = (bf16[8,64,256]{2,1,0:T(8,128)(2,1)S(1)}, bf16[8,64,256]{2,1,0:T(8,128)(2,1)S(1)}, u32[]{:S(2)}, u32[]{:S(2)}) collective-permute-start(bf16[8,64,256]{2,1,0:T(8,128)(2,1)S(1)} %all-to-all-done.slab_ref), channel_id=1, source_target_pairs={{0,448},{8,456},{16,464},{24,472},{32,480},{40,488},{48,496},{56,5... | collective-permute-start | bytes 786440 | tf_op jit(solution)/shard_map/ppermute | solution.py:211
  32.9 0.0 collective-permute-done.1.up_ref
  32.9 0.7 collective-permute-start.2
  33.6 0.0 collective-permute-done.other_in_ref
  33.6 2.5 %shard_map.49 = (bf16[4,512,128]{2,1,0:T(8,128)(2,1)S(1)}, f32[4,1,512]{2,1,0:T(1,128)S(1)}, f32[4,1,512]{2,1,0:T(1,128)S(1)}, f32[4,128,512]{2,1,0:T(8,128)S(1)}) custom-call(s32[3]{0:T(128)S(1)} %pad_add_fusion.place_ref, bf16[512,512]{1,0:T(8,128)(2,1)S(1)} %copy-done.2, bf16[512,512]{1,0:T(8,128)(2,1)S(1)} %copy-done, bf16[512,512]{1,0:T(8,128)(2,1)S(1)} %copy-done.1, ...), custom_call_target="tpu_custom_call" | custom-call | flops 3000000000 | bytes 1048576 | tf_op jit(solution)/shard_map/pallas_call | solution.py:261
  36.1 0.9 %collective-permute-done.4.down_ref = bf16[8,64,256]{2,1,0:T(8,128)(2,1)S(1)} collective-permute-done((bf16[8,64,256]{2,1,0:T(8,128)(2,1)S(1)}, bf16[8,64,256]{2,1,0:T(8,128)(2,1)S(1)}, u32[]{:S(2)}, u32[]{:S(2)}) %collective-permute-start.4) | collective-permute-done | bytes 262176 | tf_op jit(solution)/shard_map/ppermute | solution.py:211
  36.9 6.6 %collective-permute-start.5 = (bf16[8,64,256]{2,1,0:T(8,128)(2,1)S(1)}, bf16[8,64,256]{2,1,0:T(8,128)(2,1)S(1)}, u32[]{:S(2)}, u32[]{:S(2)}) collective-permute-start(bf16[8,64,256]{2,1,0:T(8,128)(2,1)S(1)} %collective-permute-done.4.down_ref), channel_id=1, source_target_pairs={{0,448},{8,456},{16,464},{24,472},{32,480},{40,488},{48,496},{56,5... | collective-permute-start | bytes 786440 | tf_op jit(solution)/shard_map/ppermute | solution.py:211
  43.5 0.7 shard_map.50
  44.2 0.0 collective-permute-done.2.up_ref
  44.2 0.7 collective-permute-start.3
  44.9 1.9 %collective-permute-done.5.down_ref = bf16[8,64,256]{2,1,0:T(8,128)(2,1)S(1)} collective-permute-done((bf16[8,64,256]{2,1,0:T(8,128)(2,1)S(1)}, bf16[8,64,256]{2,1,0:T(8,128)(2,1)S(1)}, u32[]{:S(2)}, u32[]{:S(2)}) %collective-permute-start.5) | collective-permute-done | bytes 262176 | tf_op jit(solution)/shard_map/ppermute | solution.py:211
  46.8 5.0 %collective-permute-start.7 = (bf16[8,64,256]{2,1,0:T(8,128)(2,1)S(1)}, bf16[8,64,256]{2,1,0:T(8,128)(2,1)S(1)}, u32[]{:S(2)}, u32[]{:S(2)}) collective-permute-start(bf16[8,64,256]{2,1,0:T(8,128)(2,1)S(1)} %collective-permute-done.5.down_ref), channel_id=1, source_target_pairs={{0,448},{8,456},{16,464},{24,472},{32,480},{40,488},{48,496},{56,5... | collective-permute-start | bytes 786440 | tf_op jit(solution)/shard_map/ppermute | solution.py:211
  51.9 0.7 shard_map.51
  52.6 0.0 collective-permute-done.3.up_ref
  52.6 0.7 collective-permute-start.6
  53.3 1.9 %collective-permute-done.7.down_ref = bf16[8,64,256]{2,1,0:T(8,128)(2,1)S(1)} collective-permute-done((bf16[8,64,256]{2,1,0:T(8,128)(2,1)S(1)}, bf16[8,64,256]{2,1,0:T(8,128)(2,1)S(1)}, u32[]{:S(2)}, u32[]{:S(2)}) %collective-permute-start.7) | collective-permute-done | bytes 262176 | tf_op jit(solution)/shard_map/ppermute | solution.py:211
  55.1 0.9 %shard_map.52 = (f32[4,1,512]{2,1,0:T(1,128)S(1)}, f32[4,1,512]{2,1,0:T(1,128)S(1)}, f32[4,128,512]{2,1,0:T(8,128)S(1)}) custom-call(s32[3]{0:T(128)S(1)} %pad_add_fusion.place_ref, bf16[4,512,128]{2,1,0:T(8,128)(2,1)S(1)} %get-tuple-element.43.queries_ref, ...), custom_call_target="tpu_custom_call", output_to_operand_aliasing={{0}: (4, {}), {1}: (5, {}), {2}: (6, {})} | custom-call | flops 3000000000 | bytes 1048576 | tf_op jit(solution)/shard_map/pallas_call | solution.py:265
  56.0 0.0 collective-permute-done.6.up_ref
  56.0 0.8 %shard_map.53 = (f32[2,128,512]{2,1,0:T(8,128)S(1)}, f32[2,128,512]{2,1,0:T(8,128)S(1)}, f32[2,8,512]{2,1,0:T(8,128)S(1)}) custom-call(s32[3]{0:T(128)S(1)} %pad_add_fusion.place_ref, f32[2,128,8]{2,1,0:T(8,128)S(1)} %shard_map.47.gain_ref, bf16[4,512,128]{2,1,0:T(8,128)(2,1)S(1)} %get-tuple-element.43.queries_ref, ...), custom_call_target="tpu_custom_call" | custom-call | tf_op jit(solution)/shard_map/pallas_call | solution.py:274
  56.8 6.4 %collective-permute-start.8 = (f32[2,128,512]{2,1,0:T(8,128)S(1)}, f32[2,128,512]{2,1,0:T(8,128)S(1)}, u32[]{:S(2)}, u32[]{:S(2)}) collective-permute-start(f32[2,128,512]{2,1,0:T(8,128)S(1)} %get-tuple-element.71), channel_id=1, source_target_pairs={{0,8},{8,0},{16,24},{24,16},{32,40},{40,32},{48,56},{56,48},{64,72... | collective-permute-start | bytes 1572872 | tf_op jit(solution)/shard_map/ppermute | solution.py:200
  63.3 9.7 %all_to_all.16 = f32[16,1,512]{2,1,0:T(1,128)S(1)} all-to-all(f32[16,1,512]{2,1,0:T(1,128)S(1)} %copy.14), channel_id=1, replica_groups={{0,1,2,3,4,5,6,7,8,9,10,11,12,13,14,15},{16,17,18,19,20,21,22,23,24,25,..., dimensions={0} | all-to-all | bytes 65536 | tf_op jit(solution)/shard_map/all_to_all | solution.py:285
  73.0 0.0 collective-permute-done.8.other_ref
  73.0 1.6 %shard_map.54 = bf16[512,512]{1,0:T(8,128)(2,1)} custom-call(s32[3]{0:T(128)S(1)} %pad_add_fusion.place_ref, f32[2,128,512]{2,1,0:T(8,128)S(1)} %get-tuple-element.70.own_ref, f32[2,128,512]{2,1,0:T(8,128)S(1)} %collective-permute-done.8.other_ref, f32[16,512]{1,0:T(8,128)S(1)} %bitcast.8), custom_call_target="tpu_custom_call" | custom-call | tf_op jit(solution)/shard_map/pallas_call | solution.py:288
  (9 shorter events, 0.1 us)
Async XLA Ops:
  0.0 12.0 %copy-start.1 = (bf16[512,512]{1,0:T(8,128)(2,1)S(1)}, bf16[512,512]{1,0:T(8,128)(2,1)}, u32[]{:S(2)}) copy-start(bf16[512,512]{1,0:T(8,128)(2,1)} %value_ref.1) | copy-start | bytes 1572868
  0.0 12.0 %copy-start.2 = (bf16[512,512]{1,0:T(8,128)(2,1)S(1)}, bf16[512,512]{1,0:T(8,128)(2,1)}, u32[]{:S(2)}) copy-start(bf16[512,512]{1,0:T(8,128)(2,1)} %query_ref.1) | copy-start | bytes 1572868
  1.6 10.4 %copy-start = (bf16[512,512]{1,0:T(8,128)(2,1)S(1)}, bf16[512,512]{1,0:T(8,128)(2,1)}, u32[]{:S(2)}) copy-start(bf16[512,512]{1,0:T(8,128)(2,1)} %key_ref.1) | copy-start | bytes 1572868
  1.6 21.1 %all-to-all-start = ((bf16[8,64,256]{2,1,0:T(8,128)(2,1)}), bf16[8,64,256]{2,1,0:T(8,128)(2,1)S(1)}, u32[]{:S(2)}, u32[]{:S(2)}) async-start(bf16[8,64,256]{2,1,0:T(8,128)(2,1)} %shard_map.46), calls=%async_computation | async-start | bytes 524288 | tf_op jit(solution)/shard_map/all_to_all | solution.py:230
  12.0 2.7 %copy-start.3 = (f32[512]{0:T(512)S(1)}, f32[512]{0:T(512)}, u32[]{:S(2)}) copy-start(f32[512]{0:T(512)} %param.7) | copy-start | bytes 6148
  12.6 21.0 %collective-permute-start = (bf16[1536,256]{1,0:T(8,128)(2,1)S(1)}, bf16[1536,256]{1,0:T(8,128)(2,1)S(1)}, u32[]{:S(2)}, u32[]{:S(2)}) collective-permute-start(bf16[1536,256]{1,0:T(8,128)(2,1)S(1)} %shard_map.48), channel_id=1, source_target_pairs={{0,8},{8,0},{16,24},{24,16},{32,40},{40,32},{48,56},{56,48},{64,72... | collective-permute-start | bytes 2359304 | tf_op jit(solution)/shard_map/ppermute | solution.py:200
  22.7 10.2 %collective-permute-start.1 = (bf16[8,64,256]{2,1,0:T(8,128)(2,1)S(1)}, bf16[8,64,256]{2,1,0:T(8,128)(2,1)S(1)}, u32[]{:S(2)}, u32[]{:S(2)}) collective-permute-start(bf16[8,64,256]{2,1,0:T(8,128)(2,1)S(1)} %all-to-all-done.slab_ref), channel_id=1, source_target_pairs={{0,64},{8,72},{16,80},{24,88},{32,96},{40,104},{48,112},{56,120},{... | collective-permute-start | bytes 786440 | tf_op jit(solution)/shard_map/ppermute | solution.py:211
  24.9 12.0 %collective-permute-start.4 = (bf16[8,64,256]{2,1,0:T(8,128)(2,1)S(1)}, bf16[8,64,256]{2,1,0:T(8,128)(2,1)S(1)}, u32[]{:S(2)}, u32[]{:S(2)}) collective-permute-start(bf16[8,64,256]{2,1,0:T(8,128)(2,1)S(1)} %all-to-all-done.slab_ref), channel_id=1, source_target_pairs={{0,448},{8,456},{16,464},{24,472},{32,480},{40,488},{48,496},{56,5... | collective-permute-start | bytes 786440 | tf_op jit(solution)/shard_map/ppermute | solution.py:211
  32.9 11.4 %collective-permute-start.2 = (bf16[8,64,256]{2,1,0:T(8,128)(2,1)S(1)}, bf16[8,64,256]{2,1,0:T(8,128)(2,1)S(1)}, u32[]{:S(2)}, u32[]{:S(2)}) collective-permute-start(bf16[8,64,256]{2,1,0:T(8,128)(2,1)S(1)} %collective-permute-done.1.up_ref), channel_id=1, source_target_pairs={{64,128},{72,136},{80,144},{88,152},{96,160},{104,168},{112,176},{... | collective-permute-start | bytes 786440 | tf_op jit(solution)/shard_map/ppermute | solution.py:211
  36.9 9.9 %collective-permute-start.5 = (bf16[8,64,256]{2,1,0:T(8,128)(2,1)S(1)}, bf16[8,64,256]{2,1,0:T(8,128)(2,1)S(1)}, u32[]{:S(2)}, u32[]{:S(2)}) collective-permute-start(bf16[8,64,256]{2,1,0:T(8,128)(2,1)S(1)} %collective-permute-done.4.down_ref), channel_id=1, source_target_pairs={{0,448},{8,456},{16,464},{24,472},{32,480},{40,488},{48,496},{56,5... | collective-permute-start | bytes 786440 | tf_op jit(solution)/shard_map/ppermute | solution.py:211
  44.2 8.3 %collective-permute-start.3 = (bf16[8,64,256]{2,1,0:T(8,128)(2,1)S(1)}, bf16[8,64,256]{2,1,0:T(8,128)(2,1)S(1)}, u32[]{:S(2)}, u32[]{:S(2)}) collective-permute-start(bf16[8,64,256]{2,1,0:T(8,128)(2,1)S(1)} %collective-permute-done.2.up_ref), channel_id=1, source_target_pairs={{128,192},{136,200},{144,208},{152,216},{160,224},{168,232},{176,2... | collective-permute-start | bytes 786440 | tf_op jit(solution)/shard_map/ppermute | solution.py:211
  46.8 8.3 %collective-permute-start.7 = (bf16[8,64,256]{2,1,0:T(8,128)(2,1)S(1)}, bf16[8,64,256]{2,1,0:T(8,128)(2,1)S(1)}, u32[]{:S(2)}, u32[]{:S(2)}) collective-permute-start(bf16[8,64,256]{2,1,0:T(8,128)(2,1)S(1)} %collective-permute-done.5.down_ref), channel_id=1, source_target_pairs={{0,448},{8,456},{16,464},{24,472},{32,480},{40,488},{48,496},{56,5... | collective-permute-start | bytes 786440 | tf_op jit(solution)/shard_map/ppermute | solution.py:211
  52.6 3.5 %collective-permute-start.6 = (bf16[8,64,256]{2,1,0:T(8,128)(2,1)S(1)}, bf16[8,64,256]{2,1,0:T(8,128)(2,1)S(1)}, u32[]{:S(2)}, u32[]{:S(2)}) collective-permute-start(bf16[8,64,256]{2,1,0:T(8,128)(2,1)S(1)} %collective-permute-done.3.up_ref), channel_id=1, source_target_pairs={{192,256},{200,264},{208,272},{216,280},{224,288},{232,296},{240,3... | collective-permute-start | bytes 786440 | tf_op jit(solution)/shard_map/ppermute | solution.py:211
  56.8 16.2 %collective-permute-start.8 = (f32[2,128,512]{2,1,0:T(8,128)S(1)}, f32[2,128,512]{2,1,0:T(8,128)S(1)}, u32[]{:S(2)}, u32[]{:S(2)}) collective-permute-start(f32[2,128,512]{2,1,0:T(8,128)S(1)} %get-tuple-element.71), channel_id=1, source_target_pairs={{0,8},{8,0},{16,24},{24,16},{32,40},{40,32},{48,56},{56,48},{64,72... | collective-permute-start | bytes 1572872 | tf_op jit(solution)/shard_map/ppermute | solution.py:200

commit v6 on v5

--- a/solution.py
+++ b/solution.py
@@ -137,28 +137,30 @@
     fold_slab(queries_ref, state, [slab_ref], first_blocks)
 
 
-def go_on(step, place_ref, queries_ref, up_ref, down_ref, *refs):
-    old_state, state = refs[:3], refs[3:]
+def go_on(steps, place_ref, queries_ref, *refs):
+    slabs, old_state, state = refs[: 2 * len(steps)], refs[2 * len(steps) : -3], refs[-3:]
     here = place_ref[0]
     for old_ref, ref in zip(old_state, state):
         ref[...] = old_ref[...]
-    below, above = here >= step, here + step >= CHIPS_Z
-    if step == 4:
-        cases = ((below, [up_ref]),)
-    elif step == 1:
-        cases = ((below & ~above, [up_ref]), (below & above, [up_ref, down_ref]))
-    else:
-        cases = ((below & ~above, [up_ref]), (above & ~below, [down_ref]), (below & above, [up_ref, down_ref]))
-    for reached, slabs in cases:
-
-        @pl.when(reached)
-        def _(slabs=slabs):
-            fold_slab(queries_ref, state, slabs, None)
+    for turn, step in enumerate(steps):
+        up_ref, down_ref = slabs[2 * turn : 2 * turn + 2]
+        below, above = here >= step, here + step >= CHIPS_Z
+        if step == 4:
+            cases = ((below, [up_ref]),)
+        elif step == 1:
+            cases = ((below & ~above, [up_ref]), (below & above, [up_ref, down_ref]))
+        else:
+            cases = ((below & ~above, [up_ref]), (above & ~below, [down_ref]), (below & above, [up_ref, down_ref]))
+        for reached, taken in cases:
+
+            @pl.when(reached)
+            def _(taken=taken):
+                fold_slab(queries_ref, state, taken, None)
 
 
 def end_attention(step, place_ref, gain_ref, queries_ref, up_ref, down_ref, *refs):
     old_state, outs, state = refs[:3], refs[3:6], refs[6:]
-    go_on(step, place_ref, queries_ref, up_ref, down_ref, *old_state, *state)
+    go_on((step,), place_ref, queries_ref, up_ref, down_ref, *old_state, *state)
     finish(place_ref[2], gain_ref, state, *outs)
 
 
@@ -249,7 +251,7 @@
         if step == 1:
             up, down, gain = lax.optimization_barrier((up, down, gain))
         else:
-            if step < 4:
+            if step == 2:
                 down, now = lax.optimization_barrier((down, now))
             else:
                 up, now = lax.optimization_barrier((up, now))
@@ -261,14 +263,16 @@
             queries, *now = call(start_attention, attention(VIRTUAL), [SMEM] + [VMEM] * 5, cost=COST)(
                 place, query_rows, key_rows, value_rows, from_other, slab
             )
-        else:
+        elif step > 2:
+            steps = (1,) if step == 3 else (2, 3)
+            slabs = [part for past in steps for part in arrived[past - 1]]
             now = call(
-                functools.partial(go_on, step - 1),
+                functools.partial(go_on, steps),
                 state,
-                [SMEM] + [VMEM] * 6,
+                [SMEM] + [VMEM] * (4 + len(slabs)),
                 cost=COST,
-                input_output_aliases={4 + i: i for i in range(3)},
-            )(place, queries, *arrived[-1], *now)
+                input_output_aliases={2 + len(slabs) + i: i for i in range(3)},
+            )(place, queries, *slabs, *now)
         arrived.append((up, down))
     attended = jax.ShapeDtypeStruct((2, HEAD_DIM, ROWS), F32)
     own, other, squares = call(

time: 76 us -> 76 us (level)
    pallas_call x3 -> x2, Pallas kernels: 2.25 us -> 1.57 us  [local(): call(functools.partial(go_on, steps), state, [SMEM] + [VMEM] * (4 + len(s...]
  transfers between devices with their start and end apart: 10 -> 10, of which waited for: 4 -> 4; matrix products, arithmetic and copies ran while one was open for 0% -> 0% of each run, Pallas kernels for 8% -> 7%
where the time goes in v6:
time: 76 us; the launch traced here: 74.6 us
  starting transfers between devices  42.6 us (56%)
  waiting for transfers between devices  12.7 us (17%)
  blocking collectives  9.75 us (13%)
  Pallas kernels  9.27 us (12%)
    ppermute x7, starting transfers between devices, pass_on(): return lax.ppermute(array, 'ctx', pairs)  23.9 us
    all_to_all x1, starting transfers between devices, local(): lax.all_to_all(packed, 'ctx', 0, 0, axis_index_groups=groups('yc'), tiled...  10.3 us
    all_to_all x1, blocking collectives, local(): lax.all_to_all(squares.reshape(CORES * head_count, ROWS), ('ctx', 'head')...  9.75 us
    ppermute x2, starting transfers between devices, swap_cores(): return lax.ppermute(array, 'ctx', pairs)  8.38 us
    all_to_all x1, waiting for transfers between devices, local(): lax.all_to_all(packed, 'ctx', 0, 0, axis_index_groups=groups('yc'), tiled...  7.33 us
    ppermute x7, waiting for transfers between devices, pass_on(): return lax.ppermute(array, 'ctx', pairs)  5.34 us
    pallas_call x1, Pallas kernels, local(): call(start_attention, attention(VIRTUAL), [SMEM] + [VMEM] * 5, cost=COST)  2.49 us
    pallas_call x2, Pallas kernels, local(): call(functools.partial(go_on, steps), state, [SMEM] + [VMEM] * (4 + len(s...  1.57 us
  transfers between devices with their start and end apart: 10, of which 4 were waited for; matrix products, arithmetic and copies ran while one was open for 0% of the time, Pallas kernels for 7%

profile of v6, /device:TPU:1, one launch (start us, length us, event | category | flops | bytes accessed | tf_op | source)
XLA Modules:
  0.0 74.6 jit_solution(2809249937526964162)
XLA Ops:
  0.0 1.6 %shard_map.46 = bf16[8,64,256]{2,1,0:T(8,128)(2,1)} custom-call(bf16[512,512]{1,0:T(8,128)(2,1)} %key_ref.1, bf16[512,512]{1,0:T(8,128)(2,1)} %key_ref.1, bf16[512,512]{1,0:T(8,128)(2,1)} %value_ref.1, bf16[512,512]{1,0:T(8,128)(2,1)} %value_ref.1), custom_call_target="tpu_custom_call" | custom-call | tf_op jit(solution)/shard_map/pallas_call | solution.py:225
  1.6 10.3 %all-to-all-start = ((bf16[8,64,256]{2,1,0:T(8,128)(2,1)}), bf16[8,64,256]{2,1,0:T(8,128)(2,1)S(1)}, u32[]{:S(2)}, u32[]{:S(2)}) async-start(bf16[8,64,256]{2,1,0:T(8,128)(2,1)} %shard_map.46), calls=%async_computation | async-start | bytes 524288 | tf_op jit(solution)/shard_map/all_to_all | solution.py:232
  11.9 0.1 pad_add_fusion.place_ref
  12.0 0.0 copy-done.1
  12.0 0.0 copy-start.3
  12.0 0.6 shard_map.48
  12.6 2.0 %collective-permute-start = (bf16[1536,256]{1,0:T(8,128)(2,1)S(1)}, bf16[1536,256]{1,0:T(8,128)(2,1)S(1)}, u32[]{:S(2)}, u32[]{:S(2)}) collective-permute-start(bf16[1536,256]{1,0:T(8,128)(2,1)S(1)} %shard_map.48), channel_id=1, source_target_pairs={{0,8},{8,0},{16,24},{24,16},{32,40},{40,32},{48,56},{56,48},{64,72... | collective-permute-start | bytes 2359304 | tf_op jit(solution)/shard_map/ppermute | solution.py:202
  14.7 0.7 shard_map.47.gain_ref
  15.3 7.3 %all-to-all-done.slab_ref = bf16[8,64,256]{2,1,0:T(8,128)(2,1)S(1)} async-done(((bf16[8,64,256]{2,1,0:T(8,128)(2,1)}), bf16[8,64,256]{2,1,0:T(8,128)(2,1)S(1)}, u32[]{:S(2)}, u32[]{:S(2)}) %all-to-all-start) | async-done | bytes 262176 | tf_op jit(solution)/shard_map/all_to_all | solution.py:232
  22.7 2.3 %collective-permute-start.1 = (bf16[8,64,256]{2,1,0:T(8,128)(2,1)S(1)}, bf16[8,64,256]{2,1,0:T(8,128)(2,1)S(1)}, u32[]{:S(2)}, u32[]{:S(2)}) collective-permute-start(bf16[8,64,256]{2,1,0:T(8,128)(2,1)S(1)} %all-to-all-done.slab_ref), channel_id=1, source_target_pairs={{0,64},{8,72},{16,80},{24,88},{32,96},{40,104},{48,112},{56,120},{... | collective-permute-start | bytes 786440 | tf_op jit(solution)/shard_map/ppermute | solution.py:213
  24.9 7.9 %collective-permute-start.3 = (bf16[8,64,256]{2,1,0:T(8,128)(2,1)S(1)}, bf16[8,64,256]{2,1,0:T(8,128)(2,1)S(1)}, u32[]{:S(2)}, u32[]{:S(2)}) collective-permute-start(bf16[8,64,256]{2,1,0:T(8,128)(2,1)S(1)} %all-to-all-done.slab_ref), channel_id=1, source_target_pairs={{0,448},{8,456},{16,464},{24,472},{32,480},{40,488},{48,496},{56,5... | collective-permute-start | bytes 786440 | tf_op jit(solution)/shard_map/ppermute | solution.py:213
  32.9 0.0 collective-permute-done.1.refs_0_
  32.9 0.7 collective-permute-start.2
  33.6 0.0 collective-permute-done.other_in_ref
  33.6 2.5 %shard_map.49 = (bf16[4,512,128]{2,1,0:T(8,128)(2,1)S(1)}, f32[4,1,512]{2,1,0:T(1,128)S(1)}, f32[4,1,512]{2,1,0:T(1,128)S(1)}, f32[4,128,512]{2,1,0:T(8,128)S(1)}) custom-call(s32[3]{0:T(128)S(1)} %pad_add_fusion.place_ref, bf16[512,512]{1,0:T(8,128)(2,1)S(1)} %copy-done.2, bf16[512,512]{1,0:T(8,128)(2,1)S(1)} %copy-done, bf16[512,512]{1,0:T(8,128)(2,1)S(1)} %copy-done.1, ...), custom_call_target="tpu_custom_call" | custom-call | flops 3000000000 | bytes 1048576 | tf_op jit(solution)/shard_map/pallas_call | solution.py:263
  36.1 0.8 %collective-permute-done.3.refs_1_ = bf16[8,64,256]{2,1,0:T(8,128)(2,1)S(1)} collective-permute-done((bf16[8,64,256]{2,1,0:T(8,128)(2,1)S(1)}, bf16[8,64,256]{2,1,0:T(8,128)(2,1)S(1)}, u32[]{:S(2)}, u32[]{:S(2)}) %collective-permute-start.3) | collective-permute-done | bytes 262176 | tf_op jit(solution)/shard_map/ppermute | solution.py:213
  36.9 6.6 %collective-permute-start.6 = (bf16[8,64,256]{2,1,0:T(8,128)(2,1)S(1)}, bf16[8,64,256]{2,1,0:T(8,128)(2,1)S(1)}, u32[]{:S(2)}, u32[]{:S(2)}) collective-permute-start(bf16[8,64,256]{2,1,0:T(8,128)(2,1)S(1)} %collective-permute-done.3.refs_1_), channel_id=1, source_target_pairs={{0,448},{8,456},{16,464},{24,472},{32,480},{40,488},{48,496},{56,5... | collective-permute-start | bytes 786440 | tf_op jit(solution)/shard_map/ppermute | solution.py:213
  43.6 0.0 collective-permute-done.2.refs_0_
  43.6 0.7 collective-permute-start.4
  44.2 2.6 %collective-permute-done.6.refs_1_ = bf16[8,64,256]{2,1,0:T(8,128)(2,1)S(1)} collective-permute-done((bf16[8,64,256]{2,1,0:T(8,128)(2,1)S(1)}, bf16[8,64,256]{2,1,0:T(8,128)(2,1)S(1)}, u32[]{:S(2)}, u32[]{:S(2)}) %collective-permute-start.6) | collective-permute-done | bytes 262176 | tf_op jit(solution)/shard_map/ppermute | solution.py:213
  46.8 5.0 %collective-permute-start.7 = (bf16[8,64,256]{2,1,0:T(8,128)(2,1)S(1)}, bf16[8,64,256]{2,1,0:T(8,128)(2,1)S(1)}, u32[]{:S(2)}, u32[]{:S(2)}) collective-permute-start(bf16[8,64,256]{2,1,0:T(8,128)(2,1)S(1)} %collective-permute-done.6.refs_1_), channel_id=1, source_target_pairs={{0,448},{8,456},{16,464},{24,472},{32,480},{40,488},{48,496},{56,5... | collective-permute-start | bytes 786440 | tf_op jit(solution)/shard_map/ppermute | solution.py:213
  51.9 0.7 shard_map.50
  52.6 0.0 collective-permute-done.4.refs_2_
  52.6 0.7 collective-permute-start.5
  53.3 1.9 %collective-permute-done.7.refs_3_.down_ref = bf16[8,64,256]{2,1,0:T(8,128)(2,1)S(1)} collective-permute-done((bf16[8,64,256]{2,1,0:T(8,128)(2,1)S(1)}, bf16[8,64,256]{2,1,0:T(8,128)(2,1)S(1)}, u32[]{:S(2)}, u32[]{:S(2)}) %collective-permute-start.7) | collective-permute-done | bytes 262176 | tf_op jit(solution)/shard_map/ppermute | solution.py:213
  55.2 0.9 %shard_map.51 = (f32[4,1,512]{2,1,0:T(1,128)S(1)}, f32[4,1,512]{2,1,0:T(1,128)S(1)}, f32[4,128,512]{2,1,0:T(8,128)S(1)}) custom-call(s32[3]{0:T(128)S(1)} %pad_add_fusion.place_ref, bf16[4,512,128]{2,1,0:T(8,128)(2,1)S(1)} %get-tuple-element.40.queries_ref, ...), custom_call_target="tpu_custom_call", output_to_operand_aliasing={{0}: (6, {}), {1}: (7, {}), {2}: (8, {})} | custom-call | flops 3000000000 | bytes 1048576 | tf_op jit(solution)/shard_map/pallas_call | solution.py:269
  56.1 0.0 collective-permute-done.5.up_ref
  56.1 0.8 %shard_map.52 = (f32[2,128,512]{2,1,0:T(8,128)S(1)}, f32[2,128,512]{2,1,0:T(8,128)S(1)}, f32[2,8,512]{2,1,0:T(8,128)S(1)}) custom-call(s32[3]{0:T(128)S(1)} %pad_add_fusion.place_ref, f32[2,128,8]{2,1,0:T(8,128)S(1)} %shard_map.47.gain_ref, bf16[4,512,128]{2,1,0:T(8,128)(2,1)S(1)} %get-tuple-element.40.queries_ref, ...), custom_call_target="tpu_custom_call" | custom-call | tf_op jit(solution)/shard_map/pallas_call | solution.py:278
  56.9 6.4 %collective-permute-start.8 = (f32[2,128,512]{2,1,0:T(8,128)S(1)}, f32[2,128,512]{2,1,0:T(8,128)S(1)}, u32[]{:S(2)}, u32[]{:S(2)}) collective-permute-start(f32[2,128,512]{2,1,0:T(8,128)S(1)} %get-tuple-element.65), channel_id=1, source_target_pairs={{0,8},{8,0},{16,24},{24,16},{32,40},{40,32},{48,56},{56,48},{64,72... | collective-permute-start | bytes 1572872 | tf_op jit(solution)/shard_map/ppermute | solution.py:202
  63.3 9.8 %all_to_all.16 = f32[16,1,512]{2,1,0:T(1,128)S(1)} all-to-all(f32[16,1,512]{2,1,0:T(1,128)S(1)} %copy.11), channel_id=1, replica_groups={{0,1,2,3,4,5,6,7,8,9,10,11,12,13,14,15},{16,17,18,19,20,21,22,23,24,25,..., dimensions={0} | all-to-all | bytes 65536 | tf_op jit(solution)/shard_map/all_to_all | solution.py:289
  73.0 0.0 collective-permute-done.8.other_ref
  73.0 1.6 %shard_map.53 = bf16[512,512]{1,0:T(8,128)(2,1)} custom-call(s32[3]{0:T(128)S(1)} %pad_add_fusion.place_ref, f32[2,128,512]{2,1,0:T(8,128)S(1)} %get-tuple-element.64.own_ref, f32[2,128,512]{2,1,0:T(8,128)S(1)} %collective-permute-done.8.other_ref, f32[16,512]{1,0:T(8,128)S(1)} %bitcast.8), custom_call_target="tpu_custom_call" | custom-call | tf_op jit(solution)/shard_map/pallas_call | solution.py:292
  (8 shorter events, 0.0 us)
Async XLA Ops:
  0.0 12.0 %copy-start.1 = (bf16[512,512]{1,0:T(8,128)(2,1)S(1)}, bf16[512,512]{1,0:T(8,128)(2,1)}, u32[]{:S(2)}) copy-start(bf16[512,512]{1,0:T(8,128)(2,1)} %value_ref.1) | copy-start | bytes 1572868
  0.0 12.0 %copy-start.2 = (bf16[512,512]{1,0:T(8,128)(2,1)S(1)}, bf16[512,512]{1,0:T(8,128)(2,1)}, u32[]{:S(2)}) copy-start(bf16[512,512]{1,0:T(8,128)(2,1)} %query_ref.1) | copy-start | bytes 1572868
  1.6 10.4 %copy-start = (bf16[512,512]{1,0:T(8,128)(2,1)S(1)}, bf16[512,512]{1,0:T(8,128)(2,1)}, u32[]{:S(2)}) copy-start(bf16[512,512]{1,0:T(8,128)(2,1)} %key_ref.1) | copy-start | bytes 1572868
  1.6 21.1 %all-to-all-start = ((bf16[8,64,256]{2,1,0:T(8,128)(2,1)}), bf16[8,64,256]{2,1,0:T(8,128)(2,1)S(1)}, u32[]{:S(2)}, u32[]{:S(2)}) async-start(bf16[8,64,256]{2,1,0:T(8,128)(2,1)} %shard_map.46), calls=%async_computation | async-start | bytes 524288 | tf_op jit(solution)/shard_map/all_to_all | solution.py:232
  12.0 2.7 %copy-start.3 = (f32[512]{0:T(512)S(1)}, f32[512]{0:T(512)}, u32[]{:S(2)}) copy-start(f32[512]{0:T(512)} %param.7) | copy-start | bytes 6148
  12.6 21.0 %collective-permute-start = (bf16[1536,256]{1,0:T(8,128)(2,1)S(1)}, bf16[1536,256]{1,0:T(8,128)(2,1)S(1)}, u32[]{:S(2)}, u32[]{:S(2)}) collective-permute-start(bf16[1536,256]{1,0:T(8,128)(2,1)S(1)} %shard_map.48), channel_id=1, source_target_pairs={{0,8},{8,0},{16,24},{24,16},{32,40},{40,32},{48,56},{56,48},{64,72... | collective-permute-start | bytes 2359304 | tf_op jit(solution)/shard_map/ppermute | solution.py:202
  22.7 10.2 %collective-permute-start.1 = (bf16[8,64,256]{2,1,0:T(8,128)(2,1)S(1)}, bf16[8,64,256]{2,1,0:T(8,128)(2,1)S(1)}, u32[]{:S(2)}, u32[]{:S(2)}) collective-permute-start(bf16[8,64,256]{2,1,0:T(8,128)(2,1)S(1)} %all-to-all-done.slab_ref), channel_id=1, source_target_pairs={{0,64},{8,72},{16,80},{24,88},{32,96},{40,104},{48,112},{56,120},{... | collective-permute-start | bytes 786440 | tf_op jit(solution)/shard_map/ppermute | solution.py:213
  24.9 12.0 %collective-permute-start.3 = (bf16[8,64,256]{2,1,0:T(8,128)(2,1)S(1)}, bf16[8,64,256]{2,1,0:T(8,128)(2,1)S(1)}, u32[]{:S(2)}, u32[]{:S(2)}) collective-permute-start(bf16[8,64,256]{2,1,0:T(8,128)(2,1)S(1)} %all-to-all-done.slab_ref), channel_id=1, source_target_pairs={{0,448},{8,456},{16,464},{24,472},{32,480},{40,488},{48,496},{56,5... | collective-permute-start | bytes 786440 | tf_op jit(solution)/shard_map/ppermute | solution.py:213
  32.9 10.7 %collective-permute-start.2 = (bf16[8,64,256]{2,1,0:T(8,128)(2,1)S(1)}, bf16[8,64,256]{2,1,0:T(8,128)(2,1)S(1)}, u32[]{:S(2)}, u32[]{:S(2)}) collective-permute-start(bf16[8,64,256]{2,1,0:T(8,128)(2,1)S(1)} %collective-permute-done.1.refs_0_), channel_id=1, source_target_pairs={{64,128},{72,136},{80,144},{88,152},{96,160},{104,168},{112,176},{... | collective-permute-start | bytes 786440 | tf_op jit(solution)/shard_map/ppermute | solution.py:213
  36.9 9.9 %collective-permute-start.6 = (bf16[8,64,256]{2,1,0:T(8,128)(2,1)S(1)}, bf16[8,64,256]{2,1,0:T(8,128)(2,1)S(1)}, u32[]{:S(2)}, u32[]{:S(2)}) collective-permute-start(bf16[8,64,256]{2,1,0:T(8,128)(2,1)S(1)} %collective-permute-done.3.refs_1_), channel_id=1, source_target_pairs={{0,448},{8,456},{16,464},{24,472},{32,480},{40,488},{48,496},{56,5... | collective-permute-start | bytes 786440 | tf_op jit(solution)/shard_map/ppermute | solution.py:213
  43.6 9.0 %collective-permute-start.4 = (bf16[8,64,256]{2,1,0:T(8,128)(2,1)S(1)}, bf16[8,64,256]{2,1,0:T(8,128)(2,1)S(1)}, u32[]{:S(2)}, u32[]{:S(2)}) collective-permute-start(bf16[8,64,256]{2,1,0:T(8,128)(2,1)S(1)} %collective-permute-done.2.refs_0_), channel_id=1, source_target_pairs={{128,192},{136,200},{144,208},{152,216},{160,224},{168,232},{176,2... | collective-permute-start | bytes 786440 | tf_op jit(solution)/shard_map/ppermute | solution.py:213
  46.8 8.3 %collective-permute-start.7 = (bf16[8,64,256]{2,1,0:T(8,128)(2,1)S(1)}, bf16[8,64,256]{2,1,0:T(8,128)(2,1)S(1)}, u32[]{:S(2)}, u32[]{:S(2)}) collective-permute-start(bf16[8,64,256]{2,1,0:T(8,128)(2,1)S(1)} %collective-permute-done.6.refs_1_), channel_id=1, source_target_pairs={{0,448},{8,456},{16,464},{24,472},{32,480},{40,488},{48,496},{56,5... | collective-permute-start | bytes 786440 | tf_op jit(solution)/shard_map/ppermute | solution.py:213
  52.6 3.5 %collective-permute-start.5 = (bf16[8,64,256]{2,1,0:T(8,128)(2,1)S(1)}, bf16[8,64,256]{2,1,0:T(8,128)(2,1)S(1)}, u32[]{:S(2)}, u32[]{:S(2)}) collective-permute-start(bf16[8,64,256]{2,1,0:T(8,128)(2,1)S(1)} %collective-permute-done.4.refs_2_), channel_id=1, source_target_pairs={{192,256},{200,264},{208,272},{216,280},{224,288},{232,296},{240,3... | collective-permute-start | bytes 786440 | tf_op jit(solution)/shard_map/ppermute | solution.py:213
  56.9 16.2 %collective-permute-start.8 = (f32[2,128,512]{2,1,0:T(8,128)S(1)}, f32[2,128,512]{2,1,0:T(8,128)S(1)}, u32[]{:S(2)}, u32[]{:S(2)}) collective-permute-start(f32[2,128,512]{2,1,0:T(8,128)S(1)} %get-tuple-element.65), channel_id=1, source_target_pairs={{0,8},{8,0},{16,24},{24,16},{32,40},{40,32},{48,56},{56,48},{64,72... | collective-permute-start | bytes 1572872 | tf_op jit(solution)/shard_map/ppermute | solution.py:202

commit v7 on v6

--- a/solution.py
+++ b/solution.py
@@ -115,7 +115,9 @@
             attended = acc_ref[virtual] * (1.0 / sum_ref[virtual])
             ref[head] = attended * gain_ref[head, :, :1]
             total += jnp.sum(attended * attended, axis=0, keepdims=True)
-        square_ref[core if owner == 0 else 1 - core] = jnp.broadcast_to(total, square_ref.shape[1:])
+        heads = square_ref.shape[0] // CORES
+        first = (core if owner == 0 else 1 - core) * heads
+        square_ref[pl.ds(first, heads)] = jnp.broadcast_to(total[None], (heads, 1, ROWS))
 
 
 def start_attention(place_ref, query_ref, key_ref, value_ref, other_in_ref, slab_ref, queries_ref, *state):
@@ -166,7 +168,7 @@
 
 def scale_rows(place_ref, own_ref, other_ref, square_ref, out_ref):
     core = place_ref[2]
-    total = jnp.sum(square_ref[...], axis=0, keepdims=True)
+    total = jnp.sum(square_ref[...], axis=0)
     scale = lax.rsqrt(total * (1.0 / FEATURES) + 1e-06)
     for owner, ref in enumerate((own_ref, other_ref)):
         first = pl.multiple_of((core if owner == 0 else 1 - core) * HALF, HALF)
@@ -277,7 +279,7 @@
     attended = jax.ShapeDtypeStruct((2, HEAD_DIM, ROWS), F32)
     own, other, squares = call(
         functools.partial(end_attention, 4),
-        (attended, attended, jax.ShapeDtypeStruct((CORES, head_count, ROWS), F32)),
+        (attended, attended, jax.ShapeDtypeStruct((CORES * head_count, 1, ROWS), F32)),
         [SMEM] + [VMEM] * 7,
         scratch=[pltpu.VMEM(part.shape, F32) for part in state],
     )(place, gain, queries, *arrived[3], *now)
@@ -287,7 +289,7 @@
         for chip in range(CHIPS_Z * CHIPS_Y)
     ]
     totals = lax.all_to_all(
-        squares.reshape(CORES * head_count, ROWS), ("ctx", "head"), 0, 0, axis_index_groups=chips, tiled=True
+        squares, ("ctx", "head"), 0, 0, axis_index_groups=chips, tiled=True
     )
     return call(scale_rows, jax.ShapeDtypeStruct((ROWS, 4 * HEAD_DIM), BF16), [SMEM] + [VMEM] * 3)(
         place, own, back, totals

time: 76 us -> 76 us (level)
  no operation moved by 1% of the time
where the time goes in v7:
time: 76 us; the launch traced here: 74.6 us
  starting transfers between devices  42.6 us (56%)
  waiting for transfers between devices  12.7 us (17%)
  blocking collectives  9.75 us (13%)
  Pallas kernels  9.29 us (12%)
    ppermute x7, starting transfers between devices, pass_on(): return lax.ppermute(array, 'ctx', pairs)  23.9 us
    all_to_all x1, starting transfers between devices, local(): lax.all_to_all(packed, 'ctx', 0, 0, axis_index_groups=groups('yc'), tiled...  10.3 us
    all_to_all x1, blocking collectives, local(): lax.all_to_all(squares, ('ctx', 'head'), 0, 0, axis_index_groups=chips, t...  9.75 us
    ppermute x2, starting transfers between devices, swap_cores(): return lax.ppermute(array, 'ctx', pairs)  8.38 us
    all_to_all x1, waiting for transfers between devices, local(): lax.all_to_all(packed, 'ctx', 0, 0, axis_index_groups=groups('yc'), tiled...  7.33 us
    ppermute x7, waiting for transfers between devices, pass_on(): return lax.ppermute(array, 'ctx', pairs)  5.34 us
    pallas_call x1, Pallas kernels, local(): call(start_attention, attention(VIRTUAL), [SMEM] + [VMEM] * 5, cost=COST)  2.49 us
    pallas_call x1, Pallas kernels, local(): call(scale_rows, jax.ShapeDtypeStruct((ROWS, 4 * HEAD_DIM), BF16), [SMEM]...  1.58 us
  transfers between devices with their start and end apart: 10, of which 4 were waited for; matrix products, arithmetic and copies ran while one was open for 0% of the time, Pallas kernels for 7%

profile of v7, /device:TPU:1, one launch (start us, length us, event | category | flops | bytes accessed | tf_op | source)
XLA Modules:
  0.0 74.6 jit_solution(6988458592803353787)
XLA Ops:
  0.0 1.6 %shard_map.46 = bf16[8,64,256]{2,1,0:T(8,128)(2,1)} custom-call(bf16[512,512]{1,0:T(8,128)(2,1)} %key_ref.1, bf16[512,512]{1,0:T(8,128)(2,1)} %key_ref.1, bf16[512,512]{1,0:T(8,128)(2,1)} %value_ref.1, bf16[512,512]{1,0:T(8,128)(2,1)} %value_ref.1), custom_call_target="tpu_custom_call" | custom-call | tf_op jit(solution)/shard_map/pallas_call | solution.py:227
  1.6 10.3 %all-to-all-start = ((bf16[8,64,256]{2,1,0:T(8,128)(2,1)}), bf16[8,64,256]{2,1,0:T(8,128)(2,1)S(1)}, u32[]{:S(2)}, u32[]{:S(2)}) async-start(bf16[8,64,256]{2,1,0:T(8,128)(2,1)} %shard_map.46), calls=%async_computation | async-start | bytes 524288 | tf_op jit(solution)/shard_map/all_to_all | solution.py:234
  11.9 0.1 pad_add_fusion.place_ref
  12.0 0.0 copy-done.1
  12.0 0.0 copy-start.3
  12.0 0.6 shard_map.48
  12.6 2.0 %collective-permute-start = (bf16[1536,256]{1,0:T(8,128)(2,1)S(1)}, bf16[1536,256]{1,0:T(8,128)(2,1)S(1)}, u32[]{:S(2)}, u32[]{:S(2)}) collective-permute-start(bf16[1536,256]{1,0:T(8,128)(2,1)S(1)} %shard_map.48), channel_id=1, source_target_pairs={{0,8},{8,0},{16,24},{24,16},{32,40},{40,32},{48,56},{56,48},{64,72... | collective-permute-start | bytes 2359304 | tf_op jit(solution)/shard_map/ppermute | solution.py:204
  14.7 0.7 shard_map.47.gain_ref
  15.3 7.3 %all-to-all-done.slab_ref = bf16[8,64,256]{2,1,0:T(8,128)(2,1)S(1)} async-done(((bf16[8,64,256]{2,1,0:T(8,128)(2,1)}), bf16[8,64,256]{2,1,0:T(8,128)(2,1)S(1)}, u32[]{:S(2)}, u32[]{:S(2)}) %all-to-all-start) | async-done | bytes 262176 | tf_op jit(solution)/shard_map/all_to_all | solution.py:234
  22.7 2.3 %collective-permute-start.1 = (bf16[8,64,256]{2,1,0:T(8,128)(2,1)S(1)}, bf16[8,64,256]{2,1,0:T(8,128)(2,1)S(1)}, u32[]{:S(2)}, u32[]{:S(2)}) collective-permute-start(bf16[8,64,256]{2,1,0:T(8,128)(2,1)S(1)} %all-to-all-done.slab_ref), channel_id=1, source_target_pairs={{0,64},{8,72},{16,80},{24,88},{32,96},{40,104},{48,112},{56,120},{... | collective-permute-start | bytes 786440 | tf_op jit(solution)/shard_map/ppermute | solution.py:215
  24.9 7.9 %collective-permute-start.3 = (bf16[8,64,256]{2,1,0:T(8,128)(2,1)S(1)}, bf16[8,64,256]{2,1,0:T(8,128)(2,1)S(1)}, u32[]{:S(2)}, u32[]{:S(2)}) collective-permute-start(bf16[8,64,256]{2,1,0:T(8,128)(2,1)S(1)} %all-to-all-done.slab_ref), channel_id=1, source_target_pairs={{0,448},{8,456},{16,464},{24,472},{32,480},{40,488},{48,496},{56,5... | collective-permute-start | bytes 786440 | tf_op jit(solution)/shard_map/ppermute | solution.py:215
  32.9 0.0 collective-permute-done.1.refs_0_
  32.9 0.7 collective-permute-start.2
  33.6 0.0 collective-permute-done.other_in_ref
  33.6 2.5 %shard_map.49 = (bf16[4,512,128]{2,1,0:T(8,128)(2,1)S(1)}, f32[4,1,512]{2,1,0:T(1,128)S(1)}, f32[4,1,512]{2,1,0:T(1,128)S(1)}, f32[4,128,512]{2,1,0:T(8,128)S(1)}) custom-call(s32[3]{0:T(128)S(1)} %pad_add_fusion.place_ref, bf16[512,512]{1,0:T(8,128)(2,1)S(1)} %copy-done.2, bf16[512,512]{1,0:T(8,128)(2,1)S(1)} %copy-done, bf16[512,512]{1,0:T(8,128)(2,1)S(1)} %copy-done.1, ...), custom_call_target="tpu_custom_call" | custom-call | flops 3000000000 | bytes 1048576 | tf_op jit(solution)/shard_map/pallas_call | solution.py:265
  36.1 0.8 %collective-permute-done.3.refs_1_ = bf16[8,64,256]{2,1,0:T(8,128)(2,1)S(1)} collective-permute-done((bf16[8,64,256]{2,1,0:T(8,128)(2,1)S(1)}, bf16[8,64,256]{2,1,0:T(8,128)(2,1)S(1)}, u32[]{:S(2)}, u32[]{:S(2)}) %collective-permute-start.3) | collective-permute-done | bytes 262176 | tf_op jit(solution)/shard_map/ppermute | solution.py:215
  36.9 6.6 %collective-permute-start.6 = (bf16[8,64,256]{2,1,0:T(8,128)(2,1)S(1)}, bf16[8,64,256]{2,1,0:T(8,128)(2,1)S(1)}, u32[]{:S(2)}, u32[]{:S(2)}) collective-permute-start(bf16[8,64,256]{2,1,0:T(8,128)(2,1)S(1)} %collective-permute-done.3.refs_1_), channel_id=1, source_target_pairs={{0,448},{8,456},{16,464},{24,472},{32,480},{40,488},{48,496},{56,5... | collective-permute-start | bytes 786440 | tf_op jit(solution)/shard_map/ppermute | solution.py:215
  43.6 0.0 collective-permute-done.2.refs_0_
  43.6 0.7 collective-permute-start.4
  44.2 2.6 %collective-permute-done.6.refs_1_ = bf16[8,64,256]{2,1,0:T(8,128)(2,1)S(1)} collective-permute-done((bf16[8,64,256]{2,1,0:T(8,128)(2,1)S(1)}, bf16[8,64,256]{2,1,0:T(8,128)(2,1)S(1)}, u32[]{:S(2)}, u32[]{:S(2)}) %collective-permute-start.6) | collective-permute-done | bytes 262176 | tf_op jit(solution)/shard_map/ppermute | solution.py:215
  46.8 5.0 %collective-permute-start.7 = (bf16[8,64,256]{2,1,0:T(8,128)(2,1)S(1)}, bf16[8,64,256]{2,1,0:T(8,128)(2,1)S(1)}, u32[]{:S(2)}, u32[]{:S(2)}) collective-permute-start(bf16[8,64,256]{2,1,0:T(8,128)(2,1)S(1)} %collective-permute-done.6.refs_1_), channel_id=1, source_target_pairs={{0,448},{8,456},{16,464},{24,472},{32,480},{40,488},{48,496},{56,5... | collective-permute-start | bytes 786440 | tf_op jit(solution)/shard_map/ppermute | solution.py:215
  51.9 0.7 shard_map.50
  52.6 0.0 collective-permute-done.4.refs_2_
  52.6 0.7 collective-permute-start.5
  53.3 1.9 %collective-permute-done.7.refs_3_.down_ref = bf16[8,64,256]{2,1,0:T(8,128)(2,1)S(1)} collective-permute-done((bf16[8,64,256]{2,1,0:T(8,128)(2,1)S(1)}, bf16[8,64,256]{2,1,0:T(8,128)(2,1)S(1)}, u32[]{:S(2)}, u32[]{:S(2)}) %collective-permute-start.7) | collective-permute-done | bytes 262176 | tf_op jit(solution)/shard_map/ppermute | solution.py:215
  55.2 0.9 %shard_map.51 = (f32[4,1,512]{2,1,0:T(1,128)S(1)}, f32[4,1,512]{2,1,0:T(1,128)S(1)}, f32[4,128,512]{2,1,0:T(8,128)S(1)}) custom-call(s32[3]{0:T(128)S(1)} %pad_add_fusion.place_ref, bf16[4,512,128]{2,1,0:T(8,128)(2,1)S(1)} %get-tuple-element.40.queries_ref, ...), custom_call_target="tpu_custom_call", output_to_operand_aliasing={{0}: (6, {}), {1}: (7, {}), {2}: (8, {})} | custom-call | flops 3000000000 | bytes 1048576 | tf_op jit(solution)/shard_map/pallas_call | solution.py:271
  56.1 0.0 collective-permute-done.5.up_ref
  56.1 0.8 %shard_map.52 = (f32[2,128,512]{2,1,0:T(8,128)S(1)}, f32[2,128,512]{2,1,0:T(8,128)S(1)}, f32[16,1,512]{2,1,0:T(1,128)S(1)}) custom-call(s32[3]{0:T(128)S(1)} %pad_add_fusion.place_ref, f32[2,128,8]{2,1,0:T(8,128)S(1)} %shard_map.47.gain_ref, bf16[4,512,128]{2,1,0:T(8,128)(2,1)S(1)} %get-tuple-element.40.queries_ref, ...), custom_call_target="tpu_custom_call" | custom-call | tf_op jit(solution)/shard_map/pallas_call | solution.py:280
  56.9 6.4 %collective-permute-start.8 = (f32[2,128,512]{2,1,0:T(8,128)S(1)}, f32[2,128,512]{2,1,0:T(8,128)S(1)}, u32[]{:S(2)}, u32[]{:S(2)}) collective-permute-start(f32[2,128,512]{2,1,0:T(8,128)S(1)} %get-tuple-element.65), channel_id=1, source_target_pairs={{0,8},{8,0},{16,24},{24,16},{32,40},{40,32},{48,56},{56,48},{64,72... | collective-permute-start | bytes 1572872 | tf_op jit(solution)/shard_map/ppermute | solution.py:204
  63.2 9.8 %all_to_all.10.square_ref = f32[16,1,512]{2,1,0:T(1,128)S(1)} all-to-all(f32[16,1,512]{2,1,0:T(1,128)S(1)} %get-tuple-element.66), channel_id=1, replica_groups={{0,1,2,3,4,5,6,7,8,9,10,11,12,13,14,15},{16,17,18,19,20,21,22,23,24,25,..., dimensions={0} | all-to-all | bytes 65536 | tf_op jit(solution)/shard_map/all_to_all | solution.py:291
  73.0 0.0 collective-permute-done.8.other_ref
  73.0 1.6 %shard_map.53 = bf16[512,512]{1,0:T(8,128)(2,1)} custom-call(s32[3]{0:T(128)S(1)} %pad_add_fusion.place_ref, f32[2,128,512]{2,1,0:T(8,128)S(1)} %get-tuple-element.64.own_ref, f32[2,128,512]{2,1,0:T(8,128)S(1)} %collective-permute-done.8.other_ref, f32[16,1,512]{2,1,0:T(1,128)S(1)} %all_to_all.10.square_ref), custom_call_target="tpu_custom_call" | custom-call | tf_op jit(solution)/shard_map/pallas_call | solution.py:294
  (6 shorter events, 0.0 us)
Async XLA Ops:
  0.0 12.0 %copy-start.1 = (bf16[512,512]{1,0:T(8,128)(2,1)S(1)}, bf16[512,512]{1,0:T(8,128)(2,1)}, u32[]{:S(2)}) copy-start(bf16[512,512]{1,0:T(8,128)(2,1)} %value_ref.1) | copy-start | bytes 1572868
  0.0 12.0 %copy-start.2 = (bf16[512,512]{1,0:T(8,128)(2,1)S(1)}, bf16[512,512]{1,0:T(8,128)(2,1)}, u32[]{:S(2)}) copy-start(bf16[512,512]{1,0:T(8,128)(2,1)} %query_ref.1) | copy-start | bytes 1572868
  1.6 10.4 %copy-start = (bf16[512,512]{1,0:T(8,128)(2,1)S(1)}, bf16[512,512]{1,0:T(8,128)(2,1)}, u32[]{:S(2)}) copy-start(bf16[512,512]{1,0:T(8,128)(2,1)} %key_ref.1) | copy-start | bytes 1572868
  1.6 21.1 %all-to-all-start = ((bf16[8,64,256]{2,1,0:T(8,128)(2,1)}), bf16[8,64,256]{2,1,0:T(8,128)(2,1)S(1)}, u32[]{:S(2)}, u32[]{:S(2)}) async-start(bf16[8,64,256]{2,1,0:T(8,128)(2,1)} %shard_map.46), calls=%async_computation | async-start | bytes 524288 | tf_op jit(solution)/shard_map/all_to_all | solution.py:234
  12.0 2.7 %copy-start.3 = (f32[512]{0:T(512)S(1)}, f32[512]{0:T(512)}, u32[]{:S(2)}) copy-start(f32[512]{0:T(512)} %param.7) | copy-start | bytes 6148
  12.6 21.0 %collective-permute-start = (bf16[1536,256]{1,0:T(8,128)(2,1)S(1)}, bf16[1536,256]{1,0:T(8,128)(2,1)S(1)}, u32[]{:S(2)}, u32[]{:S(2)}) collective-permute-start(bf16[1536,256]{1,0:T(8,128)(2,1)S(1)} %shard_map.48), channel_id=1, source_target_pairs={{0,8},{8,0},{16,24},{24,16},{32,40},{40,32},{48,56},{56,48},{64,72... | collective-permute-start | bytes 2359304 | tf_op jit(solution)/shard_map/ppermute | solution.py:204
  22.7 10.2 %collective-permute-start.1 = (bf16[8,64,256]{2,1,0:T(8,128)(2,1)S(1)}, bf16[8,64,256]{2,1,0:T(8,128)(2,1)S(1)}, u32[]{:S(2)}, u32[]{:S(2)}) collective-permute-start(bf16[8,64,256]{2,1,0:T(8,128)(2,1)S(1)} %all-to-all-done.slab_ref), channel_id=1, source_target_pairs={{0,64},{8,72},{16,80},{24,88},{32,96},{40,104},{48,112},{56,120},{... | collective-permute-start | bytes 786440 | tf_op jit(solution)/shard_map/ppermute | solution.py:215
  24.9 12.0 %collective-permute-start.3 = (bf16[8,64,256]{2,1,0:T(8,128)(2,1)S(1)}, bf16[8,64,256]{2,1,0:T(8,128)(2,1)S(1)}, u32[]{:S(2)}, u32[]{:S(2)}) collective-permute-start(bf16[8,64,256]{2,1,0:T(8,128)(2,1)S(1)} %all-to-all-done.slab_ref), channel_id=1, source_target_pairs={{0,448},{8,456},{16,464},{24,472},{32,480},{40,488},{48,496},{56,5... | collective-permute-start | bytes 786440 | tf_op jit(solution)/shard_map/ppermute | solution.py:215
  32.9 10.7 %collective-permute-start.2 = (bf16[8,64,256]{2,1,0:T(8,128)(2,1)S(1)}, bf16[8,64,256]{2,1,0:T(8,128)(2,1)S(1)}, u32[]{:S(2)}, u32[]{:S(2)}) collective-permute-start(bf16[8,64,256]{2,1,0:T(8,128)(2,1)S(1)} %collective-permute-done.1.refs_0_), channel_id=1, source_target_pairs={{64,128},{72,136},{80,144},{88,152},{96,160},{104,168},{112,176},{... | collective-permute-start | bytes 786440 | tf_op jit(solution)/shard_map/ppermute | solution.py:215
  36.9 9.9 %collective-permute-start.6 = (bf16[8,64,256]{2,1,0:T(8,128)(2,1)S(1)}, bf16[8,64,256]{2,1,0:T(8,128)(2,1)S(1)}, u32[]{:S(2)}, u32[]{:S(2)}) collective-permute-start(bf16[8,64,256]{2,1,0:T(8,128)(2,1)S(1)} %collective-permute-done.3.refs_1_), channel_id=1, source_target_pairs={{0,448},{8,456},{16,464},{24,472},{32,480},{40,488},{48,496},{56,5... | collective-permute-start | bytes 786440 | tf_op jit(solution)/shard_map/ppermute | solution.py:215
  43.6 9.0 %collective-permute-start.4 = (bf16[8,64,256]{2,1,0:T(8,128)(2,1)S(1)}, bf16[8,64,256]{2,1,0:T(8,128)(2,1)S(1)}, u32[]{:S(2)}, u32[]{:S(2)}) collective-permute-start(bf16[8,64,256]{2,1,0:T(8,128)(2,1)S(1)} %collective-permute-done.2.refs_0_), channel_id=1, source_target_pairs={{128,192},{136,200},{144,208},{152,216},{160,224},{168,232},{176,2... | collective-permute-start | bytes 786440 | tf_op jit(solution)/shard_map/ppermute | solution.py:215
  46.8 8.3 %collective-permute-start.7 = (bf16[8,64,256]{2,1,0:T(8,128)(2,1)S(1)}, bf16[8,64,256]{2,1,0:T(8,128)(2,1)S(1)}, u32[]{:S(2)}, u32[]{:S(2)}) collective-permute-start(bf16[8,64,256]{2,1,0:T(8,128)(2,1)S(1)} %collective-permute-done.6.refs_1_), channel_id=1, source_target_pairs={{0,448},{8,456},{16,464},{24,472},{32,480},{40,488},{48,496},{56,5... | collective-permute-start | bytes 786440 | tf_op jit(solution)/shard_map/ppermute | solution.py:215
  52.6 3.5 %collective-permute-start.5 = (bf16[8,64,256]{2,1,0:T(8,128)(2,1)S(1)}, bf16[8,64,256]{2,1,0:T(8,128)(2,1)S(1)}, u32[]{:S(2)}, u32[]{:S(2)}) collective-permute-start(bf16[8,64,256]{2,1,0:T(8,128)(2,1)S(1)} %collective-permute-done.4.refs_2_), channel_id=1, source_target_pairs={{192,256},{200,264},{208,272},{216,280},{224,288},{232,296},{240,3... | collective-permute-start | bytes 786440 | tf_op jit(solution)/shard_map/ppermute | solution.py:215
  56.9 16.1 %collective-permute-start.8 = (f32[2,128,512]{2,1,0:T(8,128)S(1)}, f32[2,128,512]{2,1,0:T(8,128)S(1)}, u32[]{:S(2)}, u32[]{:S(2)}) collective-permute-start(f32[2,128,512]{2,1,0:T(8,128)S(1)} %get-tuple-element.65), channel_id=1, source_target_pairs={{0,8},{8,0},{16,24},{24,16},{32,40},{40,32},{48,56},{56,48},{64,72... | collective-permute-start | bytes 1572872 | tf_op jit(solution)/shard_map/ppermute | solution.py:204
